TPU v7x, 32 devices: a whole 2x2x4 slice. The times are simulated.
32 devices in a mesh: lb: 4 (over x, core), rb: 4 (over z), rep: 2 (over y).
Axes of the slice: x: 2, y: 2, z: 4, core: 2. Of those that a mesh axis runs over, the one named last changes fastest.
Arguments:
- left_factor: bfloat16 [1024, 1024], P('lb', 'rep'), may hold values from -5 to 5
- boundary_site: bfloat16 [1024, 16, 1024], P('rep', None, 'rb'), may hold values from -6 to 6
- double_layer: float32 [16, 16], replicated, may hold values from -1.5 to 1.5
Outputs:
- site_q: float32 [16, 1024, 1024], P('rep', 'lb', 'rb')
- factor: float32 [1024, 1024], P('lb')
All inputs are finite; a program needn't handle non-finite values.
Results may differ from a plain program's by a relative error of at most 0.0032.
Values sent between devices are 32-bit elements; how exact they have to be, the bound alone decides.
No kernel may reach another device: no remote copies, remote signals or barrier semaphores. Data moves between devices by JAX's collectives and lax.ppermute only.
A program may use at most 128 MiB of HBM per device.

v0:
```python
import math

import jax
import jax.numpy as jnp
from jax import lax
from jax.sharding import PartitionSpec as P

CHI = 1024
PHYS = 16


def shards(left_factor, boundary_site, double_layer):
    highest = lax.Precision.HIGHEST
    absorbed = jnp.einsum(
        "kur,ue->ker", boundary_site.astype(jnp.float32), double_layer, precision=highest
    ).astype(jnp.bfloat16)
    row_count = left_factor.shape[0]
    grown_part = lax.psum_scatter(
        jnp.einsum("ik,ker->eir", left_factor, absorbed, preferred_element_type=jnp.float32),
        "rep",
        scatter_dimension=0,
        tiled=True,
    )
    grown_all = lax.all_gather(grown_part, "lb", axis=1, tiled=True)
    gram_part = jnp.einsum("eir,ejr->ij", grown_part, grown_all, precision=highest)
    gram_block = lax.psum(gram_part, ("rb", "rep"))
    gram = lax.all_gather(gram_block, "lb", axis=0, tiled=True)
    lower = jnp.linalg.cholesky(gram)
    east_count = grown_all.shape[0]
    right_count = grown_all.shape[2]
    matrix = jnp.transpose(grown_all, (1, 0, 2)).reshape(CHI, east_count * right_count)
    solved = jax.scipy.linalg.solve_triangular(lower, matrix, lower=True)
    offset = lax.axis_index("lb") * row_count
    mine = lax.dynamic_slice_in_dim(solved, offset, row_count, 0)
    scale = math.sqrt(PHYS * CHI)
    site_q = jnp.transpose(mine.reshape(row_count, east_count, right_count), (1, 0, 2)) * scale
    factor = lax.dynamic_slice_in_dim(lower, offset, row_count, 0) / scale
    return (site_q, factor)


def solution(mesh):
    return jax.shard_map(
        shards,
        mesh=mesh,
        in_specs=(P("lb", "rep"), P("rep", None, "rb"), P()),
        out_specs=(P("rep", "lb", "rb"), P("lb", None)),
        check_vma=False,
    )
```

profile of v0, /device:TPU:0, one launch (start us, length us, event | category | flops | bytes accessed | tf_op | source)
XLA Modules:
  0.0 688.8 jit_solution(15646722316059868065)
XLA Ops:
  7.2 7.0 %fusion.73 = bf16[16,512,256]{2,0,1:T(8,128)(2,1)} fusion(bf16[512,16,256]{2,1,0:T(8,128)(2,1)} %param.4, f32[16,16]{1,0:T(8,128)} %param.5), kind=kOutput, calls=%fused_computation.145 | convolution fusion | flops 402653184 | bytes 8389632 | tf_op jit(solution)/shard_map/kur,ue->ker/dot_general | solution.py:14
  14.2 7.6 %copy.10 = bf16[16,512,256]{1,2,0:T(8,128)(2,1)} copy(bf16[16,512,256]{2,0,1:T(8,128)(2,1)} %fusion.73) | data formatting | bytes 8388608 | tf_op jit(solution)/shard_map/kur,ue->ker/dot_general | solution.py:14
  21.8 5.4 fusion.25
  27.3 57.1 %reduce-scatter.2.cloned.1.call-done = f32[8,256,256]{1,2,0:T(8,128)} async-done(((f32[16,256,256]{1,2,0:T(8,128)}), f32[8,256,256]{1,2,0:T(8,128)}) %reduce-scatter.2.cloned.1.call-update) | async-done | bytes 2097168 | tf_op jit(solution)/shard_map/reduce_scatter | solution.py:18
  84.5 59.9 %all-gather.3.cloned.1.call-done = f32[8,1024,256]{1,2,0:T(8,128)} async-done(((f32[8,256,256]{1,2,0:T(8,128)}), f32[8,1024,256]{1,2,0:T(8,128)}) %all-gather.3.cloned.1.call-update) | async-done | bytes 8388624 | tf_op jit(solution)/shard_map/all_gather | solution.py:24
  144.4 17.1 %convolution_bitcast_fusion = f32[256,1024]{0,1:T(8,128)} fusion(f32[8,256,256]{1,2,0:T(8,128)} %reduce-scatter.2.cloned.1.call-done, f32[8,1024,256]{1,2,0:T(8,128)} %all-gather.3.cloned.1.call-done), kind=kOutput, calls=%fused_computation.38 | convolution fusion | flops 6442450944 | bytes 11534336 | tf_op jit(solution)/shard_map/eir,ejr->ij/dot_general | solution.py:25
  161.5 78.2 %all-reduce.3.cloned.1.call-done = f32[256,1024]{0,1:T(8,128)} async-done(((f32[256,1024]{0,1:T(8,128)}), f32[256,1024]{0,1:T(8,128)}) %all-reduce.3.cloned.1.call-update) | async-done | bytes 1048592 | tf_op jit(solution)/shard_map/psum | solution.py:26
  239.7 6.0 fusion.79
  245.7 29.5 %all-gather.5.cloned.1.call-done = f32[1024,1024]{0,1:T(8,128)} async-done(((f32[256,1024]{0,1:T(8,128)}), f32[1024,1024]{0,1:T(8,128)}) %all-gather.5.cloned.1.call-update) | async-done | bytes 4194320 | tf_op jit(solution)/shard_map/all_gather | solution.py:27
  275.2 5.8 copy.8
  281.0 4.4 fusion.8
  287.4 11.7 %cholesky.223 = f32[128,128]{1,0:T(8,128)S(1)} custom-call(f32[128,128]{1,0:T(8,128)S(1)} %cholesky.580), custom_call_target="Cholesky" | custom-call | tf_op jit(solution)/shard_map/jit(cholesky)/cholesky | solution.py:28
  299.1 9.8 %custom-call.63 = f32[1,128,128]{1,2,0:T(8,128)S(1)} custom-call(f32[1,128,128]{2,1,0:T(8,128)S(1)} %get-tuple-element.76), custom_call_target="InvertDiagBlocksLowerTriangular" | custom-call | tf_op jit(solution)/shard_map/jit(cholesky)/cholesky | solution.py:28
  308.9 2.5 cholesky.255
  311.4 2.3 constant_dynamic-update-slice_fusion.31
  316.1 11.9 %cholesky.244 = f32[128,128]{1,0:T(8,128)S(1)} custom-call(f32[128,128]{1,0:T(8,128)S(1)} %cholesky.584), custom_call_target="Cholesky" | custom-call | tf_op jit(solution)/shard_map/jit(cholesky)/cholesky | solution.py:28
  328.6 9.8 %custom-call.64 = f32[1,128,128]{1,2,0:T(8,128)S(1)} custom-call(f32[1,128,128]{2,1,0:T(8,128)S(1)} %get-tuple-element.73), custom_call_target="InvertDiagBlocksLowerTriangular" | custom-call | tf_op jit(solution)/shard_map/jit(cholesky)/cholesky | solution.py:28
  343.5 11.7 %cholesky.468 = f32[128,128]{1,0:T(8,128)S(1)} custom-call(f32[128,128]{1,0:T(8,128)S(1)} %cholesky.589), custom_call_target="Cholesky" | custom-call | tf_op jit(solution)/shard_map/jit(cholesky)/cholesky | solution.py:28
  356.5 9.8 %custom-call.65 = f32[1,128,128]{1,2,0:T(8,128)S(1)} custom-call(f32[1,128,128]{2,1,0:T(8,128)S(1)} %get-tuple-element.70), custom_call_target="InvertDiagBlocksLowerTriangular" | custom-call | tf_op jit(solution)/shard_map/jit(cholesky)/cholesky | solution.py:28
  368.5 2.4 convolution_subtract_fusion.7
  371.6 11.9 %cholesky.487 = f32[128,128]{1,0:T(8,128)S(1)} custom-call(f32[128,128]{1,0:T(8,128)S(1)} %cholesky.594), custom_call_target="Cholesky" | custom-call | tf_op jit(solution)/shard_map/jit(cholesky)/cholesky | solution.py:28
  384.9 9.8 %custom-call.66 = f32[1,128,128]{1,2,0:T(8,128)S(1)} custom-call(f32[1,128,128]{2,1,0:T(8,128)S(1)} %get-tuple-element.67), custom_call_target="InvertDiagBlocksLowerTriangular" | custom-call | tf_op jit(solution)/shard_map/jit(cholesky)/cholesky | solution.py:28
  399.1 11.7 %cholesky.506 = f32[128,128]{1,0:T(8,128)S(1)} custom-call(f32[128,128]{1,0:T(8,128)S(1)} %cholesky.599), custom_call_target="Cholesky" | custom-call | tf_op jit(solution)/shard_map/jit(cholesky)/cholesky | solution.py:28
  412.1 10.2 %custom-call.67 = f32[1,128,128]{1,2,0:T(8,128)S(1)} custom-call(f32[1,128,128]{2,1,0:T(8,128)S(1)} %get-tuple-element.64), custom_call_target="InvertDiagBlocksLowerTriangular" | custom-call | tf_op jit(solution)/shard_map/jit(cholesky)/cholesky | solution.py:28
  425.6 11.7 %cholesky.526 = f32[128,128]{1,0:T(8,128)S(1)} custom-call(f32[128,128]{1,0:T(8,128)S(1)} %cholesky.604), custom_call_target="Cholesky" | custom-call | tf_op jit(solution)/shard_map/jit(cholesky)/cholesky | solution.py:28
  438.7 9.8 %custom-call.68 = f32[1,128,128]{1,2,0:T(8,128)S(1)} custom-call(f32[1,128,128]{2,1,0:T(8,128)S(1)} %get-tuple-element.61), custom_call_target="InvertDiagBlocksLowerTriangular" | custom-call | tf_op jit(solution)/shard_map/jit(cholesky)/cholesky | solution.py:28
  451.5 11.8 %cholesky.546 = f32[128,128]{1,0:T(8,128)S(1)} custom-call(f32[128,128]{1,0:T(8,128)S(1)} %cholesky.609), custom_call_target="Cholesky" | custom-call | tf_op jit(solution)/shard_map/jit(cholesky)/cholesky | solution.py:28
  464.6 9.8 %custom-call.69 = f32[1,128,128]{1,2,0:T(8,128)S(1)} custom-call(f32[1,128,128]{2,1,0:T(8,128)S(1)} %get-tuple-element.58), custom_call_target="InvertDiagBlocksLowerTriangular" | custom-call | tf_op jit(solution)/shard_map/jit(cholesky)/cholesky | solution.py:28
  477.0 11.7 %cholesky.564 = f32[128,128]{1,0:T(8,128)S(1)} custom-call(f32[128,128]{1,0:T(8,128)S(1)} %convolution_subtract_fusion.11), custom_call_target="Cholesky" | custom-call | tf_op jit(solution)/shard_map/jit(cholesky)/cholesky | solution.py:28
  495.7 6.6 fusion.12
  502.3 28.3 %while.1 = (s32[]{:T(128)}, f32[1024,1024]{1,0:T(8,128)}, s32[8,2]{0,1:T(2,128)S(1)}, f32[8,128,128]{2,1,0:T(8,128)}, s32[]{:T(128)}) while((s32[]{:T(128)}, f32[1024,1024]{1,0:T(8,128)}, s32[8,2]{0,1:T(2,128)S(1)}, f32[8,128,128]{2,1,0:T(8,128)}, s32[]{:T(128)}) %tuple.69), condition=%wide.while_cond, body=%wide.while_body.sunk | while | flops 2 | bytes 132205 | solution.py:32
  503.0 2.9 bitcast_dynamic-update-slice_fusion.2
  506.5 2.9 bitcast_dynamic-update-slice_fusion.2
  510.1 2.9 bitcast_dynamic-update-slice_fusion.2
  513.6 2.9 bitcast_dynamic-update-slice_fusion.2
  517.2 2.9 bitcast_dynamic-update-slice_fusion.2
  520.7 2.9 bitcast_dynamic-update-slice_fusion.2
  524.3 2.9 bitcast_dynamic-update-slice_fusion.2
  527.8 2.8 bitcast_dynamic-update-slice_fusion.2
  530.6 80.2 %custom-call.70 = f32[8,128,128]{1,2,0:T(8,128)} custom-call(f32[8,128,128]{2,1,0:T(8,128)} %get-tuple-element.9), custom_call_target="InvertDiagBlocksLowerTriangular" | custom-call | tf_op jit(solution)/shard_map/jit(_solve_triangular)/triangular_solve | solution.py:32
  613.2 2.6 constant_dynamic-update-slice_fusion.17
  615.8 2.7 convolution_subtract_fusion.4
  619.8 4.4 convolution_subtract_fusion.3
  625.6 6.7 fusion.19
  633.6 7.6 %fusion.22 = f32[128,2048]{0,1:T(8,128)S(1)} fusion(f32[128,2048]{0,1:T(8,128)S(1)} %bitcast.146, f32[128,2048]{1,0:T(8,128)S(1)} %get-tuple-element.82, f32[128,2048]{1,0:T(8,128)S(1)} %get-tuple-element.81, f32[128,2048]{1,0:T(8,128)S(1)} %get-tuple-element.80, f32[128,2048]{1,0:T(8,128)S(1)} %get-tuple-element.79, f32[1024,1024]{1,0:T(8,128)} %get-tuple-element.137), kind=kOutput, calls=%fused_computation.31 | convolution fusion | flops 1614020608 | bytes 6553600 | tf_op jit(solution)/shard_map/jit(_solve_triangular)/triangular_solve | solution.py:32
  642.5 9.9 %convolution_subtract_fusion.2 = f32[128,2048]{0,1:T(8,128)S(1)} fusion(f32[128,2048]{0,1:T(8,128)S(1)} %bitcast.144, f32[640,2048]{1,0:T(8,128)S(1)} %get-tuple-element.38, f32[1024,1024]{1,0:T(8,128)} %get-tuple-element.137), kind=kOutput, calls=%fused_computation.28 | convolution fusion | flops 2013528064 | bytes 7667712 | tf_op jit(solution)/shard_map/jit(_solve_triangular)/triangular_solve | solution.py:32
  653.5 11.1 %convolution_subtract_fusion = f32[128,2048]{0,1:T(8,128)S(1)} fusion(f32[128,2048]{0,1:T(8,128)S(1)} %bitcast.139, f32[768,2048]{1,0:T(8,128)S(1)} %get-tuple-element.34, f32[1024,1024]{1,0:T(8,128)} %get-tuple-element.137), kind=kOutput, calls=%fused_computation.25 | convolution fusion | flops 2416181248 | bytes 8781824 | tf_op jit(solution)/shard_map/jit(_solve_triangular)/triangular_solve | solution.py:32
  665.7 13.3 %convolution_subtract_fusion.1 = f32[128,2048]{0,1:T(8,128)S(1)} fusion(f32[128,2048]{0,1:T(8,128)S(1)} %bitcast.138, f32[896,2048]{1,0:T(8,128)S(1)} %get-tuple-element.30, f32[1024,1024]{1,0:T(8,128)} %get-tuple-element.137), kind=kOutput, calls=%fused_computation.27 | convolution fusion | flops 2818834432 | bytes 9895936 | tf_op jit(solution)/shard_map/jit(_solve_triangular)/triangular_solve | solution.py:32
  (93 shorter events, 52.7 us)
Async XLA Ops:
  7.2 14.6 %copy-start = (bf16[256,512]{1,0:T(8,128)(2,1)S(1)}, bf16[256,512]{1,0:T(8,128)(2,1)}, u32[]{:S(2)}) copy-start(bf16[256,512]{1,0:T(8,128)(2,1)} %param.3) | copy-start | bytes 786436
  7.2 77.2 %reduce-scatter.2.cloned.1.call-start = ((), (), s32[]{:S(2)}) async-start(), calls=%async_computation.1 | async-start | bytes 6291456 | tf_op jit(solution)/shard_map/reduce_scatter | solution.py:18
  27.3 117.1 %all-gather.3.cloned.1.call-start = ((), (), s32[]{:S(2)}) async-start(), calls=%async_computation.2 | async-start | bytes 10485760 | tf_op jit(solution)/shard_map/all_gather | solution.py:24
  84.4 155.2 %all-reduce.3.cloned.1.call-start = ((), (), s32[]{:S(2)}) async-start(), calls=%async_computation.3 | async-start | bytes 2097152 | tf_op jit(solution)/shard_map/psum | solution.py:26
  161.5 113.7 %all-gather.5.cloned.1.call-start = ((), (), s32[]{:S(2)}) async-start(), calls=%async_computation.4 | async-start | bytes 5242880 | tf_op jit(solution)/shard_map/all_gather | solution.py:27
  285.4 1.9 copy-start.2
  315.3 0.8 copy-start.6
  342.8 0.8 copy-start.7
  370.9 0.7 copy-start.8
  613.2 5.3 copy-start.10
  615.8 4.1 copy-start.4
  624.3 1.3 copy-start.3
  632.3 1.3 copy-start.9
  641.2 1.2 copy-start.5
  679.0 2.8 copy-start.1
Sparse Core Ops, SparseCore 0:
  27.4 56.9 reduce-scatter.1
  86.1 58.2 all-gather.2
  161.6 78.0 all-reduce.2
  241.1 34.0 all-gather.4
where the time goes:
time: 698 us; the launch traced here: 689 us
  other arithmetic  266 us (38%)
  waiting for transfers between devices  225 us (32%)
  matrix products  122 us (17%)
  local copies, waits for them, and re-layouts  55.9 us (8%)
  between operations  19.6 us (3%)
    another operation x30, other arithmetic, shards(): lower = jnp.linalg.cholesky(gram)  172 us
    another operation x3, other arithmetic, shards(): solved = jax.scipy.linalg.solve_triangular(lower, matrix, lower=True)  86.8 us
    psum x1, waiting for transfers between devices, shards(): gram_block = lax.psum(gram_part, ('rb', 'rep'))  78.2 us
    another operation x15, matrix products, shards(): solved = jax.scipy.linalg.solve_triangular(lower, matrix, lower=True)  66.7 us
    all_gather x1, waiting for transfers between devices, shards(): grown_all = lax.all_gather(grown_part, 'lb', axis=1, tiled=True)  59.9 us
    reduce_scatter x1, waiting for transfers between devices, shards(): lax.psum_scatter(jnp.einsum('ik,ker->eir', left_factor, absorbed, preferr...  57.1 us
    all_gather x1, waiting for transfers between devices, shards(): gram = lax.all_gather(gram_block, 'lb', axis=0, tiled=True)  29.5 us
    another operation x24, local copies, waits for them, and re-layouts  28.3 us
  transfers between devices with their start and end apart: 4, of which 4 were waited for; matrix products, arithmetic and copies ran while one was open for 1% of the time, Pallas kernels for 0%

commit v1 on v0

v1 whole, which is shorter than its diff:
```python
import functools
import math

import jax
import jax.numpy as jnp
from jax import lax
from jax.sharding import PartitionSpec as P

BLOCK = 128


def swap(array, axis, size, distance):
    return lax.ppermute(array, axis, [(i, i ^ distance) for i in range(size)])


def upper_bit(axis, distance):
    return lax.rem(lax.div(lax.axis_index(axis), distance), 2)


def distances(size):
    out = []
    while 1 << len(out) < size:
        out.append(1 << len(out))
    return out


def join(array, axis, size, distance, dim):
    other = swap(array, axis, size, distance)
    mine_second = upper_bit(axis, distance) == 1
    first = jnp.where(mine_second, other, array)
    second = jnp.where(mine_second, array, other)
    return jnp.concatenate([first, second], dim)


def halves(array, bit):
    half = array.shape[0] // 2
    mine = lax.dynamic_slice_in_dim(array, bit * half, half, 0)
    other = lax.dynamic_slice_in_dim(array, (1 - bit) * half, half, 0)
    return mine, other


def reduce_scatter(parts, orders):
    halved = []
    for stage in zip(*orders):
        sent, kept, cut = [], [], []
        for part, (axis, size, distance) in zip(parts, stage):
            cut.append(part.shape[0] % 16 == 0)
            if cut[-1]:
                mine, other = halves(part, upper_bit(axis, distance))
            else:
                mine, other = part, part
            kept.append(mine)
            sent.append(swap(other, axis, size, distance))
        parts = [k + s for k, s in zip(kept, sent)]
        halved.append(cut)
    return parts, halved


def all_gather(parts, orders, halved):
    stages = list(zip(*orders))
    for stage, cut in zip(stages[::-1], halved[::-1]):
        parts = [
            join(part, axis, size, distance, 0) if was_cut else part
            for part, (axis, size, distance), was_cut in zip(parts, stage, cut)
        ]
    return parts


def gather_slots(array, axis, size):
    held = [(0, array)]
    for d in distances(size)[::-1]:
        held += [(slot ^ d, swap(piece, axis, size, d)) for slot, piece in held]
    return held


def split3(array):
    high = lax.reduce_precision(array, 8, 7)
    rest = array - high
    middle = lax.reduce_precision(rest, 8, 7)
    low = rest - middle
    return [piece.astype(jnp.bfloat16) for piece in (high, middle, low)]


def pack(matrix):
    n = matrix.shape[0] // BLOCK
    rows = []
    for i in range(n // 2):
        j = n - 1 - i
        rows.append(
            jnp.concatenate(
                [
                    matrix[i * BLOCK : (i + 1) * BLOCK, : (i + 1) * BLOCK],
                    matrix[j * BLOCK : (j + 1) * BLOCK, : (j + 1) * BLOCK],
                ],
                1,
            )
        )
    return jnp.concatenate(rows, 0)


def unpack(packed, size):
    n = size // BLOCK
    rows = [None] * n
    for i in range(n // 2):
        j = n - 1 - i
        row = packed[i * BLOCK : (i + 1) * BLOCK]
        for at, lo in ((i, 0), (j, (i + 1) * BLOCK)):
            blocks = [row[:, lo : lo + at * BLOCK], row[:, lo + at * BLOCK : lo + (at + 1) * BLOCK] * 0.5]
            blocks.append(jnp.zeros((BLOCK, size - (at + 1) * BLOCK), packed.dtype))
            rows[at] = jnp.concatenate(blocks, 1)
    return jnp.concatenate(rows, 0)


def shards(sizes, left_factor, boundary_site, double_layer):
    lb, rb, rep = sizes["lb"], sizes["rb"], sizes["rep"]
    highest = lax.Precision.HIGHEST
    l, p = lax.axis_index("lb"), lax.axis_index("rep")
    depth, phys, right = boundary_site.shape
    east = phys // rep
    chi = depth * rep
    row_count = left_factor.shape[0]

    nothing = double_layer[0, 0] * 0.0

    rows = left_factor.astype(jnp.float32)
    for d in distances(rep):
        rows = join(rows, "rep", rep, d, 1)
    left = jnp.zeros((chi, chi), jnp.bfloat16)
    for slot, piece in gather_slots(rows, "lb", lb):
        piece = (piece + nothing).astype(jnp.bfloat16)
        left = lax.dynamic_update_slice(left, piece, ((l ^ slot) * row_count, 0))

    absorbed = jnp.einsum(
        "kur,ue->ekr", boundary_site.astype(jnp.float32), double_layer, precision=highest
    ).astype(jnp.bfloat16)
    own = lax.dynamic_slice_in_dim(absorbed, p * east, east, 0)

    east_part, right_parts = max(1, east // lb), max(1, lb // east)
    right_part = right // right_parts
    east_at, right_at = (l // right_parts) * east_part, (l % right_parts) * right_part

    def chunk(q):
        return lax.dynamic_slice(
            absorbed, (q * east + east_at, 0, right_at), (east_part, depth, right_part)
        )

    columns = jnp.zeros((east_part, chi, right_part), jnp.bfloat16)
    columns = lax.dynamic_update_slice(columns, chunk(p), (0, p * depth, 0))
    others = []
    for s in range(1, rep):
        q = p ^ s
        got = swap(chunk(q).astype(jnp.float32), "rep", rep, s)
        others.append(got)
        got = (got + nothing).astype(jnp.bfloat16)
        columns = lax.dynamic_update_slice(columns, got, (0, q * depth, 0))
    moment = jnp.einsum("ekr,ejr->kj", columns, columns, preferred_element_type=jnp.float32)

    packed = pack(moment)
    steps = {a: [(a, n, d) for d in distances(n)] for a, n in (("lb", lb), ("rb", rb), ("rep", rep))}
    core, across = steps["lb"][:1], steps["lb"][1:]
    base = across + steps["rep"] + steps["rb"]
    near = across[:1] + steps["rep"][:1] + steps["rb"][:1]
    far = [step for step in base if step not in near]
    orders = [near[i:] + near[:i] + far for i in range(3)]
    (packed,), cut_core = reduce_scatter([packed], [core])
    third = packed.shape[1] // 3
    parts = [packed[:, i * third : (i + 1) * third] for i in range(3)]
    parts, cut = reduce_scatter(parts, orders)
    parts = all_gather(parts, orders, cut)
    (packed,) = all_gather([jnp.concatenate(parts, 1)], [core], cut_core)

    lower_half = unpack(packed, chi)
    dot = functools.partial(jnp.dot, preferred_element_type=jnp.float32)
    product = sum(dot(left, piece) for piece in split3(lower_half)[::-1])
    half_gram = sum(dot(piece, left.T) for piece in split3(product)[::-1])
    gram = half_gram + half_gram.T
    lower = jnp.linalg.cholesky(gram)
    weights = jax.scipy.linalg.solve_triangular(lower, left.astype(jnp.float32), lower=True)
    weights = lax.dynamic_slice_in_dim(weights, l * row_count, row_count, 0)

    scale = math.sqrt(phys * rb * right)
    site = jnp.zeros((east, chi, right), jnp.bfloat16)
    site = lax.dynamic_update_slice(site, own, (0, p * depth, 0))
    for s, got in zip(range(1, rep), others):
        for slot, piece in gather_slots(got, "lb", lb):
            owner = l ^ slot
            at = ((owner // right_parts) * east_part, (p ^ s) * depth, (owner % right_parts) * right_part)
            piece = (piece + nothing).astype(jnp.bfloat16)
            site = lax.dynamic_update_slice(site, piece, at)
    site_q = jnp.einsum(
        "ik,ekr->eir", (weights * scale).astype(jnp.bfloat16), site, preferred_element_type=jnp.float32
    )
    factor = lax.dynamic_slice_in_dim(lower, l * row_count, row_count, 0) / scale
    return (site_q, factor)


def solution(mesh):
    return jax.shard_map(
        functools.partial(shards, dict(mesh.shape)),
        mesh=mesh,
        in_specs=(P("lb", "rep"), P("rep", None, "rb"), P()),
        out_specs=(P("rep", "lb", "rb"), P("lb", None)),
        check_vma=False,
    )
```

time: 698 us -> 596 us (0.85)
  waiting for transfers between devices: 225 us -> 108 us
  matrix products: 122 us -> 71.4 us
  starting transfers between devices: 0.16 us -> 49.6 us
  other arithmetic: 266 us -> 287 us
  between operations: 19.6 us -> 8.02 us
  local copies, waits for them, and re-layouts: 55.9 us -> 65.3 us
    ppermute x0 -> x34, waiting for transfers between devices: none -> 108 us  [swap(): return lax.ppermute(array, axis, [(i, i ^ distance) for i in range(size)])]
    all_gather x2 -> x0, waiting for transfers between devices: 89.4 us -> none  [the longest x1 59.9 us: shards(): grown_all = lax.all_gather(grown_part, 'lb', axis=1, tiled=True)]
    psum x1 -> x0, waiting for transfers between devices: 78.2 us -> none  [shards(): gram_block = lax.psum(gram_part, ('rb', 'rep'))]
    reduce_scatter x1 -> x0, waiting for transfers between devices: 57.1 us -> none  [shards(): lax.psum_scatter(jnp.einsum('ik,ker->eir', left_factor, absorbed, preferr...]
    ppermute x0 -> x34, starting transfers between devices: none -> 49.6 us  [swap(): return lax.ppermute(array, axis, [(i, i ^ distance) for i in range(size)])]
    another operation x15, matrix products: 66.7 us -> 23.3 us  [shards(): jax.scipy.linalg.solve_triangular(lower, left.astype(jnp.float32), lower=...]
    convert_element_type x0 -> x6, other arithmetic: none -> 8.56 us  [the longest x3 4.72 us: shards(): piece = (piece + nothing).astype(jnp.bfloat16)]
    another operation x26 -> x25, local copies, waits for them, and re-layouts: 34.3 us -> 29 us
  transfers between devices with their start and end apart: 4 -> 34, of which waited for: 4 -> 19; matrix products, arithmetic and copies ran while one was open for 1% -> 7% of each run, Pallas kernels for 0% -> 0%
where the time goes in v1:
time: 596 us; the launch traced here: 589 us
  other arithmetic  287 us (48%)
  waiting for transfers between devices  108 us (18%)
  matrix products  71.4 us (12%)
  local copies, waits for them, and re-layouts  65.3 us (11%)
  starting transfers between devices  49.6 us (8%)
  between operations  8.02 us (1%)
    another operation x31, other arithmetic, shards(): lower = jnp.linalg.cholesky(gram)  173 us
    ppermute x34, waiting for transfers between devices, swap(): return lax.ppermute(array, axis, [(i, i ^ distance) for i in range(size)])  108 us
    another operation x3, other arithmetic, shards(): jax.scipy.linalg.solve_triangular(lower, left.astype(jnp.float32), lower=...  85.2 us
    ppermute x34, starting transfers between devices, swap(): return lax.ppermute(array, axis, [(i, i ^ distance) for i in range(size)])  49.6 us
    another operation x24, local copies, waits for them, and re-layouts  29 us
    another operation x15, matrix products, shards(): jax.scipy.linalg.solve_triangular(lower, left.astype(jnp.float32), lower=...  23.3 us
    another operation x14, matrix products, shards(): lower = jnp.linalg.cholesky(gram)  23 us
  transfers between devices with their start and end apart: 34, of which 19 were waited for; matrix products, arithmetic and copies ran while one was open for 7% of the time, Pallas kernels for 0%

profile of v1, /device:TPU:0, one launch (start us, length us, event | category | flops | bytes accessed | tf_op | source)
XLA Modules:
  0.0 589.3 jit_solution(9779786245603953173)
XLA Ops:
  0.6 5.4 fusion.85
  6.0 3.5 copy.62
  10.9 3.0 collective-permute-start
  16.7 31.7 %collective-permute-done.4 = f32[256,512]{1,0:T(8,128)} collective-permute-done((f32[256,512]{1,0:T(8,128)S(1)}, f32[256,512]{1,0:T(8,128)}, u32[]{:S(2)}, u32[]{:S(2)}) %collective-permute-start.4) | collective-permute-done | bytes 524320 | tf_op jit(solution)/shard_map/ppermute | solution.py:13
  61.0 3.2 copy.40
  70.6 6.5 %collective-permute-done.5 = f32[256,1024]{1,0:T(8,128)} collective-permute-done((f32[256,1024]{1,0:T(8,128)}, f32[256,1024]{1,0:T(8,128)}, u32[]{:S(2)}, u32[]{:S(2)}) %collective-permute-start.5) | collective-permute-done | bytes 1048608 | tf_op jit(solution)/shard_map/ppermute | solution.py:13
  79.8 18.1 %collective-permute-done.1 = f32[2,512,256]{2,1,0:T(8,128)} collective-permute-done((f32[2,512,256]{2,1,0:T(8,128)}, f32[2,512,256]{2,1,0:T(8,128)}, u32[]{:S(2)}, u32[]{:S(2)}) %collective-permute-start.1) | collective-permute-done | bytes 1048608 | tf_op jit(solution)/shard_map/ppermute | solution.py:13
  102.6 4.2 collective-permute-done.17
  110.2 3.2 collective-permute-done.9
  131.4 3.3 collective-permute-start.28
  134.9 6.3 %collective-permute-done.20 = f32[16,384]{0,1:T(8,128)S(1)} collective-permute-done((f32[16,384]{0,1:T(8,128)S(1)}, f32[16,384]{0,1:T(8,128)S(1)}, u32[]{:S(2)}, u32[]{:S(2)}) %collective-permute-start.20) | collective-permute-done | bytes 24608 | tf_op jit(solution)/shard_map/ppermute | solution.py:13
  141.4 6.2 %collective-permute-done.28 = f32[16,384]{0,1:T(8,128)S(1)} collective-permute-done((f32[16,384]{0,1:T(8,128)S(1)}, f32[16,384]{0,1:T(8,128)S(1)}, u32[]{:S(2)}, u32[]{:S(2)}) %collective-permute-start.28) | collective-permute-done | bytes 24608 | tf_op jit(solution)/shard_map/ppermute | solution.py:13
  147.7 4.1 collective-permute-done.12
  151.9 8.6 %collective-permute-done.21 = f32[16,384]{0,1:T(8,128)S(1)} collective-permute-done((f32[16,384]{0,1:T(8,128)S(1)}, f32[16,384]{0,1:T(8,128)S(1)}, u32[]{:S(2)}, u32[]{:S(2)}) %collective-permute-start.21) | collective-permute-done | bytes 24608 | tf_op jit(solution)/shard_map/ppermute | solution.py:13
  160.8 3.8 collective-permute-done.29
  164.5 9.5 %collective-permute-start.22 = (f32[32,384]{1,0:T(8,128)S(1)}, f32[32,384]{1,0:T(8,128)S(1)}, u32[]{:S(2)}, u32[]{:S(2)}) collective-permute-start(f32[32,384]{1,0:T(8,128)S(1)} %pad_maximum_fusion.8), channel_id=1, source_target_pairs={{0,16},{8,24},{16,0},{24,8},{1,17},{9,25},{17,1},{25,9},{2,18},{10... | collective-permute-start | bytes 147464 | tf_op jit(solution)/shard_map/ppermute | solution.py:13
  176.1 3.7 collective-permute-start.14
  195.0 3.1 collective-permute-done.16
  217.2 2.9 fusion.10
  227.3 4.5 add_add_fusion
  231.9 5.5 copy.54
  237.4 4.5 fusion.3
  243.8 11.7 %cholesky.222 = f32[128,128]{1,0:T(8,128)S(1)} custom-call(f32[128,128]{1,0:T(8,128)S(1)} %cholesky.577), custom_call_target="Cholesky" | custom-call | tf_op jit(solution)/shard_map/jit(cholesky)/cholesky | solution.py:177
  258.7 9.8 %custom-call.63 = f32[1,128,128]{1,2,0:T(8,128)S(1)} custom-call(f32[1,128,128]{2,1,0:T(8,128)S(1)} %get-tuple-element.118), custom_call_target="InvertDiagBlocksLowerTriangular" | custom-call | tf_op jit(solution)/shard_map/jit(cholesky)/cholesky | solution.py:177
  272.5 11.9 %cholesky.242 = f32[128,128]{1,0:T(8,128)S(1)} custom-call(f32[128,128]{1,0:T(8,128)S(1)} %cholesky.581), custom_call_target="Cholesky" | custom-call | tf_op jit(solution)/shard_map/jit(cholesky)/cholesky | solution.py:177
  285.6 9.8 %custom-call.64 = f32[1,128,128]{1,2,0:T(8,128)S(1)} custom-call(f32[1,128,128]{2,1,0:T(8,128)S(1)} %get-tuple-element.115), custom_call_target="InvertDiagBlocksLowerTriangular" | custom-call | tf_op jit(solution)/shard_map/jit(cholesky)/cholesky | solution.py:177
  298.8 11.7 %cholesky.465 = f32[128,128]{1,0:T(8,128)S(1)} custom-call(f32[128,128]{1,0:T(8,128)S(1)} %cholesky.586), custom_call_target="Cholesky" | custom-call | tf_op jit(solution)/shard_map/jit(cholesky)/cholesky | solution.py:177
  311.8 9.8 %custom-call.65 = f32[1,128,128]{1,2,0:T(8,128)S(1)} custom-call(f32[1,128,128]{2,1,0:T(8,128)S(1)} %get-tuple-element.112), custom_call_target="InvertDiagBlocksLowerTriangular" | custom-call | tf_op jit(solution)/shard_map/jit(cholesky)/cholesky | solution.py:177
  325.2 12.1 %cholesky.484 = f32[128,128]{1,0:T(8,128)S(1)} custom-call(f32[128,128]{1,0:T(8,128)S(1)} %cholesky.591), custom_call_target="Cholesky" | custom-call | tf_op jit(solution)/shard_map/jit(cholesky)/cholesky | solution.py:177
  338.6 9.8 %custom-call.66 = f32[1,128,128]{1,2,0:T(8,128)S(1)} custom-call(f32[1,128,128]{2,1,0:T(8,128)S(1)} %get-tuple-element.109), custom_call_target="InvertDiagBlocksLowerTriangular" | custom-call | tf_op jit(solution)/shard_map/jit(cholesky)/cholesky | solution.py:177
  351.8 11.7 %cholesky.503 = f32[128,128]{1,0:T(8,128)S(1)} custom-call(f32[128,128]{1,0:T(8,128)S(1)} %cholesky.596), custom_call_target="Cholesky" | custom-call | tf_op jit(solution)/shard_map/jit(cholesky)/cholesky | solution.py:177
  364.8 10.0 %custom-call.67 = f32[1,128,128]{1,2,0:T(8,128)S(1)} custom-call(f32[1,128,128]{2,1,0:T(8,128)S(1)} %get-tuple-element.106), custom_call_target="InvertDiagBlocksLowerTriangular" | custom-call | tf_op jit(solution)/shard_map/jit(cholesky)/cholesky | solution.py:177
  378.1 11.7 %cholesky.523 = f32[128,128]{1,0:T(8,128)S(1)} custom-call(f32[128,128]{1,0:T(8,128)S(1)} %cholesky.601), custom_call_target="Cholesky" | custom-call | tf_op jit(solution)/shard_map/jit(cholesky)/cholesky | solution.py:177
  391.2 9.8 %custom-call.68 = f32[1,128,128]{1,2,0:T(8,128)S(1)} custom-call(f32[1,128,128]{2,1,0:T(8,128)S(1)} %get-tuple-element.103), custom_call_target="InvertDiagBlocksLowerTriangular" | custom-call | tf_op jit(solution)/shard_map/jit(cholesky)/cholesky | solution.py:177
  404.0 11.9 %cholesky.543 = f32[128,128]{1,0:T(8,128)S(1)} custom-call(f32[128,128]{1,0:T(8,128)S(1)} %cholesky.606), custom_call_target="Cholesky" | custom-call | tf_op jit(solution)/shard_map/jit(cholesky)/cholesky | solution.py:177
  417.2 9.8 %custom-call.69 = f32[1,128,128]{1,2,0:T(8,128)S(1)} custom-call(f32[1,128,128]{2,1,0:T(8,128)S(1)} %get-tuple-element.100), custom_call_target="InvertDiagBlocksLowerTriangular" | custom-call | tf_op jit(solution)/shard_map/jit(cholesky)/cholesky | solution.py:177
  429.7 11.7 %cholesky.561 = f32[128,128]{1,0:T(8,128)S(1)} custom-call(f32[128,128]{1,0:T(8,128)S(1)} %convolution_subtract_fusion.6), custom_call_target="Cholesky" | custom-call | tf_op jit(solution)/shard_map/jit(cholesky)/cholesky | solution.py:177
  447.8 4.8 fusion.4
  453.7 29.0 %while.1 = (s32[]{:T(128)}, f32[1024,1024]{1,0:T(8,128)}, s32[8,2]{0,1:T(2,128)S(1)}, f32[8,128,128]{2,1,0:T(8,128)}, s32[]{:T(128)}) while((s32[]{:T(128)}, f32[1024,1024]{1,0:T(8,128)}, s32[8,2]{0,1:T(2,128)S(1)}, f32[8,128,128]{2,1,0:T(8,128)}, s32[]{:T(128)}) %tuple.93), condition=%wide.while_cond, body=%wide.while_body.sunk | while | flops 2 | bytes 132205 | solution.py:178
  454.4 3.0 bitcast_dynamic-update-slice_fusion.2
  458.0 3.0 bitcast_dynamic-update-slice_fusion.2
  461.6 3.0 bitcast_dynamic-update-slice_fusion.2
  465.3 3.0 bitcast_dynamic-update-slice_fusion.2
  468.9 3.0 bitcast_dynamic-update-slice_fusion.2
  472.5 3.0 bitcast_dynamic-update-slice_fusion.2
  476.2 3.0 bitcast_dynamic-update-slice_fusion.2
  482.7 79.8 %custom-call.70 = f32[8,128,128]{1,2,0:T(8,128)S(1)} custom-call(f32[8,128,128]{2,1,0:T(8,128)} %get-tuple-element.9), custom_call_target="InvertDiagBlocksLowerTriangular" | custom-call | tf_op jit(solution)/shard_map/jit(_solve_triangular)/triangular_solve | solution.py:178
  581.5 3.8 fusion.49
  (279 shorter events, 164.2 us)
Async XLA Ops:
  6.0 7.9 %copy-start.11 = (bf16[256,512]{1,0:T(8,128)(2,1)S(1)}, bf16[256,512]{1,0:T(8,128)(2,1)}, u32[]{:S(2)}) copy-start(bf16[256,512]{1,0:T(8,128)(2,1)} %param.3) | copy-start | bytes 786436
  10.9 41.5 %collective-permute-start = (f32[2,512,256]{2,1,0:T(8,128)S(1)}, f32[2,512,256]{2,1,0:T(8,128)}, u32[]{:S(2)}, u32[]{:S(2)}) collective-permute-start(f32[2,512,256]{2,1,0:T(8,128)S(1)} %get-tuple-element.30), channel_id=1, source_target_pairs={{0,1},{1,0},{2,3},{3,2},{4,5},{5,4},{6,7},{7,6},{8,9},{9,8},{10,11... | collective-permute-start | bytes 3145736 | tf_op jit(solution)/shard_map/ppermute | solution.py:13
  14.0 34.4 %collective-permute-start.4 = (f32[256,512]{1,0:T(8,128)S(1)}, f32[256,512]{1,0:T(8,128)}, u32[]{:S(2)}, u32[]{:S(2)}) collective-permute-start(f32[256,512]{1,0:T(8,128)S(1)} %convert_element_type.65), channel_id=1, source_target_pairs={{0,1},{1,0},{2,3},{3,2},{4,5},{5,4},{6,7},{7,6},{8,9},{9,8},{10,11... | collective-permute-start | bytes 1572872 | tf_op jit(solution)/shard_map/ppermute | solution.py:13
  50.7 26.4 %collective-permute-start.5 = (f32[256,1024]{1,0:T(8,128)}, f32[256,1024]{1,0:T(8,128)}, u32[]{:S(2)}, u32[]{:S(2)}) collective-permute-start(f32[256,1024]{1,0:T(8,128)} %pad_maximum_fusion), channel_id=1, source_target_pairs={{0,16},{8,24},{16,0},{24,8},{1,17},{9,25},{17,1},{25,9},{2,18},{10... | collective-permute-start | bytes 3145736 | tf_op jit(solution)/shard_map/ppermute | solution.py:13
  52.4 26.0 %collective-permute-start.6 = (f32[256,1024]{1,0:T(8,128)}, f32[256,1024]{1,0:T(8,128)}, u32[]{:S(2)}, u32[]{:S(2)}) collective-permute-start(f32[256,1024]{1,0:T(8,128)} %pad_maximum_fusion), channel_id=1, source_target_pairs={{0,8},{8,0},{16,24},{24,16},{1,9},{9,1},{17,25},{25,17},{2,10},{10... | collective-permute-start | bytes 3145736 | tf_op jit(solution)/shard_map/ppermute | solution.py:13
  56.1 3.5 copy-start.1
  56.3 1.5 copy-start.3
  59.0 38.8 %collective-permute-start.8 = (f32[256,1152]{0,1:T(8,128)}, f32[256,1152]{0,1:T(8,128)}, u32[]{:S(2)}, u32[]{:S(2)}) collective-permute-start(f32[256,1152]{0,1:T(8,128)} %constant_dynamic-slice_fusion.13), channel_id=1, source_target_pairs={{0,8},{8,0},{16,24},{24,16},{1,9},{9,1},{17,25},{25,17},{2,10},{10... | collective-permute-start | bytes 3538952 | tf_op jit(solution)/shard_map/ppermute | solution.py:13
  64.3 33.5 %collective-permute-start.1 = (f32[2,512,256]{2,1,0:T(8,128)}, f32[2,512,256]{2,1,0:T(8,128)}, u32[]{:S(2)}, u32[]{:S(2)}) collective-permute-start(f32[2,512,256]{2,1,0:T(8,128)} %collective-permute-done), channel_id=1, source_target_pairs={{0,16},{8,24},{16,0},{24,8},{1,17},{9,25},{17,1},{25,9},{2,18},{10... | collective-permute-start | bytes 3145736 | tf_op jit(solution)/shard_map/ppermute | solution.py:13
  66.1 2.0 copy-start.5
  69.4 28.4 %copy-start.4 = (f32[512,1152]{0,1:T(8,128)S(1)}, f32[512,1152]{0,1:T(8,128)}, u32[]{:S(2)}) copy-start(f32[512,1152]{0,1:T(8,128)} %copy-done.3) | copy-start | bytes 7077892
  69.4 129.9 %collective-permute-start.2 = (f32[2,512,256]{2,1,0:T(8,128)}, f32[2,512,256]{2,1,0:T(8,128)}, u32[]{:S(2)}, u32[]{:S(2)}) collective-permute-start(f32[2,512,256]{2,1,0:T(8,128)} %collective-permute-done), channel_id=1, source_target_pairs={{0,8},{8,0},{16,24},{24,16},{1,9},{9,1},{17,25},{25,17},{2,10},{10... | collective-permute-start | bytes 3145736 | tf_op jit(solution)/shard_map/ppermute | solution.py:13
  77.1 128.9 %collective-permute-start.7 = (f32[256,1024]{1,0:T(8,128)}, f32[256,1024]{1,0:T(8,128)}, u32[]{:S(2)}, u32[]{:S(2)}) collective-permute-start(f32[256,1024]{1,0:T(8,128)} %collective-permute-done.5), channel_id=1, source_target_pairs={{0,8},{8,0},{16,24},{24,16},{1,9},{9,1},{17,25},{25,17},{2,10},{10... | collective-permute-start | bytes 3145736 | tf_op jit(solution)/shard_map/ppermute | solution.py:13
  97.8 112.0 %collective-permute-start.3 = (f32[2,512,256]{2,1,0:T(8,128)}, f32[2,512,256]{2,1,0:T(8,128)}, u32[]{:S(2)}, u32[]{:S(2)}) collective-permute-start(f32[2,512,256]{2,1,0:T(8,128)} %collective-permute-done.1), channel_id=1, source_target_pairs={{0,8},{8,0},{16,24},{24,16},{1,9},{9,1},{17,25},{25,17},{2,10},{10... | collective-permute-start | bytes 3145736 | tf_op jit(solution)/shard_map/ppermute | solution.py:13
  99.5 7.4 %collective-permute-start.17 = (f32[128,384]{0,1:T(8,128)S(1)}, f32[128,384]{0,1:T(8,128)S(1)}, u32[]{:S(2)}, u32[]{:S(2)}) collective-permute-start(f32[128,384]{0,1:T(8,128)S(1)} %constant_dynamic-slice_fusion.8), channel_id=1, source_target_pairs={{0,1},{1,0},{2,3},{3,2},{4,5},{5,4},{6,7},{7,6},{8,9},{9,8},{10,11... | collective-permute-start | bytes 589832 | tf_op jit(solution)/shard_map/ppermute | solution.py:13
  101.0 7.4 %collective-permute-start.25 = (f32[128,384]{0,1:T(8,128)S(1)}, f32[128,384]{0,1:T(8,128)S(1)}, u32[]{:S(2)}, u32[]{:S(2)}) collective-permute-start(f32[128,384]{0,1:T(8,128)S(1)} %constant_dynamic-slice_fusion.4), channel_id=1, source_target_pairs={{0,2},{2,0},{4,6},{6,4},{1,3},{3,1},{5,7},{7,5},{8,10},{10,8},{12,... | collective-permute-start | bytes 589832 | tf_op jit(solution)/shard_map/ppermute | solution.py:13
  106.8 6.5 %collective-permute-start.9 = (f32[128,384]{0,1:T(8,128)S(1)}, f32[128,384]{0,1:T(8,128)S(1)}, u32[]{:S(2)}, u32[]{:S(2)}) collective-permute-start(f32[128,384]{0,1:T(8,128)S(1)} %constant_dynamic-slice_fusion.12), channel_id=1, source_target_pairs={{0,16},{8,24},{16,0},{24,8},{1,17},{9,25},{17,1},{25,9},{2,18},{10... | collective-permute-start | bytes 589832 | tf_op jit(solution)/shard_map/ppermute | solution.py:13
  108.4 6.5 %collective-permute-start.18 = (f32[64,384]{0,1:T(8,128)S(1)}, f32[64,384]{0,1:T(8,128)S(1)}, u32[]{:S(2)}, u32[]{:S(2)}) collective-permute-start(f32[64,384]{0,1:T(8,128)S(1)} %constant_dynamic-slice_fusion.7), channel_id=1, source_target_pairs={{0,2},{2,0},{4,6},{6,4},{1,3},{3,1},{5,7},{7,5},{8,10},{10,8},{12,... | collective-permute-start | bytes 294920 | tf_op jit(solution)/shard_map/ppermute | solution.py:13
  113.3 5.7 collective-permute-start.26
  114.9 5.8 collective-permute-start.10
  119.0 5.7 collective-permute-start.19
  120.6 5.7 collective-permute-start.27
  124.7 6.7 %collective-permute-start.11 = (f32[32,384]{0,1:T(8,128)S(1)}, f32[32,384]{0,1:T(8,128)S(1)}, u32[]{:S(2)}, u32[]{:S(2)}) collective-permute-start(f32[32,384]{0,1:T(8,128)S(1)} %constant_dynamic-slice_fusion.10), channel_id=1, source_target_pairs={{0,2},{2,0},{4,6},{6,4},{1,3},{3,1},{5,7},{7,5},{8,10},{10,8},{12,... | collective-permute-start | bytes 147464 | tf_op jit(solution)/shard_map/ppermute | solution.py:13
  126.4 14.9 %collective-permute-start.20 = (f32[16,384]{0,1:T(8,128)S(1)}, f32[16,384]{0,1:T(8,128)S(1)}, u32[]{:S(2)}, u32[]{:S(2)}) collective-permute-start(f32[16,384]{0,1:T(8,128)S(1)} %constant_dynamic-slice_fusion.5), channel_id=1, source_target_pairs={{0,4},{2,6},{4,0},{6,2},{1,5},{3,7},{5,1},{7,3},{8,12},{10,14},{12... | collective-permute-start | bytes 73736 | tf_op jit(solution)/shard_map/ppermute | solution.py:13
  131.4 16.2 %collective-permute-start.28 = (f32[16,384]{0,1:T(8,128)S(1)}, f32[16,384]{0,1:T(8,128)S(1)}, u32[]{:S(2)}, u32[]{:S(2)}) collective-permute-start(f32[16,384]{0,1:T(8,128)S(1)} %constant_dynamic-slice_fusion.1), channel_id=1, source_target_pairs={{0,4},{2,6},{4,0},{6,2},{1,5},{3,7},{5,1},{7,3},{8,12},{10,14},{12... | collective-permute-start | bytes 73736 | tf_op jit(solution)/shard_map/ppermute | solution.py:13
  141.2 10.5 %collective-permute-start.12 = (f32[16,384]{0,1:T(8,128)S(1)}, f32[16,384]{0,1:T(8,128)S(1)}, u32[]{:S(2)}, u32[]{:S(2)}) collective-permute-start(f32[16,384]{0,1:T(8,128)S(1)} %constant_dynamic-slice_fusion.9), channel_id=1, source_target_pairs={{0,4},{2,6},{4,0},{6,2},{1,5},{3,7},{5,1},{7,3},{8,12},{10,14},{12... | collective-permute-start | bytes 73736 | tf_op jit(solution)/shard_map/ppermute | solution.py:13
  147.6 13.0 %collective-permute-start.21 = (f32[16,384]{0,1:T(8,128)S(1)}, f32[16,384]{0,1:T(8,128)S(1)}, u32[]{:S(2)}, u32[]{:S(2)}) collective-permute-start(f32[16,384]{0,1:T(8,128)S(1)} %dynamic-slice_add_fusion.5), channel_id=1, source_target_pairs={{0,4},{2,6},{4,0},{6,2},{1,5},{3,7},{5,1},{7,3},{8,12},{10,14},{12... | collective-permute-start | bytes 73736 | tf_op jit(solution)/shard_map/ppermute | solution.py:13
  151.8 12.7 %collective-permute-start.29 = (f32[16,384]{0,1:T(8,128)S(1)}, f32[16,384]{0,1:T(8,128)S(1)}, u32[]{:S(2)}, u32[]{:S(2)}) collective-permute-start(f32[16,384]{0,1:T(8,128)S(1)} %dynamic-slice_add_fusion.1), channel_id=1, source_target_pairs={{0,4},{2,6},{4,0},{6,2},{1,5},{3,7},{5,1},{7,3},{8,12},{10,14},{12... | collective-permute-start | bytes 73736 | tf_op jit(solution)/shard_map/ppermute | solution.py:13
  160.5 13.8 %collective-permute-start.13 = (f32[16,384]{0,1:T(8,128)S(1)}, f32[16,384]{0,1:T(8,128)S(1)}, u32[]{:S(2)}, u32[]{:S(2)}) collective-permute-start(f32[16,384]{0,1:T(8,128)S(1)} %dynamic-slice_add_fusion.9), channel_id=1, source_target_pairs={{0,4},{2,6},{4,0},{6,2},{1,5},{3,7},{5,1},{7,3},{8,12},{10,14},{12... | collective-permute-start | bytes 73736 | tf_op jit(solution)/shard_map/ppermute | solution.py:13
  164.5 11.6 %collective-permute-start.22 = (f32[32,384]{1,0:T(8,128)S(1)}, f32[32,384]{1,0:T(8,128)S(1)}, u32[]{:S(2)}, u32[]{:S(2)}) collective-permute-start(f32[32,384]{1,0:T(8,128)S(1)} %pad_maximum_fusion.8), channel_id=1, source_target_pairs={{0,16},{8,24},{16,0},{24,8},{1,17},{9,25},{17,1},{25,9},{2,18},{10... | collective-permute-start | bytes 147464 | tf_op jit(solution)/shard_map/ppermute | solution.py:13
  174.3 5.6 collective-permute-start.30
  176.1 6.0 %collective-permute-start.14 = (f32[32,384]{1,0:T(8,128)S(1)}, f32[32,384]{1,0:T(8,128)S(1)}, u32[]{:S(2)}, u32[]{:S(2)}) collective-permute-start(f32[32,384]{1,0:T(8,128)S(1)} %pad_maximum_fusion.7), channel_id=1, source_target_pairs={{0,2},{2,0},{4,6},{6,4},{1,3},{3,1},{5,7},{7,5},{8,10},{10,8},{12,... | collective-permute-start | bytes 147464 | tf_op jit(solution)/shard_map/ppermute | solution.py:13
  179.9 4.8 collective-permute-start.23
  182.1 4.7 collective-permute-start.31
  184.7 4.6 collective-permute-start.15
  186.8 5.7 collective-permute-start.24
  189.3 5.7 collective-permute-start.32
  192.5 5.7 collective-permute-start.16
  195.0 4.3 copy-start.7
  195.0 4.3 copy-start.8
  198.2 1.1 copy-start.9
  198.2 1.1 copy-start.10
  199.3 12.9 %collective-permute-start.33 = (f32[256,1152]{1,0:T(8,128)}, f32[256,1152]{1,0:T(8,128)}, u32[]{:S(2)}, u32[]{:S(2)}) collective-permute-start(f32[256,1152]{1,0:T(8,128)} %maximum_maximum_fusion.1), channel_id=1, source_target_pairs={{0,8},{8,0},{16,24},{24,16},{1,9},{9,1},{17,25},{25,17},{2,10},{10... | collective-permute-start | bytes 3538952 | tf_op jit(solution)/shard_map/ppermute | solution.py:13
  213.8 0.7 copy-start.12
  241.8 1.9 copy-start.2
  447.8 5.9 copy-start.13
  562.5 5.6 copy-start
  580.8 5.1 copy-start.6

commit v2 on v1

--- a/solution.py
+++ b/solution.py
@@ -4,6 +4,8 @@
 import jax
 import jax.numpy as jnp
 from jax import lax
+from jax.experimental import pallas as pl
+from jax.experimental.pallas import tpu as pltpu
 from jax.sharding import PartitionSpec as P
 
 BLOCK = 128
@@ -111,6 +113,140 @@
     return jnp.concatenate(rows, 0)
 
 
+def sub(x, s):
+    return jnp.broadcast_to(x[s : s + 1, :], x.shape)
+
+
+def lane(x, k):
+    return jnp.broadcast_to(x[:, k : k + 1], x.shape)
+
+
+def inverse_factor(block):
+    n, wide = BLOCK // 8, 8
+    rows = [block[8 * b : 8 * b + 8] for b in range(n)]
+    sub_id = lax.broadcasted_iota(jnp.int32, (8, BLOCK), 0)
+    lane_id = lax.broadcasted_iota(jnp.int32, (8, BLOCK), 1)
+    pivots = []
+    head = [lane(rows[0], c) for c in range(wide)]
+    for b in range(n):
+        k = wide * b
+        cols = [[head[c]] + [lane(rows[i], k + c) for i in range(b + 1, n)] for c in range(wide)]
+        if b + 1 < n:
+            head = [lane(rows[b + 1], k + wide + c) for c in range(wide)]
+        inside = (lane_id >= k) & (lane_id < k + wide)
+        for i in range(b, n):
+            rows[i] = jnp.where(inside, 0.0, rows[i])
+        pivot = jnp.ones((8, BLOCK), jnp.float32)
+        for c in range(wide):
+            d = sub(cols[c][0], c)
+            inverse = 1.0 / d
+            pivot = jnp.where(sub_id == c, d, pivot)
+            for c2 in range(c + 1, wide):
+                m = sub(cols[c][0], c2) * inverse
+                for i in range(n - b):
+                    cols[c2][i] = cols[c2][i] - cols[c][i] * m
+            factors = [cols[c][i] * inverse for i in range(n - b)]
+            if b + 1 < n:
+                for c2 in range(wide):
+                    head[c2] = head[c2] - factors[1] * sub(cols[c][1], c2)
+            factors[0] = jnp.where(sub_id > c, factors[0], 0.0)
+            row = jnp.where(lane_id == k + c, 1.0, sub(rows[b], c))
+            for i in range(n - b):
+                rows[b + i] = rows[b + i] - factors[i] * row
+        pivots.append(pivot)
+    out = []
+    for b in range(n):
+        diagonal = sub_id + 8 * b
+        row = jnp.where(lane_id < diagonal, rows[b], jnp.where(lane_id == diagonal, 1.0, 0.0))
+        out.append(row * lax.rsqrt(pivots[b]))
+    return jnp.concatenate(out, 0)
+
+
+def split(x, pieces):
+    out = []
+    for i in range(pieces):
+        out.append(x.astype(jnp.bfloat16))
+        if i + 1 < pieces:
+            x = x - out[-1].astype(jnp.float32)
+    return out
+
+
+def product(a, b):
+    terms = [
+        jnp.dot(a[i], b[j], preferred_element_type=jnp.float32)
+        for i in range(len(a))
+        for j in range(len(b))
+        if i + j < max(len(a), len(b))
+    ]
+    return sum(terms[1:], terms[0])
+
+
+PIECES = 2
+
+
+def factor_kernel(scale, at_ref, gram_ref, left_ref, factor_ref, weights_ref, now, solved, lows, low):
+    chi = gram_ref.shape[0]
+    n = chi // BLOCK
+    solved[...] = jnp.zeros_like(solved)
+    lows[...] = jnp.zeros_like(lows)
+    now[:, :chi] = gram_ref[:BLOCK]
+    now[:, chi:] = left_ref[:BLOCK].astype(jnp.float32)
+
+    def body(j, _):
+        here = pl.ds(pl.multiple_of(j * BLOCK, BLOCK), BLOCK)
+        after = pl.ds(pl.multiple_of(jnp.minimum(j + 1, n - 1) * BLOCK, BLOCK), BLOCK)
+        inverse = split(inverse_factor(now[:, here]), PIECES)
+        multiples = [lows[i, after, :] for i in range(PIECES)]
+        next_gram = gram_ref[after, :] - product(multiples, [solved[i, :, :chi] for i in range(PIECES)])
+        next_left = left_ref[after, :].astype(jnp.float32) - product(
+            multiples, [solved[i, :, chi:] for i in range(PIECES)]
+        )
+        row = now[...]
+        row_gram = product(inverse, split(row[:, :chi], PIECES))
+        row_left = product(inverse, split(row[:, chi:], PIECES))
+        row_gram_pieces, row_left_pieces = split(row_gram, PIECES), split(row_left, PIECES)
+        for i in range(PIECES):
+            solved[i, here, :chi] = row_gram_pieces[i]
+            solved[i, here, chi:] = row_left_pieces[i]
+        low[:, here] = row_gram.T
+        for i, piece in enumerate(split(low[:, here], PIECES)):
+            lows[i, :, here] = piece
+        multiples = [lows[i, after, here] for i in range(PIECES)]
+        now[:, :chi] = next_gram - product(multiples, row_gram_pieces)
+        now[:, chi:] = next_left - product(multiples, row_left_pieces)
+        return 0
+
+    lax.fori_loop(0, n, body, 0)
+    rows = factor_ref.shape[0]
+    mine = pl.ds(pl.multiple_of(at_ref[0], 16), rows)
+    row_id = lax.broadcasted_iota(jnp.int32, (rows, chi), 0) + at_ref[0]
+    column_id = lax.broadcasted_iota(jnp.int32, (rows, chi), 1)
+    factor_ref[...] = jnp.where(column_id <= row_id, low[mine, :] * (1.0 / scale), 0.0)
+    weights_ref[...] = solved[0, mine, chi:]
+
+
+def factorize(gram, left, at, rows, scale):
+    chi = gram.shape[0]
+    whole = pl.BlockSpec(memory_space=pltpu.VMEM)
+    return pl.pallas_call(
+        functools.partial(factor_kernel, scale),
+        out_shape=[
+            jax.ShapeDtypeStruct((rows, chi), jnp.float32),
+            jax.ShapeDtypeStruct((rows, chi), jnp.bfloat16),
+        ],
+        in_specs=[pl.BlockSpec(memory_space=pltpu.SMEM), whole, whole],
+        out_specs=[whole, whole],
+        scratch_shapes=[
+            pltpu.VMEM((BLOCK, 2 * chi), jnp.float32),
+            pltpu.VMEM((PIECES, chi, 2 * chi), jnp.bfloat16),
+            pltpu.VMEM((PIECES, chi, chi), jnp.bfloat16),
+            pltpu.VMEM((chi, chi), jnp.float32),
+        ],
+        compiler_params=pltpu.CompilerParams(vmem_limit_bytes=48 * 2**20),
+        cost_estimate=pl.CostEstimate(flops=6 * 2 * chi**3, bytes_accessed=8 * chi**2, transcendentals=0),
+    )(at, gram, left)
+
+
 def shards(sizes, left_factor, boundary_site, double_layer):
     lb, rb, rep = sizes["lb"], sizes["rb"], sizes["rep"]
     highest = lax.Precision.HIGHEST
@@ -174,11 +310,10 @@
     product = sum(dot(left, piece) for piece in split3(lower_half)[::-1])
     half_gram = sum(dot(piece, left.T) for piece in split3(product)[::-1])
     gram = half_gram + half_gram.T
-    lower = jnp.linalg.cholesky(gram)
-    weights = jax.scipy.linalg.solve_triangular(lower, left.astype(jnp.float32), lower=True)
-    weights = lax.dynamic_slice_in_dim(weights, l * row_count, row_count, 0)
-
     scale = math.sqrt(phys * rb * right)
+    at = (l * row_count).astype(jnp.int32)[None]
+    factor, weights = factorize(gram, left, at, row_count, scale)
+
     site = jnp.zeros((east, chi, right), jnp.bfloat16)
     site = lax.dynamic_update_slice(site, own, (0, p * depth, 0))
     for s, got in zip(range(1, rep), others):
@@ -187,10 +322,7 @@
             at = ((owner // right_parts) * east_part, (p ^ s) * depth, (owner % right_parts) * right_part)
             piece = (piece + nothing).astype(jnp.bfloat16)
             site = lax.dynamic_update_slice(site, piece, at)
-    site_q = jnp.einsum(
-        "ik,ekr->eir", (weights * scale).astype(jnp.bfloat16), site, preferred_element_type=jnp.float32
-    )
-    factor = lax.dynamic_slice_in_dim(lower, l * row_count, row_count, 0) / scale
+    site_q = jnp.einsum("ik,ekr->eir", weights, site, preferred_element_type=jnp.float32) * scale
     return (site_q, factor)
 
 

time: 596 us -> 297 us (0.50)
  other arithmetic: 287 us -> 27.6 us
  matrix products: 71.4 us -> 24.6 us
  Pallas kernels: 0 us -> 45.9 us
  local copies, waits for them, and re-layouts: 65.3 us -> 33.8 us
  waiting for transfers between devices: 108 us -> 124 us
  starting transfers between devices: 49.6 us -> 37.7 us
    another operation x34 -> x0, other arithmetic: 258 us -> none  [the longest x31 173 us: shards(): lower = jnp.linalg.cholesky(gram)]
    another operation x29 -> x0, matrix products: 46.3 us -> none  [the longest x15 23.3 us: shards(): jax.scipy.linalg.solve_triangular(lower, left.astype(jnp.float32), lower=...]
    pallas_call x0 -> x1, Pallas kernels: none -> 45.9 us  [factorize(): pl.pallas_call(functools.partial(factor_kernel, scale), out_shape=[jax.Sh...]
    another operation x33 -> x0, local copies, waits for them, and re-layouts: 31.6 us -> none
    ppermute x34, waiting for transfers between devices: 108 us -> 124 us  [swap(): return lax.ppermute(array, axis, [(i, i ^ distance) for i in range(size)])]
    ppermute x34, starting transfers between devices: 49.6 us -> 37.7 us  [swap(): return lax.ppermute(array, axis, [(i, i ^ distance) for i in range(size)])]
    add x0 -> x1, other arithmetic: none -> 6.9 us  [shards(): gram = half_gram + half_gram.T]
  transfers between devices with their start and end apart: 34 -> 34, of which waited for: 19 -> 23; matrix products, arithmetic and copies ran while one was open for 7% -> 13% of each run, Pallas kernels for 0% -> 0%
where the time goes in v2:
time: 297 us; the launch traced here: 296 us
  waiting for transfers between devices  124 us (42%)
  Pallas kernels  45.9 us (15%)
  starting transfers between devices  37.7 us (13%)
  local copies, waits for them, and re-layouts  33.8 us (11%)
  other arithmetic  27.6 us (9%)
  matrix products  24.6 us (8%)
    ppermute x34, waiting for transfers between devices, swap(): return lax.ppermute(array, axis, [(i, i ^ distance) for i in range(size)])  124 us
    pallas_call x1, Pallas kernels, factorize(): pl.pallas_call(functools.partial(factor_kernel, scale), out_shape=[jax.Sh...  45.9 us
    ppermute x34, starting transfers between devices, swap(): return lax.ppermute(array, axis, [(i, i ^ distance) for i in range(size)])  37.7 us
    dot_general x3, matrix products, shards(): half_gram = sum((dot(piece, left.T) for piece in split3(product)[::-1]))  9.27 us
    dot_general x3, matrix products, shards(): product = sum((dot(left, piece) for piece in split3(lower_half)[::-1]))  7.44 us
    add x1, other arithmetic, shards(): gram = half_gram + half_gram.T  6.9 us
    dynamic_slice x2, local copies, waits for them, and re-layouts, shards(): own = lax.dynamic_slice_in_dim(absorbed, p * east, east, 0)  6.08 us
  transfers between devices with their start and end apart: 34, of which 23 were waited for; matrix products, arithmetic and copies ran while one was open for 13% of the time, Pallas kernels for 0%

profile of v2, /device:TPU:0, one launch (start us, length us, event | category | flops | bytes accessed | tf_op | source)
XLA Modules:
  0.0 295.7 jit_solution(1306785747893592382)
XLA Ops:
  0.6 5.4 %fusion.15 = bf16[16,512,256]{2,0,1:T(8,128)(2,1)S(1)} fusion(bf16[512,16,256]{2,1,0:T(8,128)(2,1)} %param.4, f32[16,16]{1,0:T(8,128)} %param.5), kind=kOutput, calls=%fused_computation.126 | convolution fusion | flops 402653184 | bytes 8389632 | tf_op jit(solution)/shard_map/kur,ue->ekr/dot_general | solution.py:269
  6.0 3.5 %copy.61 = bf16[16,512,256]{2,1,0:T(8,128)(2,1)} copy(bf16[16,512,256]{2,0,1:T(8,128)(2,1)S(1)} %fusion.15) | data formatting | bytes 8388608 | tf_op jit(solution)/shard_map/kur,ue->ekr/dot_general | solution.py:269
  10.9 3.0 %collective-permute-start = (f32[2,512,256]{2,1,0:T(8,128)S(1)}, f32[2,512,256]{2,1,0:T(8,128)}, u32[]{:S(2)}, u32[]{:S(2)}) collective-permute-start(f32[2,512,256]{2,1,0:T(8,128)S(1)} %get-tuple-element.14), channel_id=1, source_target_pairs={{0,1},{1,0},{2,3},{3,2},{4,5},{5,4},{6,7},{7,6},{8,9},{9,8},{10,11... | collective-permute-start | bytes 3145736 | tf_op jit(solution)/shard_map/ppermute | solution.py:15
  15.9 32.5 %collective-permute-done.4 = f32[256,512]{1,0:T(8,128)} collective-permute-done((f32[256,512]{1,0:T(8,128)S(1)}, f32[256,512]{1,0:T(8,128)}, u32[]{:S(2)}, u32[]{:S(2)}) %collective-permute-start.4) | collective-permute-done | bytes 524320 | tf_op jit(solution)/shard_map/ppermute | solution.py:15
  50.7 1.7 collective-permute-start.5
  52.4 2.1 constant_dynamic-update-slice_fusion
  59.8 3.0 %constant_dynamic-slice_fusion.13 = bf16[8,512,256]{2,1,0:T(8,128)(2,1)} fusion(bf16[16,512,256]{2,1,0:T(8,128)(2,1)} %copy.61, s32[]{:T(128)S(6)} %select_n.287), kind=kLoop, calls=%fused_computation.125 | loop fusion | bytes 4194308 | tf_op jit(solution)/shard_map/dynamic_slice | solution.py:272
  62.9 3.0 %copy.39 = bf16[8,512,256]{1,2,0:T(8,128)(2,1)S(1)} copy(bf16[8,512,256]{2,1,0:T(8,128)(2,1)} %constant_dynamic-slice_fusion.13) | data formatting | bytes 4194304 | tf_op jit(solution)/shard_map/dynamic_slice | solution.py:272
  68.5 1.6 copy-done.2
  72.4 4.6 %collective-permute-done.5 = f32[256,1024]{1,0:T(8,128)} collective-permute-done((f32[256,1024]{1,0:T(8,128)}, f32[256,1024]{1,0:T(8,128)}, u32[]{:S(2)}, u32[]{:S(2)}) %collective-permute-start.5) | collective-permute-done | bytes 1048608 | tf_op jit(solution)/shard_map/ppermute | solution.py:15
  79.7 18.1 %collective-permute-done.1 = f32[2,512,256]{2,1,0:T(8,128)} collective-permute-done((f32[2,512,256]{2,1,0:T(8,128)}, f32[2,512,256]{2,1,0:T(8,128)}, u32[]{:S(2)}, u32[]{:S(2)}) %collective-permute-start.1) | collective-permute-done | bytes 1048608 | tf_op jit(solution)/shard_map/ppermute | solution.py:15
  97.8 1.5 dynamic-slice_add_fusion
  99.4 1.5 collective-permute-start.25
  101.0 1.6 collective-permute-start.17
  102.6 4.2 %collective-permute-done.25 = f32[128,384]{0,1:T(8,128)S(1)} collective-permute-done((f32[128,384]{0,1:T(8,128)S(1)}, f32[128,384]{0,1:T(8,128)S(1)}, u32[]{:S(2)}, u32[]{:S(2)}) %collective-permute-start.25) | collective-permute-done | bytes 196640 | tf_op jit(solution)/shard_map/ppermute | solution.py:15
  109.7 4.9 %collective-permute-done.9 = f32[128,384]{0,1:T(8,128)S(1)} collective-permute-done((f32[128,384]{0,1:T(8,128)S(1)}, f32[128,384]{0,1:T(8,128)S(1)}, u32[]{:S(2)}, u32[]{:S(2)}) %collective-permute-start.9) | collective-permute-done | bytes 196640 | tf_op jit(solution)/shard_map/ppermute | solution.py:15
  121.9 3.3 %collective-permute-done.10 = f32[64,384]{0,1:T(8,128)S(1)} collective-permute-done((f32[64,384]{0,1:T(8,128)S(1)}, f32[64,384]{0,1:T(8,128)S(1)}, u32[]{:S(2)}, u32[]{:S(2)}) %collective-permute-start.10) | collective-permute-done | bytes 98336 | tf_op jit(solution)/shard_map/ppermute | solution.py:15
  129.1 1.9 collective-permute-done.19
  130.9 2.5 collective-permute-start.28
  135.1 1.9 collective-permute-start.20
  137.2 10.9 %collective-permute-done.28 = f32[16,384]{0,1:T(8,128)S(1)} collective-permute-done((f32[16,384]{0,1:T(8,128)S(1)}, f32[16,384]{0,1:T(8,128)S(1)}, u32[]{:S(2)}, u32[]{:S(2)}) %collective-permute-start.28) | collective-permute-done | bytes 24608 | tf_op jit(solution)/shard_map/ppermute | solution.py:15
  148.2 8.3 %collective-permute-done.20 = f32[16,384]{0,1:T(8,128)S(1)} collective-permute-done((f32[16,384]{0,1:T(8,128)S(1)}, f32[16,384]{0,1:T(8,128)S(1)}, u32[]{:S(2)}, u32[]{:S(2)}) %collective-permute-start.20) | collective-permute-done | bytes 24608 | tf_op jit(solution)/shard_map/ppermute | solution.py:15
  156.7 4.1 %collective-permute-done.12 = f32[16,384]{0,1:T(8,128)S(1)} collective-permute-done((f32[16,384]{0,1:T(8,128)S(1)}, f32[16,384]{0,1:T(8,128)S(1)}, u32[]{:S(2)}, u32[]{:S(2)}) %collective-permute-start.12) | collective-permute-done | bytes 24608 | tf_op jit(solution)/shard_map/ppermute | solution.py:15
  160.9 8.6 %collective-permute-done.29 = f32[16,384]{0,1:T(8,128)S(1)} collective-permute-done((f32[16,384]{0,1:T(8,128)S(1)}, f32[16,384]{0,1:T(8,128)S(1)}, u32[]{:S(2)}, u32[]{:S(2)}) %collective-permute-start.29) | collective-permute-done | bytes 24608 | tf_op jit(solution)/shard_map/ppermute | solution.py:15
  169.7 2.7 collective-permute-done.21
  172.4 1.6 collective-permute-start.30
  174.2 4.8 %collective-permute-done.13 = f32[16,384]{0,1:T(8,128)S(1)} collective-permute-done((f32[16,384]{0,1:T(8,128)S(1)}, f32[16,384]{0,1:T(8,128)S(1)}, u32[]{:S(2)}, u32[]{:S(2)}) %collective-permute-start.13) | collective-permute-done | bytes 24608 | tf_op jit(solution)/shard_map/ppermute | solution.py:15
  178.9 1.5 collective-permute-start.22
  180.7 3.3 %collective-permute-start.14 = (f32[32,384]{1,0:T(8,128)S(1)}, f32[32,384]{1,0:T(8,128)S(1)}, u32[]{:S(2)}, u32[]{:S(2)}) collective-permute-start(f32[32,384]{1,0:T(8,128)S(1)} %pad_maximum_fusion.7), channel_id=1, source_target_pairs={{0,2},{2,0},{4,6},{6,4},{1,3},{3,1},{5,7},{7,5},{8,10},{10,8},{12,... | collective-permute-start | bytes 147464 | tf_op jit(solution)/shard_map/ppermute | solution.py:15
  186.4 1.8 collective-permute-start.23
  188.7 1.6 collective-permute-start.15
  190.3 1.7 collective-permute-done.23
  192.0 1.7 collective-permute-start.32
  193.8 1.6 collective-permute-start.24
  195.4 2.3 collective-permute-done.32
  199.6 3.8 %collective-permute-done.16 = f32[128,384]{1,0:T(8,128)S(1)} collective-permute-done((f32[128,384]{1,0:T(8,128)S(1)}, f32[128,384]{1,0:T(8,128)S(1)}, u32[]{:S(2)}, u32[]{:S(2)}) %collective-permute-start.16) | collective-permute-done | bytes 196640 | tf_op jit(solution)/shard_map/ppermute | solution.py:15
  206.1 2.1 add_convert_fusion.5
  215.0 1.6 broadcast_select_fusion
  217.6 2.4 fusion.4
  220.0 2.4 fusion.7
  222.4 2.7 add_add_fusion.1
  225.1 2.4 fusion.2
  227.5 2.4 fusion.9
  229.9 4.5 %add_add_fusion = f32[1024,1024]{0,1:T(8,128)} fusion(f32[1024,1024]{0,1:T(8,128)S(1)} %fusion.2, f32[1024,1024]{0,1:T(8,128)S(1)} %fusion.9, bf16[1024,1024]{1,0:T(8,128)(2,1)S(1)} %fusion.13.left_ref, f32[1024,1024]{1,0:T(8,128)S(1)} %add_add_fusion.1), kind=kOutput, calls=%fused_computation.12 | convolution fusion | flops 2151677952 | bytes 18874368 | tf_op jit(solution)/shard_map/dot_general | solution.py:311
  234.4 5.4 %copy.53 = f32[1024,1024]{1,0:T(8,128)} copy(f32[1024,1024]{0,1:T(8,128)} %add_add_fusion) | data formatting | bytes 8388608 | tf_op jit(solution)/shard_map/add | solution.py:311
  239.8 6.9 %bitcast_add_fusion.gram_ref = f32[1024,1024]{1,0:T(8,128)} fusion(f32[1024,1024]{1,0:T(8,128)} %copy.53, f32[1024,1024]{0,1:T(8,128)} %add_add_fusion), kind=kLoop, calls=%fused_computation.11 | loop fusion | flops 1048576 | bytes 12582912 | tf_op jit(solution)/shard_map/add | solution.py:312
  246.7 45.9 %shard_map.50 = (f32[256,1024]{1,0:T(8,128)}, bf16[256,1024]{1,0:T(8,128)(2,1)S(1)}) custom-call(s32[1]{0:T(128)} %bitcast.2.at_ref, f32[1024,1024]{1,0:T(8,128)} %bitcast_add_fusion.gram_ref, bf16[1024,1024]{1,0:T(8,128)(2,1)S(1)} %fusion.13.left_ref), custom_call_target="tpu_custom_call" | custom-call | flops 12884901888 | bytes 8388608 | tf_op jit(solution)/shard_map/pallas_call | solution.py:231
  293.9 1.8 copy.54
  (175 shorter events, 51.0 us)
Async XLA Ops:
  9.5 4.4 %copy-start.8 = (bf16[256,512]{1,0:T(8,128)(2,1)S(1)}, bf16[256,512]{1,0:T(8,128)(2,1)}, u32[]{:S(2)}) copy-start(bf16[256,512]{1,0:T(8,128)(2,1)} %param.3) | copy-start | bytes 786436
  10.9 41.5 %collective-permute-start = (f32[2,512,256]{2,1,0:T(8,128)S(1)}, f32[2,512,256]{2,1,0:T(8,128)}, u32[]{:S(2)}, u32[]{:S(2)}) collective-permute-start(f32[2,512,256]{2,1,0:T(8,128)S(1)} %get-tuple-element.14), channel_id=1, source_target_pairs={{0,1},{1,0},{2,3},{3,2},{4,5},{5,4},{6,7},{7,6},{8,9},{9,8},{10,11... | collective-permute-start | bytes 3145736 | tf_op jit(solution)/shard_map/ppermute | solution.py:15
  14.0 34.4 %collective-permute-start.4 = (f32[256,512]{1,0:T(8,128)S(1)}, f32[256,512]{1,0:T(8,128)}, u32[]{:S(2)}, u32[]{:S(2)}) collective-permute-start(f32[256,512]{1,0:T(8,128)S(1)} %convert_element_type.59), channel_id=1, source_target_pairs={{0,1},{1,0},{2,3},{3,2},{4,5},{5,4},{6,7},{7,6},{8,9},{9,8},{10,11... | collective-permute-start | bytes 1572872 | tf_op jit(solution)/shard_map/ppermute | solution.py:15
  50.7 26.4 %collective-permute-start.5 = (f32[256,1024]{1,0:T(8,128)}, f32[256,1024]{1,0:T(8,128)}, u32[]{:S(2)}, u32[]{:S(2)}) collective-permute-start(f32[256,1024]{1,0:T(8,128)} %pad_maximum_fusion), channel_id=1, source_target_pairs={{0,16},{8,24},{16,0},{24,8},{1,17},{9,25},{17,1},{25,9},{2,18},{10... | collective-permute-start | bytes 3145736 | tf_op jit(solution)/shard_map/ppermute | solution.py:15
  52.4 26.0 %collective-permute-start.6 = (f32[256,1024]{1,0:T(8,128)}, f32[256,1024]{1,0:T(8,128)}, u32[]{:S(2)}, u32[]{:S(2)}) collective-permute-start(f32[256,1024]{1,0:T(8,128)} %pad_maximum_fusion), channel_id=1, source_target_pairs={{0,8},{8,0},{16,24},{24,16},{1,9},{9,1},{17,25},{25,17},{2,10},{10... | collective-permute-start | bytes 3145736 | tf_op jit(solution)/shard_map/ppermute | solution.py:15
  56.3 1.5 copy-start
  59.0 38.8 %collective-permute-start.8 = (f32[256,1152]{0,1:T(8,128)}, f32[256,1152]{0,1:T(8,128)}, u32[]{:S(2)}, u32[]{:S(2)}) collective-permute-start(f32[256,1152]{0,1:T(8,128)} %constant_dynamic-slice_fusion.11), channel_id=1, source_target_pairs={{0,8},{8,0},{16,24},{24,16},{1,9},{9,1},{17,25},{25,17},{2,10},{10... | collective-permute-start | bytes 3538952 | tf_op jit(solution)/shard_map/ppermute | solution.py:15
  59.5 38.3 %collective-permute-start.1 = (f32[2,512,256]{2,1,0:T(8,128)}, f32[2,512,256]{2,1,0:T(8,128)}, u32[]{:S(2)}, u32[]{:S(2)}) collective-permute-start(f32[2,512,256]{2,1,0:T(8,128)} %collective-permute-done), channel_id=1, source_target_pairs={{0,16},{8,24},{16,0},{24,8},{1,17},{9,25},{17,1},{25,9},{2,18},{10... | collective-permute-start | bytes 3145736 | tf_op jit(solution)/shard_map/ppermute | solution.py:15
  68.2 2.0 copy-start.2
  71.4 26.4 %copy-start.1 = (f32[512,1152]{0,1:T(8,128)S(1)}, f32[512,1152]{0,1:T(8,128)}, u32[]{:S(2)}) copy-start(f32[512,1152]{0,1:T(8,128)} %copy-done) | copy-start | bytes 7077892
  71.5 134.7 %collective-permute-start.2 = (f32[2,512,256]{2,1,0:T(8,128)}, f32[2,512,256]{2,1,0:T(8,128)}, u32[]{:S(2)}, u32[]{:S(2)}) collective-permute-start(f32[2,512,256]{2,1,0:T(8,128)} %collective-permute-done), channel_id=1, source_target_pairs={{0,8},{8,0},{16,24},{24,16},{1,9},{9,1},{17,25},{25,17},{2,10},{10... | collective-permute-start | bytes 3145736 | tf_op jit(solution)/shard_map/ppermute | solution.py:15
  77.1 134.1 %collective-permute-start.7 = (f32[256,1024]{1,0:T(8,128)}, f32[256,1024]{1,0:T(8,128)}, u32[]{:S(2)}, u32[]{:S(2)}) collective-permute-start(f32[256,1024]{1,0:T(8,128)} %collective-permute-done.5), channel_id=1, source_target_pairs={{0,8},{8,0},{16,24},{24,16},{1,9},{9,1},{17,25},{25,17},{2,10},{10... | collective-permute-start | bytes 3145736 | tf_op jit(solution)/shard_map/ppermute | solution.py:15
  97.8 114.7 %collective-permute-start.3 = (f32[2,512,256]{2,1,0:T(8,128)}, f32[2,512,256]{2,1,0:T(8,128)}, u32[]{:S(2)}, u32[]{:S(2)}) collective-permute-start(f32[2,512,256]{2,1,0:T(8,128)} %collective-permute-done.1), channel_id=1, source_target_pairs={{0,8},{8,0},{16,24},{24,16},{1,9},{9,1},{17,25},{25,17},{2,10},{10... | collective-permute-start | bytes 3145736 | tf_op jit(solution)/shard_map/ppermute | solution.py:15
  99.4 7.4 %collective-permute-start.25 = (f32[128,384]{0,1:T(8,128)S(1)}, f32[128,384]{0,1:T(8,128)S(1)}, u32[]{:S(2)}, u32[]{:S(2)}) collective-permute-start(f32[128,384]{0,1:T(8,128)S(1)} %constant_dynamic-slice_fusion.2), channel_id=1, source_target_pairs={{0,2},{2,0},{4,6},{6,4},{1,3},{3,1},{5,7},{7,5},{8,10},{10,8},{12,... | collective-permute-start | bytes 589832 | tf_op jit(solution)/shard_map/ppermute | solution.py:15
  101.0 7.4 %collective-permute-start.17 = (f32[128,384]{0,1:T(8,128)S(1)}, f32[128,384]{0,1:T(8,128)S(1)}, u32[]{:S(2)}, u32[]{:S(2)}) collective-permute-start(f32[128,384]{0,1:T(8,128)S(1)} %constant_dynamic-slice_fusion.6), channel_id=1, source_target_pairs={{0,1},{1,0},{2,3},{3,2},{4,5},{5,4},{6,7},{7,6},{8,9},{9,8},{10,11... | collective-permute-start | bytes 589832 | tf_op jit(solution)/shard_map/ppermute | solution.py:15
  106.8 7.8 %collective-permute-start.9 = (f32[128,384]{0,1:T(8,128)S(1)}, f32[128,384]{0,1:T(8,128)S(1)}, u32[]{:S(2)}, u32[]{:S(2)}) collective-permute-start(f32[128,384]{0,1:T(8,128)S(1)} %constant_dynamic-slice_fusion.10), channel_id=1, source_target_pairs={{0,16},{8,24},{16,0},{24,8},{1,17},{9,25},{17,1},{25,9},{2,18},{10... | collective-permute-start | bytes 589832 | tf_op jit(solution)/shard_map/ppermute | solution.py:15
  108.3 9.2 %collective-permute-start.26 = (f32[64,384]{0,1:T(8,128)S(1)}, f32[64,384]{0,1:T(8,128)S(1)}, u32[]{:S(2)}, u32[]{:S(2)}) collective-permute-start(f32[64,384]{0,1:T(8,128)S(1)} %constant_dynamic-slice_fusion.1), channel_id=1, source_target_pairs={{0,16},{8,24},{16,0},{24,8},{1,17},{9,25},{17,1},{25,9},{2,18},{10... | collective-permute-start | bytes 294920 | tf_op jit(solution)/shard_map/ppermute | solution.py:15
  114.6 5.7 %collective-permute-start.18 = (f32[64,384]{0,1:T(8,128)S(1)}, f32[64,384]{0,1:T(8,128)S(1)}, u32[]{:S(2)}, u32[]{:S(2)}) collective-permute-start(f32[64,384]{0,1:T(8,128)S(1)} %constant_dynamic-slice_fusion.5), channel_id=1, source_target_pairs={{0,2},{2,0},{4,6},{6,4},{1,3},{3,1},{5,7},{7,5},{8,10},{10,8},{12,... | collective-permute-start | bytes 294920 | tf_op jit(solution)/shard_map/ppermute | solution.py:15
  117.5 7.7 %collective-permute-start.10 = (f32[64,384]{0,1:T(8,128)S(1)}, f32[64,384]{0,1:T(8,128)S(1)}, u32[]{:S(2)}, u32[]{:S(2)}) collective-permute-start(f32[64,384]{0,1:T(8,128)S(1)} %constant_dynamic-slice_fusion.9), channel_id=1, source_target_pairs={{0,1},{1,0},{2,3},{3,2},{4,5},{5,4},{6,7},{7,6},{8,9},{9,8},{10,11... | collective-permute-start | bytes 294920 | tf_op jit(solution)/shard_map/ppermute | solution.py:15
  120.3 7.1 %collective-permute-start.27 = (f32[32,384]{0,1:T(8,128)S(1)}, f32[32,384]{0,1:T(8,128)S(1)}, u32[]{:S(2)}, u32[]{:S(2)}) collective-permute-start(f32[32,384]{0,1:T(8,128)S(1)} %constant_dynamic-slice_fusion), channel_id=1, source_target_pairs={{0,1},{1,0},{2,3},{3,2},{4,5},{5,4},{6,7},{7,6},{8,9},{9,8},{10,11... | collective-permute-start | bytes 147464 | tf_op jit(solution)/shard_map/ppermute | solution.py:15
  125.3 5.7 %collective-permute-start.19 = (f32[32,384]{0,1:T(8,128)S(1)}, f32[32,384]{0,1:T(8,128)S(1)}, u32[]{:S(2)}, u32[]{:S(2)}) collective-permute-start(f32[32,384]{0,1:T(8,128)S(1)} %constant_dynamic-slice_fusion.4), channel_id=1, source_target_pairs={{0,16},{8,24},{16,0},{24,8},{1,17},{9,25},{17,1},{25,9},{2,18},{10... | collective-permute-start | bytes 147464 | tf_op jit(solution)/shard_map/ppermute | solution.py:15
  127.4 7.7 %collective-permute-start.11 = (f32[32,384]{0,1:T(8,128)S(1)}, f32[32,384]{0,1:T(8,128)S(1)}, u32[]{:S(2)}, u32[]{:S(2)}) collective-permute-start(f32[32,384]{0,1:T(8,128)S(1)} %constant_dynamic-slice_fusion.8), channel_id=1, source_target_pairs={{0,2},{2,0},{4,6},{6,4},{1,3},{3,1},{5,7},{7,5},{8,10},{10,8},{12,... | collective-permute-start | bytes 147464 | tf_op jit(solution)/shard_map/ppermute | solution.py:15
  130.9 17.2 %collective-permute-start.28 = (f32[16,384]{0,1:T(8,128)S(1)}, f32[16,384]{0,1:T(8,128)S(1)}, u32[]{:S(2)}, u32[]{:S(2)}) collective-permute-start(f32[16,384]{0,1:T(8,128)S(1)} %constant_dynamic-slice_fusion.12), channel_id=1, source_target_pairs={{0,4},{2,6},{4,0},{6,2},{1,5},{3,7},{5,1},{7,3},{8,12},{10,14},{12... | collective-permute-start | bytes 73736 | tf_op jit(solution)/shard_map/ppermute | solution.py:15
  135.1 21.4 %collective-permute-start.20 = (f32[16,384]{0,1:T(8,128)S(1)}, f32[16,384]{0,1:T(8,128)S(1)}, u32[]{:S(2)}, u32[]{:S(2)}) collective-permute-start(f32[16,384]{0,1:T(8,128)S(1)} %constant_dynamic-slice_fusion.3), channel_id=1, source_target_pairs={{0,4},{2,6},{4,0},{6,2},{1,5},{3,7},{5,1},{7,3},{8,12},{10,14},{12... | collective-permute-start | bytes 73736 | tf_op jit(solution)/shard_map/ppermute | solution.py:15
  148.1 12.6 %collective-permute-start.12 = (f32[16,384]{0,1:T(8,128)S(1)}, f32[16,384]{0,1:T(8,128)S(1)}, u32[]{:S(2)}, u32[]{:S(2)}) collective-permute-start(f32[16,384]{0,1:T(8,128)S(1)} %constant_dynamic-slice_fusion.7), channel_id=1, source_target_pairs={{0,4},{2,6},{4,0},{6,2},{1,5},{3,7},{5,1},{7,3},{8,12},{10,14},{12... | collective-permute-start | bytes 73736 | tf_op jit(solution)/shard_map/ppermute | solution.py:15
  156.5 13.0 %collective-permute-start.29 = (f32[16,384]{0,1:T(8,128)S(1)}, f32[16,384]{0,1:T(8,128)S(1)}, u32[]{:S(2)}, u32[]{:S(2)}) collective-permute-start(f32[16,384]{0,1:T(8,128)S(1)} %dynamic-slice_add_fusion.1), channel_id=1, source_target_pairs={{0,4},{2,6},{4,0},{6,2},{1,5},{3,7},{5,1},{7,3},{8,12},{10,14},{12... | collective-permute-start | bytes 73736 | tf_op jit(solution)/shard_map/ppermute | solution.py:15
  160.7 11.6 %collective-permute-start.21 = (f32[16,384]{0,1:T(8,128)S(1)}, f32[16,384]{0,1:T(8,128)S(1)}, u32[]{:S(2)}, u32[]{:S(2)}) collective-permute-start(f32[16,384]{0,1:T(8,128)S(1)} %dynamic-slice_add_fusion.5), channel_id=1, source_target_pairs={{0,4},{2,6},{4,0},{6,2},{1,5},{3,7},{5,1},{7,3},{8,12},{10,14},{12... | collective-permute-start | bytes 73736 | tf_op jit(solution)/shard_map/ppermute | solution.py:15
  169.5 9.5 %collective-permute-start.13 = (f32[16,384]{0,1:T(8,128)S(1)}, f32[16,384]{0,1:T(8,128)S(1)}, u32[]{:S(2)}, u32[]{:S(2)}) collective-permute-start(f32[16,384]{0,1:T(8,128)S(1)} %dynamic-slice_add_fusion.9), channel_id=1, source_target_pairs={{0,4},{2,6},{4,0},{6,2},{1,5},{3,7},{5,1},{7,3},{8,12},{10,14},{12... | collective-permute-start | bytes 73736 | tf_op jit(solution)/shard_map/ppermute | solution.py:15
  172.4 8.3 %collective-permute-start.30 = (f32[32,384]{1,0:T(8,128)S(1)}, f32[32,384]{1,0:T(8,128)S(1)}, u32[]{:S(2)}, u32[]{:S(2)}) collective-permute-start(f32[32,384]{1,0:T(8,128)S(1)} %pad_maximum_fusion.9), channel_id=1, source_target_pairs={{0,1},{1,0},{2,3},{3,2},{4,5},{5,4},{6,7},{7,6},{8,9},{9,8},{10,11... | collective-permute-start | bytes 147464 | tf_op jit(solution)/shard_map/ppermute | solution.py:15
  178.9 5.1 %collective-permute-start.22 = (f32[32,384]{1,0:T(8,128)S(1)}, f32[32,384]{1,0:T(8,128)S(1)}, u32[]{:S(2)}, u32[]{:S(2)}) collective-permute-start(f32[32,384]{1,0:T(8,128)S(1)} %pad_maximum_fusion.8), channel_id=1, source_target_pairs={{0,16},{8,24},{16,0},{24,8},{1,17},{9,25},{17,1},{25,9},{2,18},{10... | collective-permute-start | bytes 147464 | tf_op jit(solution)/shard_map/ppermute | solution.py:15
  180.7 5.7 %collective-permute-start.14 = (f32[32,384]{1,0:T(8,128)S(1)}, f32[32,384]{1,0:T(8,128)S(1)}, u32[]{:S(2)}, u32[]{:S(2)}) collective-permute-start(f32[32,384]{1,0:T(8,128)S(1)} %pad_maximum_fusion.7), channel_id=1, source_target_pairs={{0,2},{2,0},{4,6},{6,4},{1,3},{3,1},{5,7},{7,5},{8,10},{10,8},{12,... | collective-permute-start | bytes 147464 | tf_op jit(solution)/shard_map/ppermute | solution.py:15
  184.0 4.7 %collective-permute-start.31 = (f32[64,384]{1,0:T(8,128)S(1)}, f32[64,384]{1,0:T(8,128)S(1)}, u32[]{:S(2)}, u32[]{:S(2)}) collective-permute-start(f32[64,384]{1,0:T(8,128)S(1)} %pad_maximum_fusion.6), channel_id=1, source_target_pairs={{0,16},{8,24},{16,0},{24,8},{1,17},{9,25},{17,1},{25,9},{2,18},{10... | collective-permute-start | bytes 294920 | tf_op jit(solution)/shard_map/ppermute | solution.py:15
  186.4 5.7 %collective-permute-start.23 = (f32[64,384]{1,0:T(8,128)S(1)}, f32[64,384]{1,0:T(8,128)S(1)}, u32[]{:S(2)}, u32[]{:S(2)}) collective-permute-start(f32[64,384]{1,0:T(8,128)S(1)} %pad_maximum_fusion.5), channel_id=1, source_target_pairs={{0,2},{2,0},{4,6},{6,4},{1,3},{3,1},{5,7},{7,5},{8,10},{10,8},{12,... | collective-permute-start | bytes 294920 | tf_op jit(solution)/shard_map/ppermute | solution.py:15
  188.7 5.1 %collective-permute-start.15 = (f32[64,384]{1,0:T(8,128)S(1)}, f32[64,384]{1,0:T(8,128)S(1)}, u32[]{:S(2)}, u32[]{:S(2)}) collective-permute-start(f32[64,384]{1,0:T(8,128)S(1)} %pad_maximum_fusion.4), channel_id=1, source_target_pairs={{0,1},{1,0},{2,3},{3,2},{4,5},{5,4},{6,7},{7,6},{8,9},{9,8},{10,11... | collective-permute-start | bytes 294920 | tf_op jit(solution)/shard_map/ppermute | solution.py:15
  192.0 5.7 %collective-permute-start.32 = (f32[128,384]{1,0:T(8,128)S(1)}, f32[128,384]{1,0:T(8,128)S(1)}, u32[]{:S(2)}, u32[]{:S(2)}) collective-permute-start(f32[128,384]{1,0:T(8,128)S(1)} %pad_maximum_fusion.3), channel_id=1, source_target_pairs={{0,2},{2,0},{4,6},{6,4},{1,3},{3,1},{5,7},{7,5},{8,10},{10,8},{12,... | collective-permute-start | bytes 589832 | tf_op jit(solution)/shard_map/ppermute | solution.py:15
  193.8 5.7 %collective-permute-start.24 = (f32[128,384]{1,0:T(8,128)S(1)}, f32[128,384]{1,0:T(8,128)S(1)}, u32[]{:S(2)}, u32[]{:S(2)}) collective-permute-start(f32[128,384]{1,0:T(8,128)S(1)} %pad_maximum_fusion.2), channel_id=1, source_target_pairs={{0,1},{1,0},{2,3},{3,2},{4,5},{5,4},{6,7},{7,6},{8,9},{9,8},{10,11... | collective-permute-start | bytes 589832 | tf_op jit(solution)/shard_map/ppermute | solution.py:15
  197.7 5.7 %collective-permute-start.16 = (f32[128,384]{1,0:T(8,128)S(1)}, f32[128,384]{1,0:T(8,128)S(1)}, u32[]{:S(2)}, u32[]{:S(2)}) collective-permute-start(f32[128,384]{1,0:T(8,128)S(1)} %pad_maximum_fusion.1), channel_id=1, source_target_pairs={{0,16},{8,24},{16,0},{24,8},{1,17},{9,25},{17,1},{25,9},{2,18},{10... | collective-permute-start | bytes 589832 | tf_op jit(solution)/shard_map/ppermute | solution.py:15
  199.5 5.0 %copy-start.4 = (f32[128,384]{1,0:T(8,128)}, f32[128,384]{1,0:T(8,128)S(1)}, u32[]{:S(2)}) copy-start(f32[128,384]{1,0:T(8,128)S(1)} %get-tuple-element.36) | copy-start | bytes 589828
  199.5 5.0 %copy-start.5 = (f32[128,384]{1,0:T(8,128)}, f32[128,384]{1,0:T(8,128)S(1)}, u32[]{:S(2)}) copy-start(f32[128,384]{1,0:T(8,128)S(1)} %get-tuple-element.37) | copy-start | bytes 589828
  203.4 1.1 copy-start.6
  203.4 1.1 copy-start.7
  204.6 10.4 %collective-permute-start.33 = (f32[256,1152]{1,0:T(8,128)}, f32[256,1152]{1,0:T(8,128)}, u32[]{:S(2)}, u32[]{:S(2)}) collective-permute-start(f32[256,1152]{1,0:T(8,128)} %maximum_maximum_fusion.1), channel_id=1, source_target_pairs={{0,8},{8,0},{16,24},{24,16},{1,9},{9,1},{17,25},{25,17},{2,10},{10... | collective-permute-start | bytes 3538952 | tf_op jit(solution)/shard_map/ppermute | solution.py:15
  216.7 0.7 copy-start.10
  216.7 0.7 copy-start.9
  246.7 45.9 %copy-start.3 = (bf16[8,1024,256]{1,2,0:T(8,128)(2,1)S(1)}, bf16[8,1024,256]{1,2,0:T(8,128)(2,1)}, u32[]{:S(2)}) copy-start(bf16[8,1024,256]{1,2,0:T(8,128)(2,1)} %constant_dynamic-update-slice_fusion.1) | copy-start | bytes 12582916

commit v3 on v0

v3 whole, which is shorter than its diff:
```python
import functools
import math

import jax
import jax.numpy as jnp
from jax import lax
from jax.experimental import pallas as pl
from jax.experimental.pallas import tpu as pltpu
from jax.sharding import PartitionSpec as P

BLOCK = 128


def swap(array, step):
    axis, size, distance = step
    return lax.ppermute(array, axis, [(i, i ^ distance) for i in range(size)])


def steps_of(axis, size):
    return [(axis, size, 1 << i) for i in range(size.bit_length() - 1)]


def gather_slots(held, steps):
    for step in steps:
        held = held + [(slot ^ step[2], swap(piece, step)) for slot, piece in held]
    return held


def cut_steps(steps, rows):
    count = 0
    while count < len(steps) and rows % 16 == 0:
        rows, count = rows // 2, count + 1
    return count


def position(steps):
    place = jnp.int32(0)
    for axis, _, distance in steps:
        place = place * 2 + lax.rem(lax.div(lax.axis_index(axis), distance), 2)
    return place


def reduce_parts(parts, orders, cuts):
    for at in range(max(map(len, orders))):
        moving = [(i, orders[i][at]) for i in range(len(parts)) if at < len(orders[i])]
        kept, got = {}, {}
        for i, step in moving:
            half = parts[i].shape[0] // 2
            kept[i], sent = (parts[i][:half], parts[i][half:]) if at < cuts[i] else (parts[i], parts[i])
            got[i] = swap(sent, step)
        parts = [kept[i] + got[i] if i in got else part for i, part in enumerate(parts)]
    return parts


def gather_parts(parts, orders, cuts):
    for at in range(max(cuts) - 1, -1, -1):
        got = {i: swap(parts[i], orders[i][at]) for i in range(len(parts)) if at < cuts[i]}
        parts = [jnp.concatenate([part, got[i]], 0) if i in got else part for i, part in enumerate(parts)]
    return parts


HIGHEST = lax.Precision.HIGHEST
GROUP = 16
PIECES = 2


def dot(a, b, transposed=False):
    dims = (((1,), (1 if transposed else 0,)), ((), ()))
    return lax.dot_general(a, b, dims, preferred_element_type=jnp.float32)


def absorb_kernel(east_parts, legs_ref, site_ref, double_ref, *out_refs):
    phys = double_ref.shape[0]
    legs = sum(east_parts)
    row = lax.broadcasted_iota(jnp.int32, (legs * GROUP, GROUP * phys), 0)
    column = lax.broadcasted_iota(jnp.int32, (legs * GROUP, GROUP * phys), 1)
    chosen = jnp.concatenate(
        [
            jnp.where(lax.broadcasted_iota(jnp.int32, (GROUP, phys), 1) == legs_ref[i], 1.0, 0.0)
            for i in range(legs)
        ],
        0,
    )
    values = lax.dot_general(
        chosen, double_ref[...], (((1,), (1,)), ((), ())), precision=HIGHEST, preferred_element_type=jnp.float32
    )
    spread = jnp.where(
        lax.broadcasted_iota(jnp.int32, (phys, GROUP * phys), 0)
        == lax.rem(lax.broadcasted_iota(jnp.int32, (phys, GROUP * phys), 1), phys),
        1.0,
        0.0,
    )
    values = jnp.dot(values, spread, precision=HIGHEST, preferred_element_type=jnp.float32)
    high, low = split(jnp.where(lax.rem(row, GROUP) == lax.div(column, phys), values, 0.0), 2)
    groups = site_ref.shape[0] // (GROUP * phys)
    for g in range(groups):
        rows = site_ref[g * GROUP * phys : (g + 1) * GROUP * phys, :]
        absorbed = (dot(high, rows) + dot(low, rows)).astype(jnp.bfloat16)
        leg = 0
        for out_ref, count in zip(out_refs, east_parts):
            for e in range(count):
                piece = absorbed[(leg + e) * GROUP : (leg + e + 1) * GROUP]
                out_ref[e, g * GROUP : (g + 1) * GROUP, :] = piece.astype(out_ref.dtype)
            leg += count


def absorb(boundary_site, double_layer, legs, east_parts):
    depth, phys, right = boundary_site.shape
    tiles = max(1, depth // 128)
    tile = depth // tiles
    out_shape, out_specs = [], []
    for i, count in enumerate(east_parts):
        out_shape.append(jax.ShapeDtypeStruct((count, depth, right), jnp.bfloat16 if i == 0 else jnp.float32))
        out_specs.append(pl.BlockSpec((count, tile, right), lambda t: (0, t, 0)))
    return pl.pallas_call(
        functools.partial(absorb_kernel, east_parts),
        grid=(tiles,),
        out_shape=out_shape,
        in_specs=[
            pl.BlockSpec(memory_space=pltpu.SMEM),
            pl.BlockSpec((tile * phys, right), lambda t: (t, 0)),
            pl.BlockSpec(memory_space=pltpu.VMEM),
        ],
        out_specs=out_specs,
        compiler_params=pltpu.CompilerParams(vmem_limit_bytes=32 * 2**20),
        cost_estimate=pl.CostEstimate(
            flops=2 * 2 * depth * right * GROUP * phys * sum(east_parts), bytes_accessed=8 * depth * right * phys, transcendentals=0
        ),
    )(legs, boundary_site.reshape(depth * phys, right), double_layer)


def moment_kernel(chi, chunk, third, place_ref, *refs):
    *block_refs, kept_ref, sent_ref, columns, packed = refs
    rep = len(block_refs)
    count, depth, width = block_refs[0].shape
    n = chi // BLOCK
    for i, block_ref in enumerate(block_refs):
        at = pl.ds(pl.multiple_of((place_ref[0] ^ i) * depth, depth), depth)
        for e in range(count):
            columns[at, e * width : (e + 1) * width] = block_ref[e].astype(jnp.bfloat16)
    for i in range(n):
        group, lo = (i, 0) if i < n // 2 else (n - 1 - i, (n - i) * BLOCK)
        packed[group * BLOCK : (group + 1) * BLOCK, lo : lo + (i + 1) * BLOCK] = dot(
            columns[i * BLOCK : (i + 1) * BLOCK], columns[: (i + 1) * BLOCK], True
        )
    half = kept_ref.shape[0]
    for part in range(3):
        lanes = slice(part * third, (part + 1) * third)
        for t in range(packed.shape[0] // chunk):
            rows = pl.ds(pl.multiple_of((place_ref[1 + part] ^ t) * chunk, 8), chunk)
            at = t * chunk
            to_ref = kept_ref if at < half else sent_ref
            to_ref[at % half : at % half + chunk, lanes] = packed[rows, lanes]


def moment(blocks, places, chi, chunk):
    rows, width = chi // 2, chi + BLOCK
    count, _, right = blocks[0].shape
    whole = pl.BlockSpec(memory_space=pltpu.VMEM)
    return pl.pallas_call(
        functools.partial(moment_kernel, chi, chunk, width // 3),
        out_shape=[jax.ShapeDtypeStruct((rows // 2, width), jnp.float32)] * 2,
        in_specs=[pl.BlockSpec(memory_space=pltpu.SMEM)] + [whole] * len(blocks),
        out_specs=[whole, whole],
        scratch_shapes=[pltpu.VMEM((chi, count * right), jnp.bfloat16), pltpu.VMEM((rows, width), jnp.float32)],
        compiler_params=pltpu.CompilerParams(vmem_limit_bytes=32 * 2**20),
        cost_estimate=pl.CostEstimate(flops=chi * chi * count * right, bytes_accessed=6 * chi * chi, transcendentals=0),
    )(places, *blocks)


def sub(x, s):
    return jnp.broadcast_to(x[s : s + 1, :], x.shape)


def lane(x, k):
    return jnp.broadcast_to(x[:, k : k + 1], x.shape)


def inverse_factor(block):
    n, wide = BLOCK // 8, 8
    rows = [block[8 * b : 8 * b + 8] for b in range(n)]
    sub_id = lax.broadcasted_iota(jnp.int32, (8, BLOCK), 0)
    lane_id = lax.broadcasted_iota(jnp.int32, (8, BLOCK), 1)
    pivots = []
    head = [lane(rows[0], c) for c in range(wide)]
    for b in range(n):
        k = wide * b
        cols = [[head[c]] + [lane(rows[i], k + c) for i in range(b + 1, n)] for c in range(wide)]
        if b + 1 < n:
            head = [lane(rows[b + 1], k + wide + c) for c in range(wide)]
        inside = (lane_id >= k) & (lane_id < k + wide)
        for i in range(b, n):
            rows[i] = jnp.where(inside, 0.0, rows[i])
        pivot = jnp.ones((8, BLOCK), jnp.float32)
        for c in range(wide):
            d = sub(cols[c][0], c)
            inverse = 1.0 / d
            pivot = jnp.where(sub_id == c, d, pivot)
            for c2 in range(c + 1, wide):
                m = sub(cols[c][0], c2) * inverse
                for i in range(n - b):
                    cols[c2][i] = cols[c2][i] - cols[c][i] * m
            factors = [cols[c][i] * inverse for i in range(n - b)]
            if b + 1 < n:
                for c2 in range(wide):
                    head[c2] = head[c2] - factors[1] * sub(cols[c][1], c2)
            factors[0] = jnp.where(sub_id > c, factors[0], 0.0)
            row = jnp.where(lane_id == k + c, 1.0, sub(rows[b], c))
            for i in range(n - b):
                rows[b + i] = rows[b + i] - factors[i] * row
        pivots.append(pivot)
    out = []
    for b in range(n):
        diagonal = sub_id + 8 * b
        row = jnp.where(lane_id < diagonal, rows[b], jnp.where(lane_id == diagonal, 1.0, 0.0))
        out.append(row * lax.rsqrt(pivots[b]))
    return jnp.concatenate(out, 0)


def split(x, pieces):
    out = []
    for i in range(pieces):
        out.append(x.astype(jnp.bfloat16))
        if i + 1 < pieces:
            x = x - out[-1].astype(jnp.float32)
    return out


def product(a, b):
    terms = [
        jnp.dot(a[i], b[j], preferred_element_type=jnp.float32)
        for i in range(len(a))
        for j in range(len(b))
        if i + j < max(len(a), len(b))
    ]
    return sum(terms[1:], terms[0])


def factor_kernel(scale, chunk, place_ref, mine_ref, other_ref, *refs):
    *left_refs, factor_ref, weights_ref, left, packed, moments, now, solved, lows, low = refs
    chi = left.shape[0]
    n = chi // BLOCK
    rows, width = left_refs[0].shape
    across = chi // width
    for i, left_ref in enumerate(left_refs):
        row_at = pl.multiple_of((place_ref[0] ^ (i // across)) * rows, 16)
        column_at = pl.multiple_of((place_ref[1] ^ (i % across)) * width, 128)
        left[pl.ds(row_at, rows), pl.ds(column_at, width)] = left_ref[...].astype(jnp.bfloat16)
    half, third = mine_ref.shape[0], mine_ref.shape[1] // 3
    for part in range(3):
        lanes = slice(part * third, (part + 1) * third)
        for t in range(2 * half // chunk):
            at = pl.ds(pl.multiple_of((place_ref[2 + part] ^ t) * chunk, 8), chunk)
            from_ref = mine_ref if t * chunk < half else other_ref
            packed[at, lanes] = from_ref[t * chunk % half : t * chunk % half + chunk, lanes]
    for i in range(n):
        group, lo = (i, 0) if i < n // 2 else (n - 1 - i, (n - i) * BLOCK)
        for k in range(i + 1):
            block = packed[group * BLOCK : (group + 1) * BLOCK, lo + k * BLOCK : lo + (k + 1) * BLOCK]
            for piece, value in enumerate(split(block, PIECES)):
                moments[piece, i * BLOCK : (i + 1) * BLOCK, k * BLOCK : (k + 1) * BLOCK] = value
            if k < i:
                for piece, value in enumerate(split(block.T, PIECES)):
                    moments[piece, k * BLOCK : (k + 1) * BLOCK, i * BLOCK : (i + 1) * BLOCK] = value
    solved[...] = jnp.zeros_like(solved)
    lows[...] = jnp.zeros_like(lows)

    def gram_row(at):
        held = left[at, :]
        row = sum(dot(held, moments[i]) for i in range(PIECES))
        return sum(dot(piece, left[...], True) for piece in split(row, PIECES))

    now[:, :chi] = gram_row(pl.ds(0, BLOCK))
    now[:, chi:] = left[:BLOCK, :].astype(jnp.float32)

    def body(j, _):
        here = pl.ds(pl.multiple_of(j * BLOCK, BLOCK), BLOCK)
        after = pl.ds(pl.multiple_of(jnp.minimum(j + 1, n - 1) * BLOCK, BLOCK), BLOCK)
        inverse = split(inverse_factor(now[:, here]), PIECES)
        multiples = [lows[i, after, :] for i in range(PIECES)]
        next_gram = gram_row(after) - product(multiples, [solved[i, :, :chi] for i in range(PIECES)])
        next_left = left[after, :].astype(jnp.float32) - product(
            multiples, [solved[i, :, chi:] for i in range(PIECES)]
        )
        row = now[...]
        row_gram = product(inverse, split(row[:, :chi], PIECES))
        row_left = product(inverse, split(row[:, chi:], PIECES))
        row_gram_pieces, row_left_pieces = split(row_gram, PIECES), split(row_left, PIECES)
        for i in range(PIECES):
            solved[i, here, :chi] = row_gram_pieces[i]
            solved[i, here, chi:] = row_left_pieces[i]
        low[:, here] = row_gram.T
        for i, piece in enumerate(split(low[:, here], PIECES)):
            lows[i, :, here] = piece
        multiples = [lows[i, after, here] for i in range(PIECES)]
        now[:, :chi] = next_gram - product(multiples, row_gram_pieces)
        now[:, chi:] = next_left - product(multiples, row_left_pieces)
        return 0

    lax.fori_loop(0, n, body, 0)
    count = factor_ref.shape[0]
    first = place_ref[0] * count
    mine = pl.ds(pl.multiple_of(first, 16), count)
    row_id = lax.broadcasted_iota(jnp.int32, (count, chi), 0) + first
    column_id = lax.broadcasted_iota(jnp.int32, (count, chi), 1)
    factor_ref[...] = jnp.where(column_id <= row_id, low[mine, :] * (1.0 / scale), 0.0)
    weights_ref[...] = solved[0, mine, chi:]


def factorize(mine, other, left_blocks, places, chi, chunk, scale):
    rows = left_blocks[0].shape[0]
    whole = pl.BlockSpec(memory_space=pltpu.VMEM)
    return pl.pallas_call(
        functools.partial(factor_kernel, scale, chunk),
        out_shape=[
            jax.ShapeDtypeStruct((rows, chi), jnp.float32),
            jax.ShapeDtypeStruct((rows, chi), jnp.bfloat16),
        ],
        in_specs=[pl.BlockSpec(memory_space=pltpu.SMEM)] + [whole] * (2 + len(left_blocks)),
        out_specs=[whole, whole],
        scratch_shapes=[
            pltpu.VMEM((chi, chi), jnp.bfloat16),
            pltpu.VMEM((chi // 2, chi + BLOCK), jnp.float32),
            pltpu.VMEM((PIECES, chi, chi), jnp.bfloat16),
            pltpu.VMEM((BLOCK, 2 * chi), jnp.float32),
            pltpu.VMEM((PIECES, chi, 2 * chi), jnp.bfloat16),
            pltpu.VMEM((PIECES, chi, chi), jnp.bfloat16),
            pltpu.VMEM((chi, chi), jnp.float32),
        ],
        compiler_params=pltpu.CompilerParams(vmem_limit_bytes=52 * 2**20),
        cost_estimate=pl.CostEstimate(flops=20 * 2 * chi**3, bytes_accessed=16 * chi**2, transcendentals=0),
    )(places, mine, other, *left_blocks)


def site_kernel(scale, place_ref, weights_ref, own_ref, *refs):
    *got_refs, out_ref = refs
    depth = own_ref.shape[1]
    mine = weights_ref[:, pl.ds(pl.multiple_of(place_ref[1] * depth, depth), depth)]
    other = weights_ref[:, pl.ds(pl.multiple_of((place_ref[1] ^ 1) * depth, depth), depth)]
    for slot, got_ref in enumerate(got_refs):
        count = got_ref.shape[0]
        for i in range(count):
            e = (place_ref[0] ^ slot) * count + i
            out_ref[e] = scale * (dot(mine, own_ref[e]) + dot(other, got_ref[i].astype(jnp.bfloat16)))


def make_site(weights, own, got, places, scale):
    rows, chi = weights.shape
    east, _, right = own.shape
    whole = pl.BlockSpec(memory_space=pltpu.VMEM)
    return pl.pallas_call(
        functools.partial(site_kernel, scale),
        out_shape=jax.ShapeDtypeStruct((east, rows, right), jnp.float32),
        in_specs=[pl.BlockSpec(memory_space=pltpu.SMEM)] + [whole] * (2 + len(got)),
        out_specs=whole,
        compiler_params=pltpu.CompilerParams(vmem_limit_bytes=32 * 2**20),
        cost_estimate=pl.CostEstimate(flops=2 * rows * chi * east * right, bytes_accessed=8 * east * chi * right, transcendentals=0),
    )(places, weights, own, *got)


def shards(sizes, left_factor, boundary_site, double_layer):
    lb, rb, rep = sizes["lb"], sizes["rb"], sizes["rep"]
    l, p = lax.axis_index("lb"), lax.axis_index("rep")
    depth, phys, right = boundary_site.shape
    east = phys // rep
    chi = depth * rep
    scale = math.sqrt(phys * rb * right)
    steps = {axis: steps_of(axis, size) for axis, size in sizes.items()}
    core, across = steps["lb"][:1], steps["lb"][1:]

    left_blocks = gather_slots([(0, left_factor.astype(jnp.float32))], steps["rep"])
    left_blocks = [piece for _, piece in sorted(left_blocks, key=lambda pair: pair[0])]
    left_blocks = [gather_slots([(0, piece)], across[::-1] + core) for piece in left_blocks]
    left_blocks = [sorted(pieces, key=lambda pair: pair[0]) for pieces in left_blocks]
    left_blocks = [left_blocks[q][s][1] for s in range(lb) for q in range(rep)]

    east_part, right_parts = max(1, east // lb), max(1, lb // east)
    right_part = right // right_parts
    east_at, right_at = (l // right_parts) * east_part, (l % right_parts) * right_part
    legs = [p * east + i for i in range(east)]
    for s in range(1, rep):
        legs += [(p ^ s) * east + east_at + i for i in range(east_part)]
    legs = jnp.stack(legs).astype(jnp.int32)
    own, *sent = absorb(boundary_site, double_layer, legs, [east] + [east_part] * (rep - 1))
    if right_parts > 1:
        sent = [lax.dynamic_slice_in_dim(piece, right_at, right_part, 2) for piece in sent]
    got = [swap(piece, ("rep", rep, s)) for s, piece in zip(range(1, rep), sent)]
    share = lax.dynamic_slice(own, (east_at, 0, right_at), (east_part, depth, right_part))

    near = across[:1] + steps["rep"][:1] + steps["rb"][:1]
    far = [step for step in across + steps["rep"] + steps["rb"] if step not in near]
    orders = [near[i:] + near[:i] + far for i in range(3)]
    cut = cut_steps(orders[0], chi // 4)
    chunk = (chi // 4) >> cut
    bits = [position(core + order[:cut]) for order in orders]
    places = jnp.stack([p] + bits).astype(jnp.int32)
    kept, sent = moment([share] + got, places, chi, chunk)
    whole = kept + swap(sent, core[0])
    third = whole.shape[1] // 3
    parts = [whole[:, i * third : (i + 1) * third] for i in range(3)]
    parts = reduce_parts(parts, orders, [cut] * 3)
    parts = gather_parts(parts, orders, [cut] * 3)
    whole = jnp.concatenate(parts, 1)
    other = swap(whole, core[0])

    got = [gather_slots([(0, piece)], core) for piece in got]
    held, whole = lax.optimization_barrier(([[piece for _, piece in pieces] for pieces in got], whole))
    got = [gather_slots(list(zip(range(2), pieces)), across[::-1]) for pieces in held]

    places = jnp.stack([l, p] + bits).astype(jnp.int32)
    factor, weights = factorize(whole, other, left_blocks, places, chi, chunk, scale)
    if rep == 2 and right_parts == 1:
        pieces = [piece for _, piece in sorted(got[0], key=lambda pair: pair[0])]
        site_q = make_site(weights, own, pieces, places, scale)
    else:
        nothing = double_layer[0, 0] * 0.0
        site = jnp.zeros((east, chi, right), jnp.bfloat16)
        site = lax.dynamic_update_slice(site, own, (0, p * depth, 0))
        for s, pieces in zip(range(1, rep), got):
            for slot, piece in pieces:
                owner = l ^ slot
                at = ((owner // right_parts) * east_part, (p ^ s) * depth, (owner % right_parts) * right_part)
                site = lax.dynamic_update_slice(site, (piece + nothing).astype(jnp.bfloat16), at)
        site_q = jnp.einsum("ik,ekr->eir", weights, site, preferred_element_type=jnp.float32) * scale
    return (site_q, factor)


def solution(mesh):
    return jax.shard_map(
        functools.partial(shards, dict(mesh.shape)),
        mesh=mesh,
        in_specs=(P("lb", "rep"), P("rep", None, "rb"), P()),
        out_specs=(P("rep", "lb", "rb"), P("lb", None)),
        check_vma=False,
    )
```

time: 698 us -> 205 us (0.29); the launches traced: 689 us -> 205 us
  other arithmetic: 266 us -> 2.43 us
  waiting for transfers between devices: 225 us -> 84.9 us
  matrix products: 122 us -> 0 us
  Pallas kernels: 0 us -> 66.7 us
  local copies, waits for them, and re-layouts: 55.9 us -> 4.24 us
  starting transfers between devices: 0.16 us -> 45.4 us
  between operations: 19.6 us -> 0.91 us
    another operation x33 -> x1, other arithmetic: 259 us -> 0.08 us  [shards(): places = jnp.stack([p] + bits).astype(jnp.int32)]
    another operation x29 -> x0, matrix products: 92.7 us -> none  [the longest x15 66.7 us: shards(): solved = jax.scipy.linalg.solve_triangular(lower, matrix, lower=True)]
    all_gather x2 -> x0, waiting for transfers between devices: 89.4 us -> none  [the longest x1 59.9 us: shards(): grown_all = lax.all_gather(grown_part, 'lb', axis=1, tiled=True)]
    ppermute x0 -> x37, waiting for transfers between devices: none -> 84.9 us  [swap(): return lax.ppermute(array, axis, [(i, i ^ distance) for i in range(size)])]
    psum x1 -> x0, waiting for transfers between devices: 78.2 us -> none  [shards(): gram_block = lax.psum(gram_part, ('rb', 'rep'))]
    pallas_call x0 -> x4, Pallas kernels: none -> 66.7 us  [the longest x1 55.3 us: factorize(): pl.pallas_call(functools.partial(factor_kernel, scale, chunk), out_shape=...]
    reduce_scatter x1 -> x0, waiting for transfers between devices: 57.1 us -> none  [shards(): lax.psum_scatter(jnp.einsum('ik,ker->eir', left_factor, absorbed, preferr...]
    ppermute x0 -> x37, starting transfers between devices: none -> 45.4 us  [swap(): return lax.ppermute(array, axis, [(i, i ^ distance) for i in range(size)])]
  transfers between devices with their start and end apart: 4 -> 37, of which waited for: 4 -> 22; matrix products, arithmetic and copies ran while one was open for 1% -> 1% of each run, Pallas kernels for 0% -> 27%
where the time goes in v3:
time: 205 us
  waiting for transfers between devices  84.9 us (41%)
  Pallas kernels  66.7 us (33%)
  starting transfers between devices  45.4 us (22%)
  local copies, waits for them, and re-layouts  4.24 us (2%)
  other arithmetic  2.43 us (1%)
    ppermute x37, waiting for transfers between devices, swap(): return lax.ppermute(array, axis, [(i, i ^ distance) for i in range(size)])  84.9 us
    pallas_call x1, Pallas kernels, factorize(): pl.pallas_call(functools.partial(factor_kernel, scale, chunk), out_shape=...  55.3 us
    ppermute x37, starting transfers between devices, swap(): return lax.ppermute(array, axis, [(i, i ^ distance) for i in range(size)])  45.4 us
    pallas_call x1, Pallas kernels, absorb(): pl.pallas_call(functools.partial(absorb_kernel, east_parts), grid=(tiles,...  5.82 us
  transfers between devices with their start and end apart: 37, of which 22 were waited for; matrix products, arithmetic and copies ran while one was open for 1% of the time, Pallas kernels for 27%

profile of v3, /device:TPU:0, one launch (start us, length us, event | category | flops | bytes accessed | tf_op | source)
XLA Modules:
  0.0 204.6 jit_solution(18392999620875391468)
XLA Ops:
  0.7 2.2 %copy-done.2 = bf16[512,16,256]{2,1,0:T(8,128)(2,1)S(1)} copy-done((bf16[512,16,256]{2,1,0:T(8,128)(2,1)S(1)}, bf16[512,16,256]{2,1,0:T(8,128)(2,1)}, u32[]{:S(2)}) %copy-start.2) | copy-done | bytes 4194328
  2.9 0.7 copy-done.3
  3.6 5.8 %shard_map.50 = (bf16[8,512,256]{2,1,0:T(8,128)(2,1)S(1)}, f32[2,512,256]{2,1,0:T(8,128)}) custom-call(s32[10]{0:T(128)S(1)} %stack.74.legs_ref, bf16[8192,256]{1,0:T(8,128)(2,1)S(1)} %bitcast.16, f32[16,16]{1,0:T(8,128)S(1)} %copy-done.3), custom_call_target="tpu_custom_call" | custom-call | flops 1342177280 | bytes 16777216 | tf_op jit(solution)/shard_map/pallas_call | solution.py:115
  9.4 3.0 %collective-permute-start = (f32[2,512,256]{2,1,0:T(8,128)}, f32[2,512,256]{2,1,0:T(8,128)S(1)}, u32[]{:S(2)}, u32[]{:S(2)}) collective-permute-start(f32[2,512,256]{2,1,0:T(8,128)} %get-tuple-element.11), channel_id=1, source_target_pairs={{0,1},{1,0},{2,3},{3,2},{4,5},{5,4},{6,7},{7,6},{8,9},{9,8},{10,11... | collective-permute-start | bytes 3145736 | tf_op jit(solution)/shard_map/ppermute | solution.py:16
  12.5 23.3 %collective-permute-done.refs_1_.refs_0_ = f32[2,512,256]{2,1,0:T(8,128)S(1)} collective-permute-done((f32[2,512,256]{2,1,0:T(8,128)}, f32[2,512,256]{2,1,0:T(8,128)S(1)}, u32[]{:S(2)}, u32[]{:S(2)}) %collective-permute-start) | collective-permute-done | bytes 1048608 | tf_op jit(solution)/shard_map/ppermute | solution.py:16
  35.8 2.4 %shard_map.51 = (f32[256,1152]{1,0:T(8,128)S(1)}, f32[256,1152]{1,0:T(8,128)S(1)}) custom-call(s32[4]{0:T(128)S(1)} %pad_add_fusion.place_ref, bf16[2,512,256]{2,1,0:T(8,128)(2,1)S(1)} %constant_dynamic-slice_fusion.refs_0_, f32[2,512,256]{2,1,0:T(8,128)S(1)} %collective-permute-done.refs_1_.refs_0_), custom_call_target="tpu_custom_call" | custom-call | flops 536870912 | bytes 6291456 | tf_op jit(solution)/shard_map/pallas_call | solution.py:160
  38.2 2.8 %collective-permute-done.2 = f32[256,1152]{1,0:T(8,128)S(1)} collective-permute-done((f32[256,1152]{1,0:T(8,128)S(1)}, f32[256,1152]{1,0:T(8,128)S(1)}, u32[]{:S(2)}, u32[]{:S(2)}) %collective-permute-start.2) | collective-permute-done | bytes 1179680 | tf_op jit(solution)/shard_map/ppermute | solution.py:16
  41.2 1.8 collective-permute-start.3
  43.0 5.2 %collective-permute-done.3 = f32[128,384]{1,0:T(8,128)S(1)} collective-permute-done((f32[128,384]{1,0:T(8,128)S(1)}, f32[128,384]{1,0:T(8,128)S(1)}, u32[]{:S(2)}, u32[]{:S(2)}) %collective-permute-start.3) | collective-permute-done | bytes 196640 | tf_op jit(solution)/shard_map/ppermute | solution.py:16
  48.3 1.8 collective-permute-start.4
  50.1 2.9 %collective-permute-done.4 = f32[64,384]{1,0:T(8,128)S(1)} collective-permute-done((f32[64,384]{1,0:T(8,128)S(1)}, f32[64,384]{1,0:T(8,128)S(1)}, u32[]{:S(2)}, u32[]{:S(2)}) %collective-permute-start.4) | collective-permute-done | bytes 98336 | tf_op jit(solution)/shard_map/ppermute | solution.py:16
  53.0 1.9 collective-permute-start.5
  54.9 2.3 %collective-permute-done.5 = f32[32,384]{1,0:T(8,128)S(1)} collective-permute-done((f32[32,384]{1,0:T(8,128)S(1)}, f32[32,384]{1,0:T(8,128)S(1)}, u32[]{:S(2)}, u32[]{:S(2)}) %collective-permute-start.5) | collective-permute-done | bytes 49184 | tf_op jit(solution)/shard_map/ppermute | solution.py:16
  57.2 3.1 %collective-permute-start.6 = (f32[16,384]{1,0:T(8,128)S(1)}, f32[16,384]{1,0:T(8,128)S(1)}, u32[]{:S(2)}, u32[]{:S(2)}) collective-permute-start(f32[16,384]{1,0:T(8,128)S(1)} %slice.112), channel_id=1, source_target_pairs={{0,4},{2,6},{4,0},{6,2},{1,5},{3,7},{5,1},{7,3},{8,12},{10,14},{12... | collective-permute-start | bytes 73736 | tf_op jit(solution)/shard_map/ppermute | solution.py:16
  60.3 1.8 collective-permute-done.6
  62.1 2.9 %collective-permute-start.7 = (f32[16,384]{1,0:T(8,128)S(1)}, f32[16,384]{1,0:T(8,128)S(1)}, u32[]{:S(2)}, u32[]{:S(2)}) collective-permute-start(f32[16,384]{1,0:T(8,128)S(1)} %get-tuple-element.21), channel_id=1, source_target_pairs={{0,4},{2,6},{4,0},{6,2},{1,5},{3,7},{5,1},{7,3},{8,12},{10,14},{12... | collective-permute-start | bytes 73736 | tf_op jit(solution)/shard_map/ppermute | solution.py:16
  65.1 0.9 convert_element_type.3.refs_0_
  65.9 1.5 collective-permute-start.28
  67.9 1.6 collective-permute-start.19
  70.0 9.5 %collective-permute-done.11 = f32[128,384]{1,0:T(8,128)S(1)} collective-permute-done((f32[128,384]{1,0:T(8,128)S(1)}, f32[128,384]{1,0:T(8,128)S(1)}, u32[]{:S(2)}, u32[]{:S(2)}) %collective-permute-start.11) | collective-permute-done | bytes 196640 | tf_op jit(solution)/shard_map/ppermute | solution.py:16
  79.6 2.1 %collective-permute-start.12 = (f32[64,384]{1,0:T(8,128)S(1)}, f32[64,384]{1,0:T(8,128)S(1)}, u32[]{:S(2)}, u32[]{:S(2)}) collective-permute-start(f32[64,384]{1,0:T(8,128)S(1)} %slice.116), channel_id=1, source_target_pairs={{0,2},{2,0},{4,6},{6,4},{1,3},{3,1},{5,7},{7,5},{8,10},{10,8},{12,... | collective-permute-start | bytes 294920 | tf_op jit(solution)/shard_map/ppermute | solution.py:16
  81.7 2.3 %collective-permute-start.20 = (f32[64,384]{1,0:T(8,128)S(1)}, f32[64,384]{1,0:T(8,128)S(1)}, u32[]{:S(2)}, u32[]{:S(2)}) collective-permute-start(f32[64,384]{1,0:T(8,128)S(1)} %slice.124), channel_id=1, source_target_pairs={{0,16},{8,24},{16,0},{24,8},{1,17},{9,25},{17,1},{25,9},{2,18},{10... | collective-permute-start | bytes 294920 | tf_op jit(solution)/shard_map/ppermute | solution.py:16
  84.0 1.6 collective-permute-start.9
  85.6 1.0 collective-permute-start.13
  87.1 1.3 collective-permute-start.21
  88.7 1.6 collective-permute-start.10
  91.3 2.1 %collective-permute-start.22 = (f32[16,384]{1,0:T(8,128)S(1)}, f32[16,384]{1,0:T(8,128)S(1)}, u32[]{:S(2)}, u32[]{:S(2)}) collective-permute-start(f32[16,384]{1,0:T(8,128)S(1)} %slice.128), channel_id=1, source_target_pairs={{0,4},{2,6},{4,0},{6,2},{1,5},{3,7},{5,1},{7,3},{8,12},{10,14},{12... | collective-permute-start | bytes 73736 | tf_op jit(solution)/shard_map/ppermute | solution.py:16
  93.4 1.7 collective-permute-done.14
  95.6 0.5 collective-permute-done.22
  96.1 2.2 %collective-permute-start.23 = (f32[16,384]{1,0:T(8,128)S(1)}, f32[16,384]{1,0:T(8,128)S(1)}, u32[]{:S(2)}, u32[]{:S(2)}) collective-permute-start(f32[16,384]{1,0:T(8,128)S(1)} %get-tuple-element.25), channel_id=1, source_target_pairs={{0,4},{2,6},{4,0},{6,2},{1,5},{3,7},{5,1},{7,3},{8,12},{10,14},{12... | collective-permute-start | bytes 73736 | tf_op jit(solution)/shard_map/ppermute | solution.py:16
  98.3 1.5 collective-permute-done.15
  100.9 1.4 collective-permute-start.24
  102.2 1.7 collective-permute-done.16
  104.0 0.9 collective-permute-start.17
  105.0 1.7 collective-permute-start.25
  106.7 1.9 collective-permute-done.17
  108.7 0.6 collective-permute-start.18
  109.7 1.9 collective-permute-start.26
  111.6 2.8 %collective-permute-done.18 = f32[128,384]{1,0:T(8,128)S(1)} collective-permute-done((f32[128,384]{1,0:T(8,128)S(1)}, f32[128,384]{1,0:T(8,128)S(1)}, u32[]{:S(2)}, u32[]{:S(2)}) %collective-permute-start.18) | collective-permute-done | bytes 196640 | tf_op jit(solution)/shard_map/ppermute | solution.py:16
  114.4 1.0 collective-permute-done.26
  115.4 1.1 pad_maximum_fusion.mine_ref
  116.5 1.7 collective-permute-start.31
  118.5 13.0 %collective-permute-done.31.refs_4_ = f32[256,512]{1,0:T(8,128)} collective-permute-done((f32[256,512]{1,0:T(8,128)}, f32[256,512]{1,0:T(8,128)}, u32[]{:S(2)}, u32[]{:S(2)}) %collective-permute-start.31) | collective-permute-done | bytes 524320 | tf_op jit(solution)/shard_map/ppermute | solution.py:16
  131.5 10.8 %collective-permute-done.32.refs_5_ = f32[256,512]{1,0:T(8,128)} collective-permute-done((f32[256,512]{1,0:T(8,128)}, f32[256,512]{1,0:T(8,128)}, u32[]{:S(2)}, u32[]{:S(2)}) %collective-permute-start.32) | collective-permute-done | bytes 524320 | tf_op jit(solution)/shard_map/ppermute | solution.py:16
  142.4 1.0 copy-done
  144.0 1.7 collective-permute-start.35
  146.1 55.3 %shard_map.52 = (f32[256,1024]{1,0:T(8,128)}, bf16[256,1024]{1,0:T(8,128)(2,1)S(1)}) custom-call(s32[5]{0:T(128)S(1)} %stack.63.place_ref, f32[256,1152]{1,0:T(8,128)} %pad_maximum_fusion.mine_ref, f32[256,1152]{1,0:T(8,128)} %collective-permute-done.27.other_ref, f32[256,512]{1,0:T(8,128)} %convert_element_type.3.refs_0_, ...), custom_call_target="tpu_custom_call" | custom-call | flops 42949672960 | bytes 16777216 | tf_op jit(solution)/shard_map/pallas_call | solution.py:313
  201.4 3.2 %shard_map.53 = f32[8,256,256]{2,1,0:T(8,128)} custom-call(s32[5]{0:T(128)S(1)} %stack.63.place_ref, bf16[256,1024]{1,0:T(8,128)(2,1)S(1)} %get-tuple-element.16.weights_ref, bf16[8,512,256]{2,1,0:T(8,128)(2,1)S(1)} %get-tuple-element.12.own_ref, f32[2,512,256]{2,1,0:T(8,128)S(1)} %collective-permute-done.refs_1_.refs_0_, f32[2,512,256]{2,1,0:T(8,128)S(1)} %copy-done.1, ...), custom_call_target="tpu_custom_call" | custom-call | flops 1073741824 | bytes 16777216 | tf_op jit(solution)/shard_map/pallas_call | solution.py:351
  (89 shorter events, 6.7 us)
Async XLA Ops:
  0.7 2.2 %copy-start.2 = (bf16[512,16,256]{2,1,0:T(8,128)(2,1)S(1)}, bf16[512,16,256]{2,1,0:T(8,128)(2,1)}, u32[]{:S(2)}) copy-start(bf16[512,16,256]{2,1,0:T(8,128)(2,1)} %param.4) | copy-start | bytes 12582916
  2.9 0.7 copy-start.3
  9.4 26.3 %collective-permute-start = (f32[2,512,256]{2,1,0:T(8,128)}, f32[2,512,256]{2,1,0:T(8,128)S(1)}, u32[]{:S(2)}, u32[]{:S(2)}) collective-permute-start(f32[2,512,256]{2,1,0:T(8,128)} %get-tuple-element.11), channel_id=1, source_target_pairs={{0,1},{1,0},{2,3},{3,2},{4,5},{5,4},{6,7},{7,6},{8,9},{9,8},{10,11... | collective-permute-start | bytes 3145736 | tf_op jit(solution)/shard_map/ppermute | solution.py:16
  38.1 2.9 %collective-permute-start.2 = (f32[256,1152]{1,0:T(8,128)S(1)}, f32[256,1152]{1,0:T(8,128)S(1)}, u32[]{:S(2)}, u32[]{:S(2)}) collective-permute-start(f32[256,1152]{1,0:T(8,128)S(1)} %get-tuple-element.14), channel_id=1, source_target_pairs={{0,8},{8,0},{16,24},{24,16},{1,9},{9,1},{17,25},{25,17},{2,10},{10... | collective-permute-start | bytes 3538952 | tf_op jit(solution)/shard_map/ppermute | solution.py:16
  41.2 23.9 %copy-start.4 = (bf16[256,512]{1,0:T(8,128)(2,1)S(1)}, bf16[256,512]{1,0:T(8,128)(2,1)}, u32[]{:S(2)}) copy-start(bf16[256,512]{1,0:T(8,128)(2,1)} %param.3) | copy-start | bytes 786436
  41.2 7.0 %collective-permute-start.3 = (f32[128,384]{1,0:T(8,128)S(1)}, f32[128,384]{1,0:T(8,128)S(1)}, u32[]{:S(2)}, u32[]{:S(2)}) collective-permute-start(f32[128,384]{1,0:T(8,128)S(1)} %slice.106), channel_id=1, source_target_pairs={{0,16},{8,24},{16,0},{24,8},{1,17},{9,25},{17,1},{25,9},{2,18},{10... | collective-permute-start | bytes 589832 | tf_op jit(solution)/shard_map/ppermute | solution.py:16
  48.3 4.7 %collective-permute-start.4 = (f32[64,384]{1,0:T(8,128)S(1)}, f32[64,384]{1,0:T(8,128)S(1)}, u32[]{:S(2)}, u32[]{:S(2)}) collective-permute-start(f32[64,384]{1,0:T(8,128)S(1)} %slice.108), channel_id=1, source_target_pairs={{0,1},{1,0},{2,3},{3,2},{4,5},{5,4},{6,7},{7,6},{8,9},{9,8},{10,11... | collective-permute-start | bytes 294920 | tf_op jit(solution)/shard_map/ppermute | solution.py:16
  53.0 4.2 %collective-permute-start.5 = (f32[32,384]{1,0:T(8,128)S(1)}, f32[32,384]{1,0:T(8,128)S(1)}, u32[]{:S(2)}, u32[]{:S(2)}) collective-permute-start(f32[32,384]{1,0:T(8,128)S(1)} %slice.110), channel_id=1, source_target_pairs={{0,2},{2,0},{4,6},{6,4},{1,3},{3,1},{5,7},{7,5},{8,10},{10,8},{12,... | collective-permute-start | bytes 147464 | tf_op jit(solution)/shard_map/ppermute | solution.py:16
  57.2 4.9 %collective-permute-start.6 = (f32[16,384]{1,0:T(8,128)S(1)}, f32[16,384]{1,0:T(8,128)S(1)}, u32[]{:S(2)}, u32[]{:S(2)}) collective-permute-start(f32[16,384]{1,0:T(8,128)S(1)} %slice.112), channel_id=1, source_target_pairs={{0,4},{2,6},{4,0},{6,2},{1,5},{3,7},{5,1},{7,3},{8,12},{10,14},{12... | collective-permute-start | bytes 73736 | tf_op jit(solution)/shard_map/ppermute | solution.py:16
  62.1 7.4 %collective-permute-start.7 = (f32[16,384]{1,0:T(8,128)S(1)}, f32[16,384]{1,0:T(8,128)S(1)}, u32[]{:S(2)}, u32[]{:S(2)}) collective-permute-start(f32[16,384]{1,0:T(8,128)S(1)} %get-tuple-element.21), channel_id=1, source_target_pairs={{0,4},{2,6},{4,0},{6,2},{1,5},{3,7},{5,1},{7,3},{8,12},{10,14},{12... | collective-permute-start | bytes 73736 | tf_op jit(solution)/shard_map/ppermute | solution.py:16
  65.9 52.3 %collective-permute-start.28 = (f32[256,512]{1,0:T(8,128)}, f32[256,512]{1,0:T(8,128)}, u32[]{:S(2)}, u32[]{:S(2)}) collective-permute-start(f32[256,512]{1,0:T(8,128)} %convert_element_type.3.refs_0_), channel_id=1, source_target_pairs={{0,1},{1,0},{2,3},{3,2},{4,5},{5,4},{6,7},{7,6},{8,9},{9,8},{10,11... | collective-permute-start | bytes 1572872 | tf_op jit(solution)/shard_map/ppermute | solution.py:16
  67.4 75.0 %collective-permute-start.1 = (f32[2,512,256]{2,1,0:T(8,128)S(1)}, f32[2,512,256]{2,1,0:T(8,128)S(1)}, u32[]{:S(2)}, u32[]{:S(2)}) collective-permute-start(f32[2,512,256]{2,1,0:T(8,128)S(1)} %collective-permute-done.refs_1_.refs_0_), channel_id=1, source_target_pairs={{0,8},{8,0},{16,24},{24,16},{1,9},{9,1},{17,25},{25,17},{2,10},{10... | collective-permute-start | bytes 3145736 | tf_op jit(solution)/shard_map/ppermute | solution.py:16
  67.4 12.1 %collective-permute-start.11 = (f32[128,384]{1,0:T(8,128)S(1)}, f32[128,384]{1,0:T(8,128)S(1)}, u32[]{:S(2)}, u32[]{:S(2)}) collective-permute-start(f32[128,384]{1,0:T(8,128)S(1)} %get-tuple-element.28), channel_id=1, source_target_pairs={{0,1},{1,0},{2,3},{3,2},{4,5},{5,4},{6,7},{7,6},{8,9},{9,8},{10,11... | collective-permute-start | bytes 589832 | tf_op jit(solution)/shard_map/ppermute | solution.py:16
  67.9 11.6 %collective-permute-start.19 = (f32[128,384]{1,0:T(8,128)S(1)}, f32[128,384]{1,0:T(8,128)S(1)}, u32[]{:S(2)}, u32[]{:S(2)}) collective-permute-start(f32[128,384]{1,0:T(8,128)S(1)} %get-tuple-element.27), channel_id=1, source_target_pairs={{0,2},{2,0},{4,6},{6,4},{1,3},{3,1},{5,7},{7,5},{8,10},{10,8},{12,... | collective-permute-start | bytes 589832 | tf_op jit(solution)/shard_map/ppermute | solution.py:16
  69.6 14.4 %collective-permute-start.8 = (f32[32,384]{1,0:T(8,128)S(1)}, f32[32,384]{1,0:T(8,128)S(1)}, u32[]{:S(2)}, u32[]{:S(2)}) collective-permute-start(f32[32,384]{1,0:T(8,128)S(1)} %pad_maximum_fusion.7), channel_id=1, source_target_pairs={{0,2},{2,0},{4,6},{6,4},{1,3},{3,1},{5,7},{7,5},{8,10},{10,8},{12,... | collective-permute-start | bytes 147464 | tf_op jit(solution)/shard_map/ppermute | solution.py:16
  79.6 6.0 %collective-permute-start.12 = (f32[64,384]{1,0:T(8,128)S(1)}, f32[64,384]{1,0:T(8,128)S(1)}, u32[]{:S(2)}, u32[]{:S(2)}) collective-permute-start(f32[64,384]{1,0:T(8,128)S(1)} %slice.116), channel_id=1, source_target_pairs={{0,2},{2,0},{4,6},{6,4},{1,3},{3,1},{5,7},{7,5},{8,10},{10,8},{12,... | collective-permute-start | bytes 294920 | tf_op jit(solution)/shard_map/ppermute | solution.py:16
  81.7 5.4 %collective-permute-start.20 = (f32[64,384]{1,0:T(8,128)S(1)}, f32[64,384]{1,0:T(8,128)S(1)}, u32[]{:S(2)}, u32[]{:S(2)}) collective-permute-start(f32[64,384]{1,0:T(8,128)S(1)} %slice.124), channel_id=1, source_target_pairs={{0,16},{8,24},{16,0},{24,8},{1,17},{9,25},{17,1},{25,9},{2,18},{10... | collective-permute-start | bytes 294920 | tf_op jit(solution)/shard_map/ppermute | solution.py:16
  84.0 4.7 %collective-permute-start.9 = (f32[64,384]{1,0:T(8,128)S(1)}, f32[64,384]{1,0:T(8,128)S(1)}, u32[]{:S(2)}, u32[]{:S(2)}) collective-permute-start(f32[64,384]{1,0:T(8,128)S(1)} %pad_maximum_fusion.4), channel_id=1, source_target_pairs={{0,1},{1,0},{2,3},{3,2},{4,5},{5,4},{6,7},{7,6},{8,9},{9,8},{10,11... | collective-permute-start | bytes 294920 | tf_op jit(solution)/shard_map/ppermute | solution.py:16
  85.6 4.7 %collective-permute-start.13 = (f32[32,384]{1,0:T(8,128)S(1)}, f32[32,384]{1,0:T(8,128)S(1)}, u32[]{:S(2)}, u32[]{:S(2)}) collective-permute-start(f32[32,384]{1,0:T(8,128)S(1)} %slice.118), channel_id=1, source_target_pairs={{0,16},{8,24},{16,0},{24,8},{1,17},{9,25},{17,1},{25,9},{2,18},{10... | collective-permute-start | bytes 147464 | tf_op jit(solution)/shard_map/ppermute | solution.py:16
  87.1 4.2 %collective-permute-start.21 = (f32[32,384]{1,0:T(8,128)S(1)}, f32[32,384]{1,0:T(8,128)S(1)}, u32[]{:S(2)}, u32[]{:S(2)}) collective-permute-start(f32[32,384]{1,0:T(8,128)S(1)} %slice.126), channel_id=1, source_target_pairs={{0,1},{1,0},{2,3},{3,2},{4,5},{5,4},{6,7},{7,6},{8,9},{9,8},{10,11... | collective-permute-start | bytes 147464 | tf_op jit(solution)/shard_map/ppermute | solution.py:16
  88.7 22.9 %collective-permute-start.10 = (f32[128,384]{1,0:T(8,128)S(1)}, f32[128,384]{1,0:T(8,128)S(1)}, u32[]{:S(2)}, u32[]{:S(2)}) collective-permute-start(f32[128,384]{1,0:T(8,128)S(1)} %pad_maximum_fusion.1), channel_id=1, source_target_pairs={{0,16},{8,24},{16,0},{24,8},{1,17},{9,25},{17,1},{25,9},{2,18},{10... | collective-permute-start | bytes 589832 | tf_op jit(solution)/shard_map/ppermute | solution.py:16
  90.3 4.8 %collective-permute-start.14 = (f32[16,384]{1,0:T(8,128)S(1)}, f32[16,384]{1,0:T(8,128)S(1)}, u32[]{:S(2)}, u32[]{:S(2)}) collective-permute-start(f32[16,384]{1,0:T(8,128)S(1)} %slice.120), channel_id=1, source_target_pairs={{0,4},{2,6},{4,0},{6,2},{1,5},{3,7},{5,1},{7,3},{8,12},{10,14},{12... | collective-permute-start | bytes 73736 | tf_op jit(solution)/shard_map/ppermute | solution.py:16
  91.3 4.8 %collective-permute-start.22 = (f32[16,384]{1,0:T(8,128)S(1)}, f32[16,384]{1,0:T(8,128)S(1)}, u32[]{:S(2)}, u32[]{:S(2)}) collective-permute-start(f32[16,384]{1,0:T(8,128)S(1)} %slice.128), channel_id=1, source_target_pairs={{0,4},{2,6},{4,0},{6,2},{1,5},{3,7},{5,1},{7,3},{8,12},{10,14},{12... | collective-permute-start | bytes 73736 | tf_op jit(solution)/shard_map/ppermute | solution.py:16
  95.1 4.7 %collective-permute-start.15 = (f32[16,384]{1,0:T(8,128)S(1)}, f32[16,384]{1,0:T(8,128)S(1)}, u32[]{:S(2)}, u32[]{:S(2)}) collective-permute-start(f32[16,384]{1,0:T(8,128)S(1)} %get-tuple-element.23), channel_id=1, source_target_pairs={{0,4},{2,6},{4,0},{6,2},{1,5},{3,7},{5,1},{7,3},{8,12},{10,14},{12... | collective-permute-start | bytes 73736 | tf_op jit(solution)/shard_map/ppermute | solution.py:16
  96.1 4.7 %collective-permute-start.23 = (f32[16,384]{1,0:T(8,128)S(1)}, f32[16,384]{1,0:T(8,128)S(1)}, u32[]{:S(2)}, u32[]{:S(2)}) collective-permute-start(f32[16,384]{1,0:T(8,128)S(1)} %get-tuple-element.25), channel_id=1, source_target_pairs={{0,4},{2,6},{4,0},{6,2},{1,5},{3,7},{5,1},{7,3},{8,12},{10,14},{12... | collective-permute-start | bytes 73736 | tf_op jit(solution)/shard_map/ppermute | solution.py:16
  99.9 4.1 %collective-permute-start.16 = (f32[32,384]{1,0:T(8,128)S(1)}, f32[32,384]{1,0:T(8,128)S(1)}, u32[]{:S(2)}, u32[]{:S(2)}) collective-permute-start(f32[32,384]{1,0:T(8,128)S(1)} %pad_maximum_fusion.8), channel_id=1, source_target_pairs={{0,16},{8,24},{16,0},{24,8},{1,17},{9,25},{17,1},{25,9},{2,18},{10... | collective-permute-start | bytes 147464 | tf_op jit(solution)/shard_map/ppermute | solution.py:16
  100.9 4.1 %collective-permute-start.24 = (f32[32,384]{1,0:T(8,128)S(1)}, f32[32,384]{1,0:T(8,128)S(1)}, u32[]{:S(2)}, u32[]{:S(2)}) collective-permute-start(f32[32,384]{1,0:T(8,128)S(1)} %pad_maximum_fusion.9), channel_id=1, source_target_pairs={{0,1},{1,0},{2,3},{3,2},{4,5},{5,4},{6,7},{7,6},{8,9},{9,8},{10,11... | collective-permute-start | bytes 147464 | tf_op jit(solution)/shard_map/ppermute | solution.py:16
  104.0 4.7 %collective-permute-start.17 = (f32[64,384]{1,0:T(8,128)S(1)}, f32[64,384]{1,0:T(8,128)S(1)}, u32[]{:S(2)}, u32[]{:S(2)}) collective-permute-start(f32[64,384]{1,0:T(8,128)S(1)} %pad_maximum_fusion.5), channel_id=1, source_target_pairs={{0,2},{2,0},{4,6},{6,4},{1,3},{3,1},{5,7},{7,5},{8,10},{10,8},{12,... | collective-permute-start | bytes 294920 | tf_op jit(solution)/shard_map/ppermute | solution.py:16
  105.0 4.7 %collective-permute-start.25 = (f32[64,384]{1,0:T(8,128)S(1)}, f32[64,384]{1,0:T(8,128)S(1)}, u32[]{:S(2)}, u32[]{:S(2)}) collective-permute-start(f32[64,384]{1,0:T(8,128)S(1)} %pad_maximum_fusion.6), channel_id=1, source_target_pairs={{0,16},{8,24},{16,0},{24,8},{1,17},{9,25},{17,1},{25,9},{2,18},{10... | collective-permute-start | bytes 294920 | tf_op jit(solution)/shard_map/ppermute | solution.py:16
  108.7 5.7 %collective-permute-start.18 = (f32[128,384]{1,0:T(8,128)S(1)}, f32[128,384]{1,0:T(8,128)S(1)}, u32[]{:S(2)}, u32[]{:S(2)}) collective-permute-start(f32[128,384]{1,0:T(8,128)S(1)} %pad_maximum_fusion.2), channel_id=1, source_target_pairs={{0,1},{1,0},{2,3},{3,2},{4,5},{5,4},{6,7},{7,6},{8,9},{9,8},{10,11... | collective-permute-start | bytes 589832 | tf_op jit(solution)/shard_map/ppermute | solution.py:16
  109.7 5.7 %collective-permute-start.26 = (f32[128,384]{1,0:T(8,128)S(1)}, f32[128,384]{1,0:T(8,128)S(1)}, u32[]{:S(2)}, u32[]{:S(2)}) collective-permute-start(f32[128,384]{1,0:T(8,128)S(1)} %pad_maximum_fusion.3), channel_id=1, source_target_pairs={{0,2},{2,0},{4,6},{6,4},{1,3},{3,1},{5,7},{7,5},{8,10},{10,8},{12,... | collective-permute-start | bytes 589832 | tf_op jit(solution)/shard_map/ppermute | solution.py:16
  116.5 29.6 %collective-permute-start.27 = (f32[256,1152]{1,0:T(8,128)}, f32[256,1152]{1,0:T(8,128)}, u32[]{:S(2)}, u32[]{:S(2)}) collective-permute-start(f32[256,1152]{1,0:T(8,128)} %pad_maximum_fusion.mine_ref), channel_id=1, source_target_pairs={{0,8},{8,0},{16,24},{24,16},{1,9},{9,1},{17,25},{25,17},{2,10},{10... | collective-permute-start | bytes 3538952 | tf_op jit(solution)/shard_map/ppermute | solution.py:16
  116.5 15.0 %collective-permute-start.31 = (f32[256,512]{1,0:T(8,128)}, f32[256,512]{1,0:T(8,128)}, u32[]{:S(2)}, u32[]{:S(2)}) collective-permute-start(f32[256,512]{1,0:T(8,128)} %convert_element_type.3.refs_0_), channel_id=1, source_target_pairs={{0,16},{8,24},{16,0},{24,8},{1,17},{9,25},{17,1},{25,9},{2,18},{10... | collective-permute-start | bytes 1572872 | tf_op jit(solution)/shard_map/ppermute | solution.py:16
  118.2 24.2 %collective-permute-start.32 = (f32[256,512]{1,0:T(8,128)}, f32[256,512]{1,0:T(8,128)}, u32[]{:S(2)}, u32[]{:S(2)}) collective-permute-start(f32[256,512]{1,0:T(8,128)} %collective-permute-done.28.refs_1_), channel_id=1, source_target_pairs={{0,16},{8,24},{16,0},{24,8},{1,17},{9,25},{17,1},{25,9},{2,18},{10... | collective-permute-start | bytes 1572872 | tf_op jit(solution)/shard_map/ppermute | solution.py:16
  118.5 25.4 %collective-permute-start.29 = (f32[256,512]{1,0:T(8,128)}, f32[256,512]{1,0:T(8,128)}, u32[]{:S(2)}, u32[]{:S(2)}) collective-permute-start(f32[256,512]{1,0:T(8,128)} %convert_element_type.3.refs_0_), channel_id=1, source_target_pairs={{0,8},{8,0},{16,24},{24,16},{1,9},{9,1},{17,25},{25,17},{2,10},{10... | collective-permute-start | bytes 1572872 | tf_op jit(solution)/shard_map/ppermute | solution.py:16
  131.5 14.2 %collective-permute-start.30 = (f32[256,512]{1,0:T(8,128)}, f32[256,512]{1,0:T(8,128)}, u32[]{:S(2)}, u32[]{:S(2)}) collective-permute-start(f32[256,512]{1,0:T(8,128)} %collective-permute-done.28.refs_1_), channel_id=1, source_target_pairs={{0,8},{8,0},{16,24},{24,16},{1,9},{9,1},{17,25},{25,17},{2,10},{10... | collective-permute-start | bytes 1572872 | tf_op jit(solution)/shard_map/ppermute | solution.py:16
  142.4 3.7 %collective-permute-start.33 = (f32[256,512]{1,0:T(8,128)}, f32[256,512]{1,0:T(8,128)}, u32[]{:S(2)}, u32[]{:S(2)}) collective-permute-start(f32[256,512]{1,0:T(8,128)} %collective-permute-done.31.refs_4_), channel_id=1, source_target_pairs={{0,8},{8,0},{16,24},{24,16},{1,9},{9,1},{17,25},{25,17},{2,10},{10... | collective-permute-start | bytes 1572872 | tf_op jit(solution)/shard_map/ppermute | solution.py:16
  142.4 1.0 copy-start
  143.4 2.7 %collective-permute-start.34 = (f32[256,512]{1,0:T(8,128)}, f32[256,512]{1,0:T(8,128)}, u32[]{:S(2)}, u32[]{:S(2)}) collective-permute-start(f32[256,512]{1,0:T(8,128)} %collective-permute-done.32.refs_5_), channel_id=1, source_target_pairs={{0,8},{8,0},{16,24},{24,16},{1,9},{9,1},{17,25},{25,17},{2,10},{10... | collective-permute-start | bytes 1572872 | tf_op jit(solution)/shard_map/ppermute | solution.py:16
  144.0 57.4 %copy-start.1 = (f32[2,512,256]{2,1,0:T(8,128)S(1)}, f32[2,512,256]{2,1,0:T(8,128)}, u32[]{:S(2)}) copy-start(f32[2,512,256]{2,1,0:T(8,128)} %copy-done) | copy-start | bytes 3145732
  144.0 57.4 %collective-permute-start.35 = (f32[2,512,256]{2,1,0:T(8,128)S(1)}, f32[2,512,256]{2,1,0:T(8,128)S(1)}, u32[]{:S(2)}, u32[]{:S(2)}) collective-permute-start(f32[2,512,256]{2,1,0:T(8,128)S(1)} %collective-permute-done.refs_1_.refs_0_), channel_id=1, source_target_pairs={{0,16},{8,24},{16,0},{24,8},{1,17},{9,25},{17,1},{25,9},{2,18},{10... | collective-permute-start | bytes 3145736 | tf_op jit(solution)/shard_map/ppermute | solution.py:16
  145.7 55.7 %collective-permute-start.36 = (f32[2,512,256]{2,1,0:T(8,128)}, f32[2,512,256]{2,1,0:T(8,128)S(1)}, u32[]{:S(2)}, u32[]{:S(2)}) collective-permute-start(f32[2,512,256]{2,1,0:T(8,128)} %copy-done), channel_id=1, source_target_pairs={{0,16},{8,24},{16,0},{24,8},{1,17},{9,25},{17,1},{25,9},{2,18},{10... | collective-permute-start | bytes 3145736 | tf_op jit(solution)/shard_map/ppermute | solution.py:16

commit v4 on v3

--- a/solution.py
+++ b/solution.py
@@ -40,22 +40,23 @@
     return place
 
 
+def swap_parts(parts, steps):
+    parts = lax.optimization_barrier(parts)
+    return lax.optimization_barrier([swap(part, step) for part, step in zip(parts, steps)])
+
+
 def reduce_parts(parts, orders, cuts):
-    for at in range(max(map(len, orders))):
-        moving = [(i, orders[i][at]) for i in range(len(parts)) if at < len(orders[i])]
-        kept, got = {}, {}
-        for i, step in moving:
-            half = parts[i].shape[0] // 2
-            kept[i], sent = (parts[i][:half], parts[i][half:]) if at < cuts[i] else (parts[i], parts[i])
-            got[i] = swap(sent, step)
-        parts = [kept[i] + got[i] if i in got else part for i, part in enumerate(parts)]
+    for at in range(cuts):
+        half = parts[0].shape[0] // 2
+        got = swap_parts([part[half:] for part in parts], [order[at] for order in orders])
+        parts = [part[:half] + other for part, other in zip(parts, got)]
     return parts
 
 
 def gather_parts(parts, orders, cuts):
-    for at in range(max(cuts) - 1, -1, -1):
-        got = {i: swap(parts[i], orders[i][at]) for i in range(len(parts)) if at < cuts[i]}
-        parts = [jnp.concatenate([part, got[i]], 0) if i in got else part for i, part in enumerate(parts)]
+    for at in range(cuts - 1, -1, -1):
+        got = swap_parts(parts, [order[at] for order in orders])
+        parts = [jnp.concatenate([part, other], 0) for part, other in zip(parts, got)]
     return parts
 
 
@@ -104,13 +105,14 @@
             leg += count
 
 
-def absorb(boundary_site, double_layer, legs, east_parts):
+def absorb(boundary_site, double_layer, legs, east_parts, dtype):
+    legs = jnp.stack(legs).astype(jnp.int32)
     depth, phys, right = boundary_site.shape
     tiles = max(1, depth // 128)
     tile = depth // tiles
     out_shape, out_specs = [], []
-    for i, count in enumerate(east_parts):
-        out_shape.append(jax.ShapeDtypeStruct((count, depth, right), jnp.bfloat16 if i == 0 else jnp.float32))
+    for count in east_parts:
+        out_shape.append(jax.ShapeDtypeStruct((count, depth, right), dtype))
         out_specs.append(pl.BlockSpec((count, tile, right), lambda t: (0, t, 0)))
     return pl.pallas_call(
         functools.partial(absorb_kernel, east_parts),
@@ -377,20 +379,19 @@
     east_part, right_parts = max(1, east // lb), max(1, lb // east)
     right_part = right // right_parts
     east_at, right_at = (l // right_parts) * east_part, (l % right_parts) * right_part
-    legs = [p * east + i for i in range(east)]
-    for s in range(1, rep):
-        legs += [(p ^ s) * east + east_at + i for i in range(east_part)]
-    legs = jnp.stack(legs).astype(jnp.int32)
-    own, *sent = absorb(boundary_site, double_layer, legs, [east] + [east_part] * (rep - 1))
+    legs = [(p ^ s) * east + east_at + i for s in range(1, rep) for i in range(east_part)]
+    sent = absorb(boundary_site, double_layer, legs, [east_part] * (rep - 1), jnp.float32)
     if right_parts > 1:
         sent = [lax.dynamic_slice_in_dim(piece, right_at, right_part, 2) for piece in sent]
     got = [swap(piece, ("rep", rep, s)) for s, piece in zip(range(1, rep), sent)]
+    (own,) = absorb(boundary_site, double_layer, [p * east + i for i in range(east)], [east], jnp.bfloat16)
     share = lax.dynamic_slice(own, (east_at, 0, right_at), (east_part, depth, right_part))
+    got, left_blocks = lax.optimization_barrier((got, left_blocks))
 
     near = across[:1] + steps["rep"][:1] + steps["rb"][:1]
     far = [step for step in across + steps["rep"] + steps["rb"] if step not in near]
-    orders = [near[i:] + near[:i] + far for i in range(3)]
-    cut = cut_steps(orders[0], chi // 4)
+    orders = [near[i:] + near[:i] for i in range(3)]
+    cut = cut_steps(near, chi // 4)
     chunk = (chi // 4) >> cut
     bits = [position(core + order[:cut]) for order in orders]
     places = jnp.stack([p] + bits).astype(jnp.int32)
@@ -398,14 +399,19 @@
     whole = kept + swap(sent, core[0])
     third = whole.shape[1] // 3
     parts = [whole[:, i * third : (i + 1) * third] for i in range(3)]
-    parts = reduce_parts(parts, orders, [cut] * 3)
-    parts = gather_parts(parts, orders, [cut] * 3)
+    parts = reduce_parts(parts, orders, cut)
+    whole = jnp.concatenate(parts, 1)
+    pairs = [[piece, swap(piece, core[0])] for piece in got]
+    whole, pairs = lax.optimization_barrier((whole, pairs))
+    for step in far:
+        whole = whole + swap(whole, step)
+    parts = [whole[:, i * third : (i + 1) * third] for i in range(3)]
+    parts = gather_parts(parts, orders, cut)
     whole = jnp.concatenate(parts, 1)
     other = swap(whole, core[0])
 
-    got = [gather_slots([(0, piece)], core) for piece in got]
-    held, whole = lax.optimization_barrier(([[piece for _, piece in pieces] for pieces in got], whole))
-    got = [gather_slots(list(zip(range(2), pieces)), across[::-1]) for pieces in held]
+    pairs, whole = lax.optimization_barrier((pairs, whole))
+    got = [gather_slots(list(zip(range(2), pair)), across[::-1]) for pair in pairs]
 
     places = jnp.stack([l, p] + bits).astype(jnp.int32)
     factor, weights = factorize(whole, other, left_blocks, places, chi, chunk, scale)

time: 205 us -> 160 us (0.78)
  waiting for transfers between devices: 84.9 us -> 46.2 us
  starting transfers between devices: 45.4 us -> 33.9 us
  Pallas kernels: 66.7 us -> 69.8 us
    ppermute x37 -> x32, waiting for transfers between devices: 84.9 us -> 46.2 us  [swap(): return lax.ppermute(array, axis, [(i, i ^ distance) for i in range(size)])]
    ppermute x37 -> x32, starting transfers between devices: 45.4 us -> 33.9 us  [swap(): return lax.ppermute(array, axis, [(i, i ^ distance) for i in range(size)])]
    pallas_call x1 -> x2, Pallas kernels: 5.82 us -> 8.9 us  [absorb(): pl.pallas_call(functools.partial(absorb_kernel, east_parts), grid=(tiles,...]
    unnamed x19 -> x12, local copies, waits for them, and re-layouts: 3.92 us -> 5.08 us
  transfers between devices with their start and end apart: 37 -> 32, of which waited for: 22 -> 22; matrix products, arithmetic and copies ran while one was open for 1% -> 0% of each run, Pallas kernels for 27% -> 40%
where the time goes in v4:
time: 160 us
  Pallas kernels  69.8 us (44%)
  waiting for transfers between devices  46.2 us (29%)
  starting transfers between devices  33.9 us (21%)
  local copies, waits for them, and re-layouts  5.38 us (3%)
  other arithmetic  3.44 us (2%)
    pallas_call x1, Pallas kernels, factorize(): pl.pallas_call(functools.partial(factor_kernel, scale, chunk), out_shape=...  55.3 us
    ppermute x32, waiting for transfers between devices, swap(): return lax.ppermute(array, axis, [(i, i ^ distance) for i in range(size)])  46.2 us
    ppermute x32, starting transfers between devices, swap(): return lax.ppermute(array, axis, [(i, i ^ distance) for i in range(size)])  33.9 us
    pallas_call x2, Pallas kernels, absorb(): pl.pallas_call(functools.partial(absorb_kernel, east_parts), grid=(tiles,...  8.9 us
    unnamed x12, local copies, waits for them, and re-layouts  5.08 us
  transfers between devices with their start and end apart: 32, of which 22 were waited for; matrix products, arithmetic and copies ran while one was open for 0% of the time, Pallas kernels for 40%

profile of v4, /device:TPU:0, one launch (start us, length us, event | category | flops | bytes accessed | tf_op | source)
XLA Modules:
  0.0 159.6 jit_solution(16905338990441900205)
XLA Ops:
  0.6 1.8 %convert_element_type.3.refs_0_ = f32[256,512]{1,0:T(8,128)} convert(bf16[256,512]{1,0:T(8,128)(2,1)} %param.3) | non-fusion elementwise | flops 131072 | bytes 786432 | tf_op jit(solution)/shard_map/convert_element_type | solution.py:373
  2.4 3.0 %collective-permute-start.1 = (f32[256,512]{1,0:T(8,128)}, f32[256,512]{1,0:T(8,128)}, u32[]{:S(2)}, u32[]{:S(2)}) collective-permute-start(f32[256,512]{1,0:T(8,128)} %convert_element_type.3.refs_0_), channel_id=1, source_target_pairs={{0,1},{1,0},{2,3},{3,2},{4,5},{5,4},{6,7},{7,6},{8,9},{9,8},{10,11... | collective-permute-start | bytes 1572872 | tf_op jit(solution)/shard_map/ppermute | solution.py:16
  5.4 1.5 collective-permute-start.4
  7.0 2.2 %copy-done = bf16[512,16,256]{2,1,0:T(8,128)(2,1)S(1)} copy-done((bf16[512,16,256]{2,1,0:T(8,128)(2,1)S(1)}, bf16[512,16,256]{2,1,0:T(8,128)(2,1)}, u32[]{:S(2)}) %copy-start) | copy-done | bytes 4194328
  9.2 0.7 copy-done.4
  9.9 4.4 %shard_map.51 = f32[2,512,256]{2,1,0:T(8,128)} custom-call(s32[2]{0:T(128)S(1)} %pad_add_fusion.1.legs_ref, bf16[8192,256]{1,0:T(8,128)(2,1)S(1)} %bitcast.16, f32[16,16]{1,0:T(8,128)S(1)} %copy-done.4), custom_call_target="tpu_custom_call" | custom-call | flops 268435456 | bytes 16777216 | tf_op jit(solution)/shard_map/pallas_call | solution.py:117
  14.7 3.7 %collective-permute-done.1.refs_1_ = f32[256,512]{1,0:T(8,128)} collective-permute-done((f32[256,512]{1,0:T(8,128)}, f32[256,512]{1,0:T(8,128)}, u32[]{:S(2)}, u32[]{:S(2)}) %collective-permute-start.1) | collective-permute-done | bytes 524320 | tf_op jit(solution)/shard_map/ppermute | solution.py:16
  18.5 2.0 %collective-permute-start.5 = (f32[256,512]{1,0:T(8,128)}, f32[256,512]{1,0:T(8,128)}, u32[]{:S(2)}, u32[]{:S(2)}) collective-permute-start(f32[256,512]{1,0:T(8,128)} %collective-permute-done.1.refs_1_), channel_id=1, source_target_pairs={{0,16},{8,24},{16,0},{24,8},{1,17},{9,25},{17,1},{25,9},{2,18},{10... | collective-permute-start | bytes 1572872 | tf_op jit(solution)/shard_map/ppermute | solution.py:16
  21.0 10.0 %collective-permute-done.5.refs_5_ = f32[256,512]{1,0:T(8,128)} collective-permute-done((f32[256,512]{1,0:T(8,128)}, f32[256,512]{1,0:T(8,128)}, u32[]{:S(2)}, u32[]{:S(2)}) %collective-permute-start.5) | collective-permute-done | bytes 524320 | tf_op jit(solution)/shard_map/ppermute | solution.py:16
  31.2 2.2 %copy-done.1 = bf16[512,16,256]{2,1,0:T(8,128)(2,1)S(1)} copy-done((bf16[512,16,256]{2,1,0:T(8,128)(2,1)S(1)}, bf16[512,16,256]{2,1,0:T(8,128)(2,1)}, u32[]{:S(2)}) %copy-start.1) | copy-done | bytes 4194328
  33.3 4.5 %shard_map.50.own_ref = bf16[8,512,256]{2,1,0:T(8,128)(2,1)S(1)} custom-call(s32[8]{0:T(128)S(1)} %stack.76.legs_ref, bf16[8192,256]{1,0:T(8,128)(2,1)S(1)} %bitcast.17, f32[16,16]{1,0:T(8,128)S(1)} %copy-done.5), custom_call_target="tpu_custom_call" | custom-call | flops 1073741824 | bytes 16777216 | tf_op jit(solution)/shard_map/pallas_call | solution.py:117
  38.0 2.0 %collective-permute-done.refs_1_.refs_0_ = f32[2,512,256]{2,1,0:T(8,128)S(1)} collective-permute-done((f32[2,512,256]{2,1,0:T(8,128)}, f32[2,512,256]{2,1,0:T(8,128)S(1)}, u32[]{:S(2)}, u32[]{:S(2)}) %collective-permute-start) | collective-permute-done | bytes 1048608 | tf_op jit(solution)/shard_map/ppermute | solution.py:16
  40.0 2.3 %shard_map.52 = (f32[256,1152]{1,0:T(8,128)S(1)}, f32[256,1152]{1,0:T(8,128)S(1)}) custom-call(s32[4]{0:T(128)S(1)} %pad_add_fusion.place_ref, bf16[2,512,256]{2,1,0:T(8,128)(2,1)S(1)} %constant_dynamic-slice_fusion.refs_0_, f32[2,512,256]{2,1,0:T(8,128)S(1)} %collective-permute-done.refs_1_.refs_0_), custom_call_target="tpu_custom_call" | custom-call | flops 536870912 | bytes 6291456 | tf_op jit(solution)/shard_map/pallas_call | solution.py:162
  42.5 2.8 %collective-permute-done.8 = f32[256,1152]{1,0:T(8,128)S(1)} collective-permute-done((f32[256,1152]{1,0:T(8,128)S(1)}, f32[256,1152]{1,0:T(8,128)S(1)}, u32[]{:S(2)}, u32[]{:S(2)}) %collective-permute-start.8) | collective-permute-done | bytes 1179680 | tf_op jit(solution)/shard_map/ppermute | solution.py:16
  45.5 1.8 %collective-permute-start.10 = (f32[128,384]{1,0:T(8,128)S(1)}, f32[128,384]{1,0:T(8,128)S(1)}, u32[]{:S(2)}, u32[]{:S(2)}) collective-permute-start(f32[128,384]{1,0:T(8,128)S(1)} %get-tuple-element.61), channel_id=1, source_target_pairs={{0,1},{1,0},{2,3},{3,2},{4,5},{5,4},{6,7},{7,6},{8,9},{9,8},{10,11... | collective-permute-start | bytes 589832 | tf_op jit(solution)/shard_map/ppermute | solution.py:16
  47.3 1.6 collective-permute-start.11
  48.8 1.5 collective-permute-start.9
  50.3 2.1 %collective-permute-done.10 = f32[128,384]{1,0:T(8,128)S(1)} collective-permute-done((f32[128,384]{1,0:T(8,128)S(1)}, f32[128,384]{1,0:T(8,128)S(1)}, u32[]{:S(2)}, u32[]{:S(2)}) %collective-permute-start.10) | collective-permute-done | bytes 196640 | tf_op jit(solution)/shard_map/ppermute | solution.py:16
  52.5 1.5 collective-permute-done.11
  53.9 1.3 collective-permute-done.9
  55.4 0.6 collective-permute-start.12
  56.3 1.6 %collective-permute-start.14 = (f32[64,384]{1,0:T(8,128)S(1)}, f32[64,384]{1,0:T(8,128)S(1)}, u32[]{:S(2)}, u32[]{:S(2)}) collective-permute-start(f32[64,384]{1,0:T(8,128)S(1)} %slice.102), channel_id=1, source_target_pairs={{0,16},{8,24},{16,0},{24,8},{1,17},{9,25},{17,1},{25,9},{2,18},{10... | collective-permute-start | bytes 294920 | tf_op jit(solution)/shard_map/ppermute | solution.py:16
  57.9 2.2 %collective-permute-done.12 = f32[64,384]{1,0:T(8,128)S(1)} collective-permute-done((f32[64,384]{1,0:T(8,128)S(1)}, f32[64,384]{1,0:T(8,128)S(1)}, u32[]{:S(2)}, u32[]{:S(2)}) %collective-permute-start.12) | collective-permute-done | bytes 98336 | tf_op jit(solution)/shard_map/ppermute | solution.py:16
  60.1 0.5 collective-permute-done.13
  61.0 1.8 %collective-permute-start.15 = (f32[32,384]{1,0:T(8,128)S(1)}, f32[32,384]{1,0:T(8,128)S(1)}, u32[]{:S(2)}, u32[]{:S(2)}) collective-permute-start(f32[32,384]{1,0:T(8,128)S(1)} %slice.104), channel_id=1, source_target_pairs={{0,2},{2,0},{4,6},{6,4},{1,3},{3,1},{5,7},{7,5},{8,10},{10,8},{12,... | collective-permute-start | bytes 147464 | tf_op jit(solution)/shard_map/ppermute | solution.py:16
  62.8 1.5 collective-permute-start.16
  64.2 1.5 collective-permute-start.17
  65.8 1.1 collective-permute-done.16
  66.8 1.5 collective-permute-done.17
  68.4 2.6 %collective-permute-start.19 = (f32[32,1152]{1,0:T(8,128)S(1)}, f32[32,1152]{1,0:T(8,128)S(1)}, u32[]{:S(2)}, u32[]{:S(2)}) collective-permute-start(f32[32,1152]{1,0:T(8,128)S(1)} %pad_maximum_fusion.3), channel_id=1, source_target_pairs={{0,4},{2,6},{4,0},{6,2},{1,5},{3,7},{5,1},{7,3},{8,12},{10,14},{12... | collective-permute-start | bytes 442376 | tf_op jit(solution)/shard_map/ppermute | solution.py:16
  71.1 4.9 %collective-permute-done.19 = f32[32,1152]{1,0:T(8,128)S(1)} collective-permute-done((f32[32,1152]{1,0:T(8,128)S(1)}, f32[32,1152]{1,0:T(8,128)S(1)}, u32[]{:S(2)}, u32[]{:S(2)}) %collective-permute-start.19) | collective-permute-done | bytes 147488 | tf_op jit(solution)/shard_map/ppermute | solution.py:16
  76.6 1.7 %collective-permute-start.22 = (f32[32,384]{1,0:T(8,128)S(1)}, f32[32,384]{1,0:T(8,128)S(1)}, u32[]{:S(2)}, u32[]{:S(2)}) collective-permute-start(f32[32,384]{1,0:T(8,128)S(1)} %get-tuple-element.83), channel_id=1, source_target_pairs={{0,1},{1,0},{2,3},{3,2},{4,5},{5,4},{6,7},{7,6},{8,9},{9,8},{10,11... | collective-permute-start | bytes 147464 | tf_op jit(solution)/shard_map/ppermute | solution.py:16
  78.2 2.0 %collective-permute-done.20 = f32[32,384]{1,0:T(8,128)S(1)} collective-permute-done((f32[32,384]{1,0:T(8,128)S(1)}, f32[32,384]{1,0:T(8,128)S(1)}, u32[]{:S(2)}, u32[]{:S(2)}) %collective-permute-start.20) | collective-permute-done | bytes 49184 | tf_op jit(solution)/shard_map/ppermute | solution.py:16
  80.2 0.5 collective-permute-done.21
  80.8 1.7 %collective-permute-start.23 = (f32[64,384]{1,0:T(8,128)S(1)}, f32[64,384]{1,0:T(8,128)S(1)}, u32[]{:S(2)}, u32[]{:S(2)}) collective-permute-start(f32[64,384]{1,0:T(8,128)S(1)} %pad_maximum_fusion.4), channel_id=1, source_target_pairs={{0,1},{1,0},{2,3},{3,2},{4,5},{5,4},{6,7},{7,6},{8,9},{9,8},{10,11... | collective-permute-start | bytes 294920 | tf_op jit(solution)/shard_map/ppermute | solution.py:16
  82.4 1.9 %collective-permute-start.24 = (f32[64,384]{1,0:T(8,128)S(1)}, f32[64,384]{1,0:T(8,128)S(1)}, u32[]{:S(2)}, u32[]{:S(2)}) collective-permute-start(f32[64,384]{1,0:T(8,128)S(1)} %pad_maximum_fusion.5), channel_id=1, source_target_pairs={{0,2},{2,0},{4,6},{6,4},{1,3},{3,1},{5,7},{7,5},{8,10},{10,8},{12,... | collective-permute-start | bytes 294920 | tf_op jit(solution)/shard_map/ppermute | solution.py:16
  84.4 1.5 collective-permute-start.25
  85.9 0.6 collective-permute-done.23
  86.4 1.5 collective-permute-done.24
  87.9 1.1 collective-permute-done.25
  89.1 1.6 collective-permute-start.26
  91.2 3.6 %collective-permute-done.26 = f32[128,384]{1,0:T(8,128)S(1)} collective-permute-done((f32[128,384]{1,0:T(8,128)S(1)}, f32[128,384]{1,0:T(8,128)S(1)}, u32[]{:S(2)}, u32[]{:S(2)}) %collective-permute-start.26) | collective-permute-done | bytes 196640 | tf_op jit(solution)/shard_map/ppermute | solution.py:16
  94.8 1.5 collective-permute-done.27
  96.8 1.1 maximum_maximum_fusion.mine_ref
  98.4 1.6 %collective-permute-start.31 = (f32[2,512,256]{2,1,0:T(8,128)}, f32[2,512,256]{2,1,0:T(8,128)S(1)}, u32[]{:S(2)}, u32[]{:S(2)}) collective-permute-start(f32[2,512,256]{2,1,0:T(8,128)} %copy-done.2), channel_id=1, source_target_pairs={{0,16},{8,24},{16,0},{24,8},{1,17},{9,25},{17,1},{25,9},{2,18},{10... | collective-permute-start | bytes 3145736 | tf_op jit(solution)/shard_map/ppermute | solution.py:16
  100.0 1.1 collective-permute-done.29.other_ref
  101.1 55.3 %shard_map.53 = (f32[256,1024]{1,0:T(8,128)}, bf16[256,1024]{1,0:T(8,128)(2,1)S(1)}) custom-call(s32[5]{0:T(128)S(1)} %stack.66.place_ref, f32[256,1152]{1,0:T(8,128)} %maximum_maximum_fusion.mine_ref, f32[256,1152]{1,0:T(8,128)} %collective-permute-done.29.other_ref, f32[256,512]{1,0:T(8,128)} %convert_element_type.3.refs_0_, ...), custom_call_target="tpu_custom_call" | custom-call | flops 42949672960 | bytes 16777216 | tf_op jit(solution)/shard_map/pallas_call | solution.py:315
  156.4 3.2 %shard_map.54 = f32[8,256,256]{2,1,0:T(8,128)} custom-call(s32[5]{0:T(128)S(1)} %stack.66.place_ref, bf16[256,1024]{1,0:T(8,128)(2,1)S(1)} %get-tuple-element.108.weights_ref, bf16[8,512,256]{2,1,0:T(8,128)(2,1)S(1)} %shard_map.50.own_ref, f32[2,512,256]{2,1,0:T(8,128)S(1)} %collective-permute-done.refs_1_.refs_0_, f32[2,512,256]{2,1,0:T(8,128)S(1)} %copy-done.3, ...), custom_call_target="tpu_custom_call" | custom-call | flops 1073741824 | bytes 16777216 | tf_op jit(solution)/shard_map/pallas_call | solution.py:353
  (63 shorter events, 4.6 us)
Async XLA Ops:
  2.4 16.0 %collective-permute-start.1 = (f32[256,512]{1,0:T(8,128)}, f32[256,512]{1,0:T(8,128)}, u32[]{:S(2)}, u32[]{:S(2)}) collective-permute-start(f32[256,512]{1,0:T(8,128)} %convert_element_type.3.refs_0_), channel_id=1, source_target_pairs={{0,1},{1,0},{2,3},{3,2},{4,5},{5,4},{6,7},{7,6},{8,9},{9,8},{10,11... | collective-permute-start | bytes 1572872 | tf_op jit(solution)/shard_map/ppermute | solution.py:16
  5.4 15.6 %collective-permute-start.4 = (f32[256,512]{1,0:T(8,128)}, f32[256,512]{1,0:T(8,128)}, u32[]{:S(2)}, u32[]{:S(2)}) collective-permute-start(f32[256,512]{1,0:T(8,128)} %convert_element_type.3.refs_0_), channel_id=1, source_target_pairs={{0,16},{8,24},{16,0},{24,8},{1,17},{9,25},{17,1},{25,9},{2,18},{10... | collective-permute-start | bytes 1572872 | tf_op jit(solution)/shard_map/ppermute | solution.py:16
  7.0 2.2 %copy-start = (bf16[512,16,256]{2,1,0:T(8,128)(2,1)S(1)}, bf16[512,16,256]{2,1,0:T(8,128)(2,1)}, u32[]{:S(2)}) copy-start(bf16[512,16,256]{2,1,0:T(8,128)(2,1)} %param.4) | copy-start | bytes 12582916
  9.2 0.7 copy-start.4
  9.9 21.3 %copy-start.5 = (f32[16,16]{1,0:T(8,128)S(1)}, f32[16,16]{1,0:T(8,128)}, u32[]{:S(2)}) copy-start(f32[16,16]{1,0:T(8,128)} %double_ref.3) | copy-start | bytes 3076
  14.2 25.8 %collective-permute-start = (f32[2,512,256]{2,1,0:T(8,128)}, f32[2,512,256]{2,1,0:T(8,128)S(1)}, u32[]{:S(2)}, u32[]{:S(2)}) collective-permute-start(f32[2,512,256]{2,1,0:T(8,128)} %shard_map.51), channel_id=1, source_target_pairs={{0,1},{1,0},{2,3},{3,2},{4,5},{5,4},{6,7},{7,6},{8,9},{9,8},{10,11... | collective-permute-start | bytes 3145736 | tf_op jit(solution)/shard_map/ppermute | solution.py:16
  18.5 12.6 %collective-permute-start.5 = (f32[256,512]{1,0:T(8,128)}, f32[256,512]{1,0:T(8,128)}, u32[]{:S(2)}, u32[]{:S(2)}) collective-permute-start(f32[256,512]{1,0:T(8,128)} %collective-permute-done.1.refs_1_), channel_id=1, source_target_pairs={{0,16},{8,24},{16,0},{24,8},{1,17},{9,25},{17,1},{25,9},{2,18},{10... | collective-permute-start | bytes 1572872 | tf_op jit(solution)/shard_map/ppermute | solution.py:16
  20.5 17.5 %collective-permute-start.2 = (f32[256,512]{1,0:T(8,128)}, f32[256,512]{1,0:T(8,128)}, u32[]{:S(2)}, u32[]{:S(2)}) collective-permute-start(f32[256,512]{1,0:T(8,128)} %convert_element_type.3.refs_0_), channel_id=1, source_target_pairs={{0,8},{8,0},{16,24},{24,16},{1,9},{9,1},{17,25},{25,17},{2,10},{10... | collective-permute-start | bytes 1572872 | tf_op jit(solution)/shard_map/ppermute | solution.py:16
  20.5 19.5 %collective-permute-start.3 = (f32[256,512]{1,0:T(8,128)}, f32[256,512]{1,0:T(8,128)}, u32[]{:S(2)}, u32[]{:S(2)}) collective-permute-start(f32[256,512]{1,0:T(8,128)} %collective-permute-done.1.refs_1_), channel_id=1, source_target_pairs={{0,8},{8,0},{16,24},{24,16},{1,9},{9,1},{17,25},{25,17},{2,10},{10... | collective-permute-start | bytes 1572872 | tf_op jit(solution)/shard_map/ppermute | solution.py:16
  21.0 19.0 %collective-permute-start.6 = (f32[256,512]{1,0:T(8,128)}, f32[256,512]{1,0:T(8,128)}, u32[]{:S(2)}, u32[]{:S(2)}) collective-permute-start(f32[256,512]{1,0:T(8,128)} %collective-permute-done.4.refs_4_), channel_id=1, source_target_pairs={{0,8},{8,0},{16,24},{24,16},{1,9},{9,1},{17,25},{25,17},{2,10},{10... | collective-permute-start | bytes 1572872 | tf_op jit(solution)/shard_map/ppermute | solution.py:16
  31.1 8.9 %collective-permute-start.7 = (f32[256,512]{1,0:T(8,128)}, f32[256,512]{1,0:T(8,128)}, u32[]{:S(2)}, u32[]{:S(2)}) collective-permute-start(f32[256,512]{1,0:T(8,128)} %collective-permute-done.5.refs_5_), channel_id=1, source_target_pairs={{0,8},{8,0},{16,24},{24,16},{1,9},{9,1},{17,25},{25,17},{2,10},{10... | collective-permute-start | bytes 1572872 | tf_op jit(solution)/shard_map/ppermute | solution.py:16
  31.2 2.2 %copy-start.1 = (bf16[512,16,256]{2,1,0:T(8,128)(2,1)S(1)}, bf16[512,16,256]{2,1,0:T(8,128)(2,1)}, u32[]{:S(2)}) copy-start(bf16[512,16,256]{2,1,0:T(8,128)(2,1)} %param.4) | copy-start | bytes 12582916
  42.4 2.9 %collective-permute-start.8 = (f32[256,1152]{1,0:T(8,128)S(1)}, f32[256,1152]{1,0:T(8,128)S(1)}, u32[]{:S(2)}, u32[]{:S(2)}) collective-permute-start(f32[256,1152]{1,0:T(8,128)S(1)} %get-tuple-element.59), channel_id=1, source_target_pairs={{0,8},{8,0},{16,24},{24,16},{1,9},{9,1},{17,25},{25,17},{2,10},{10... | collective-permute-start | bytes 3538952 | tf_op jit(solution)/shard_map/ppermute | solution.py:16
  45.5 7.0 %collective-permute-start.10 = (f32[128,384]{1,0:T(8,128)S(1)}, f32[128,384]{1,0:T(8,128)S(1)}, u32[]{:S(2)}, u32[]{:S(2)}) collective-permute-start(f32[128,384]{1,0:T(8,128)S(1)} %get-tuple-element.61), channel_id=1, source_target_pairs={{0,1},{1,0},{2,3},{3,2},{4,5},{5,4},{6,7},{7,6},{8,9},{9,8},{10,11... | collective-permute-start | bytes 589832 | tf_op jit(solution)/shard_map/ppermute | solution.py:16
  47.3 6.7 %collective-permute-start.11 = (f32[128,384]{1,0:T(8,128)S(1)}, f32[128,384]{1,0:T(8,128)S(1)}, u32[]{:S(2)}, u32[]{:S(2)}) collective-permute-start(f32[128,384]{1,0:T(8,128)S(1)} %get-tuple-element.62), channel_id=1, source_target_pairs={{0,2},{2,0},{4,6},{6,4},{1,3},{3,1},{5,7},{7,5},{8,10},{10,8},{12,... | collective-permute-start | bytes 589832 | tf_op jit(solution)/shard_map/ppermute | solution.py:16
  48.8 6.4 %collective-permute-start.9 = (f32[128,384]{1,0:T(8,128)S(1)}, f32[128,384]{1,0:T(8,128)S(1)}, u32[]{:S(2)}, u32[]{:S(2)}) collective-permute-start(f32[128,384]{1,0:T(8,128)S(1)} %get-tuple-element.60), channel_id=1, source_target_pairs={{0,16},{8,24},{16,0},{24,8},{1,17},{9,25},{17,1},{25,9},{2,18},{10... | collective-permute-start | bytes 589832 | tf_op jit(solution)/shard_map/ppermute | solution.py:16
  55.4 4.7 %collective-permute-start.12 = (f32[64,384]{1,0:T(8,128)S(1)}, f32[64,384]{1,0:T(8,128)S(1)}, u32[]{:S(2)}, u32[]{:S(2)}) collective-permute-start(f32[64,384]{1,0:T(8,128)S(1)} %slice.98), channel_id=1, source_target_pairs={{0,1},{1,0},{2,3},{3,2},{4,5},{5,4},{6,7},{7,6},{8,9},{9,8},{10,11... | collective-permute-start | bytes 294920 | tf_op jit(solution)/shard_map/ppermute | solution.py:16
  56.0 4.6 %collective-permute-start.13 = (f32[64,384]{1,0:T(8,128)S(1)}, f32[64,384]{1,0:T(8,128)S(1)}, u32[]{:S(2)}, u32[]{:S(2)}) collective-permute-start(f32[64,384]{1,0:T(8,128)S(1)} %slice.100), channel_id=1, source_target_pairs={{0,2},{2,0},{4,6},{6,4},{1,3},{3,1},{5,7},{7,5},{8,10},{10,8},{12,... | collective-permute-start | bytes 294920 | tf_op jit(solution)/shard_map/ppermute | solution.py:16
  56.3 4.6 %collective-permute-start.14 = (f32[64,384]{1,0:T(8,128)S(1)}, f32[64,384]{1,0:T(8,128)S(1)}, u32[]{:S(2)}, u32[]{:S(2)}) collective-permute-start(f32[64,384]{1,0:T(8,128)S(1)} %slice.102), channel_id=1, source_target_pairs={{0,16},{8,24},{16,0},{24,8},{1,17},{9,25},{17,1},{25,9},{2,18},{10... | collective-permute-start | bytes 294920 | tf_op jit(solution)/shard_map/ppermute | solution.py:16
  57.9 10.5 %collective-permute-start.18 = (f32[2,512,256]{2,1,0:T(8,128)S(1)}, f32[2,512,256]{2,1,0:T(8,128)S(1)}, u32[]{:S(2)}, u32[]{:S(2)}) collective-permute-start(f32[2,512,256]{2,1,0:T(8,128)S(1)} %collective-permute-done.refs_1_.refs_0_), channel_id=1, source_target_pairs={{0,8},{8,0},{16,24},{24,16},{1,9},{9,1},{17,25},{25,17},{2,10},{10... | collective-permute-start | bytes 3145736 | tf_op jit(solution)/shard_map/ppermute | solution.py:16
  61.0 4.8 %collective-permute-start.15 = (f32[32,384]{1,0:T(8,128)S(1)}, f32[32,384]{1,0:T(8,128)S(1)}, u32[]{:S(2)}, u32[]{:S(2)}) collective-permute-start(f32[32,384]{1,0:T(8,128)S(1)} %slice.104), channel_id=1, source_target_pairs={{0,2},{2,0},{4,6},{6,4},{1,3},{3,1},{5,7},{7,5},{8,10},{10,8},{12,... | collective-permute-start | bytes 147464 | tf_op jit(solution)/shard_map/ppermute | solution.py:16
  62.8 4.1 %collective-permute-start.16 = (f32[32,384]{1,0:T(8,128)S(1)}, f32[32,384]{1,0:T(8,128)S(1)}, u32[]{:S(2)}, u32[]{:S(2)}) collective-permute-start(f32[32,384]{1,0:T(8,128)S(1)} %slice.106), channel_id=1, source_target_pairs={{0,16},{8,24},{16,0},{24,8},{1,17},{9,25},{17,1},{25,9},{2,18},{10... | collective-permute-start | bytes 147464 | tf_op jit(solution)/shard_map/ppermute | solution.py:16
  64.2 4.1 %collective-permute-start.17 = (f32[32,384]{1,0:T(8,128)S(1)}, f32[32,384]{1,0:T(8,128)S(1)}, u32[]{:S(2)}, u32[]{:S(2)}) collective-permute-start(f32[32,384]{1,0:T(8,128)S(1)} %slice.108), channel_id=1, source_target_pairs={{0,1},{1,0},{2,3},{3,2},{4,5},{5,4},{6,7},{7,6},{8,9},{9,8},{10,11... | collective-permute-start | bytes 147464 | tf_op jit(solution)/shard_map/ppermute | solution.py:16
  68.4 20.7 %copy-start.2 = (f32[2,512,256]{2,1,0:T(8,128)}, f32[2,512,256]{2,1,0:T(8,128)S(1)}, u32[]{:S(2)}) copy-start(f32[2,512,256]{2,1,0:T(8,128)S(1)} %collective-permute-done.18.refs_1_) | copy-start | bytes 3145732
  68.4 7.6 %collective-permute-start.19 = (f32[32,1152]{1,0:T(8,128)S(1)}, f32[32,1152]{1,0:T(8,128)S(1)}, u32[]{:S(2)}, u32[]{:S(2)}) collective-permute-start(f32[32,1152]{1,0:T(8,128)S(1)} %pad_maximum_fusion.3), channel_id=1, source_target_pairs={{0,4},{2,6},{4,0},{6,2},{1,5},{3,7},{5,1},{7,3},{8,12},{10,14},{12... | collective-permute-start | bytes 442376 | tf_op jit(solution)/shard_map/ppermute | solution.py:16
  76.0 4.2 %collective-permute-start.20 = (f32[32,384]{1,0:T(8,128)S(1)}, f32[32,384]{1,0:T(8,128)S(1)}, u32[]{:S(2)}, u32[]{:S(2)}) collective-permute-start(f32[32,384]{1,0:T(8,128)S(1)} %get-tuple-element.81), channel_id=1, source_target_pairs={{0,2},{2,0},{4,6},{6,4},{1,3},{3,1},{5,7},{7,5},{8,10},{10,8},{12,... | collective-permute-start | bytes 147464 | tf_op jit(solution)/shard_map/ppermute | solution.py:16
  76.1 4.6 %collective-permute-start.21 = (f32[32,384]{1,0:T(8,128)S(1)}, f32[32,384]{1,0:T(8,128)S(1)}, u32[]{:S(2)}, u32[]{:S(2)}) collective-permute-start(f32[32,384]{1,0:T(8,128)S(1)} %get-tuple-element.82), channel_id=1, source_target_pairs={{0,16},{8,24},{16,0},{24,8},{1,17},{9,25},{17,1},{25,9},{2,18},{10... | collective-permute-start | bytes 147464 | tf_op jit(solution)/shard_map/ppermute | solution.py:16
  76.6 4.2 %collective-permute-start.22 = (f32[32,384]{1,0:T(8,128)S(1)}, f32[32,384]{1,0:T(8,128)S(1)}, u32[]{:S(2)}, u32[]{:S(2)}) collective-permute-start(f32[32,384]{1,0:T(8,128)S(1)} %get-tuple-element.83), channel_id=1, source_target_pairs={{0,1},{1,0},{2,3},{3,2},{4,5},{5,4},{6,7},{7,6},{8,9},{9,8},{10,11... | collective-permute-start | bytes 147464 | tf_op jit(solution)/shard_map/ppermute | solution.py:16
  80.8 5.7 %collective-permute-start.23 = (f32[64,384]{1,0:T(8,128)S(1)}, f32[64,384]{1,0:T(8,128)S(1)}, u32[]{:S(2)}, u32[]{:S(2)}) collective-permute-start(f32[64,384]{1,0:T(8,128)S(1)} %pad_maximum_fusion.4), channel_id=1, source_target_pairs={{0,1},{1,0},{2,3},{3,2},{4,5},{5,4},{6,7},{7,6},{8,9},{9,8},{10,11... | collective-permute-start | bytes 294920 | tf_op jit(solution)/shard_map/ppermute | solution.py:16
  82.4 5.5 %collective-permute-start.24 = (f32[64,384]{1,0:T(8,128)S(1)}, f32[64,384]{1,0:T(8,128)S(1)}, u32[]{:S(2)}, u32[]{:S(2)}) collective-permute-start(f32[64,384]{1,0:T(8,128)S(1)} %pad_maximum_fusion.5), channel_id=1, source_target_pairs={{0,2},{2,0},{4,6},{6,4},{1,3},{3,1},{5,7},{7,5},{8,10},{10,8},{12,... | collective-permute-start | bytes 294920 | tf_op jit(solution)/shard_map/ppermute | solution.py:16
  84.4 4.6 %collective-permute-start.25 = (f32[64,384]{1,0:T(8,128)S(1)}, f32[64,384]{1,0:T(8,128)S(1)}, u32[]{:S(2)}, u32[]{:S(2)}) collective-permute-start(f32[64,384]{1,0:T(8,128)S(1)} %pad_maximum_fusion.6), channel_id=1, source_target_pairs={{0,16},{8,24},{16,0},{24,8},{1,17},{9,25},{17,1},{25,9},{2,18},{10... | collective-permute-start | bytes 294920 | tf_op jit(solution)/shard_map/ppermute | solution.py:16
  89.1 5.7 %collective-permute-start.26 = (f32[128,384]{1,0:T(8,128)S(1)}, f32[128,384]{1,0:T(8,128)S(1)}, u32[]{:S(2)}, u32[]{:S(2)}) collective-permute-start(f32[128,384]{1,0:T(8,128)S(1)} %pad_maximum_fusion), channel_id=1, source_target_pairs={{0,16},{8,24},{16,0},{24,8},{1,17},{9,25},{17,1},{25,9},{2,18},{10... | collective-permute-start | bytes 589832 | tf_op jit(solution)/shard_map/ppermute | solution.py:16
  90.6 5.7 %collective-permute-start.27 = (f32[128,384]{1,0:T(8,128)S(1)}, f32[128,384]{1,0:T(8,128)S(1)}, u32[]{:S(2)}, u32[]{:S(2)}) collective-permute-start(f32[128,384]{1,0:T(8,128)S(1)} %pad_maximum_fusion.1), channel_id=1, source_target_pairs={{0,1},{1,0},{2,3},{3,2},{4,5},{5,4},{6,7},{7,6},{8,9},{9,8},{10,11... | collective-permute-start | bytes 589832 | tf_op jit(solution)/shard_map/ppermute | solution.py:16
  91.1 5.7 %collective-permute-start.28 = (f32[128,384]{1,0:T(8,128)S(1)}, f32[128,384]{1,0:T(8,128)S(1)}, u32[]{:S(2)}, u32[]{:S(2)}) collective-permute-start(f32[128,384]{1,0:T(8,128)S(1)} %pad_maximum_fusion.2), channel_id=1, source_target_pairs={{0,2},{2,0},{4,6},{6,4},{1,3},{3,1},{5,7},{7,5},{8,10},{10,8},{12,... | collective-permute-start | bytes 589832 | tf_op jit(solution)/shard_map/ppermute | solution.py:16
  97.9 3.2 %collective-permute-start.29 = (f32[256,1152]{1,0:T(8,128)}, f32[256,1152]{1,0:T(8,128)}, u32[]{:S(2)}, u32[]{:S(2)}) collective-permute-start(f32[256,1152]{1,0:T(8,128)} %maximum_maximum_fusion.mine_ref), channel_id=1, source_target_pairs={{0,8},{8,0},{16,24},{24,16},{1,9},{9,1},{17,25},{25,17},{2,10},{10... | collective-permute-start | bytes 3538952 | tf_op jit(solution)/shard_map/ppermute | solution.py:16
  98.0 58.4 %copy-start.3 = (f32[2,512,256]{2,1,0:T(8,128)S(1)}, f32[2,512,256]{2,1,0:T(8,128)}, u32[]{:S(2)}) copy-start(f32[2,512,256]{2,1,0:T(8,128)} %copy-done.2) | copy-start | bytes 3145732
  98.0 58.4 %collective-permute-start.30 = (f32[2,512,256]{2,1,0:T(8,128)S(1)}, f32[2,512,256]{2,1,0:T(8,128)S(1)}, u32[]{:S(2)}, u32[]{:S(2)}) collective-permute-start(f32[2,512,256]{2,1,0:T(8,128)S(1)} %collective-permute-done.refs_1_.refs_0_), channel_id=1, source_target_pairs={{0,16},{8,24},{16,0},{24,8},{1,17},{9,25},{17,1},{25,9},{2,18},{10... | collective-permute-start | bytes 3145736 | tf_op jit(solution)/shard_map/ppermute | solution.py:16
  98.4 58.0 %collective-permute-start.31 = (f32[2,512,256]{2,1,0:T(8,128)}, f32[2,512,256]{2,1,0:T(8,128)S(1)}, u32[]{:S(2)}, u32[]{:S(2)}) collective-permute-start(f32[2,512,256]{2,1,0:T(8,128)} %copy-done.2), channel_id=1, source_target_pairs={{0,16},{8,24},{16,0},{24,8},{1,17},{9,25},{17,1},{25,9},{2,18},{10... | collective-permute-start | bytes 3145736 | tf_op jit(solution)/shard_map/ppermute | solution.py:16
